TPU v7x, 128 devices: a whole 4x4x4 slice. The times are simulated.
128 devices in a mesh: row: 8 (over z, core), col: 16 (over x, y).
Axes of the slice: x: 4, y: 4, z: 4, core: 2. Of those that a mesh axis runs over, the one named last changes fastest.
Arguments:
- start_block: float32 [32768, 128], P(('row', 'col')), may hold values from -6 to 6
- degree: float32 [32768], P(('row', 'col')), may hold values from 3.99 to 4.01
- block_values: float32 [49152, 4096], P(('row', 'col')), may hold values from -0.0007324219 to 0.0007324219
- block_rows: int32 [49152], P(('row', 'col')), may hold values from 0 to 31
- block_slots: int32 [49152], P(('row', 'col')), may hold values from 0 to 31, as said below
- need_lists: int32 [2048, 2], P(('row', 'col')), may hold values from 0 to 4, as said below
- live_blocks: int32 [128], P(('row', 'col')), may hold values from 96 to 384, as said below
Outputs:
- alphas: float32 [2, 128, 128], replicated
- betas: float32 [2, 128, 128], replicated
- next_basis: float32 [32768, 128], P(('row', 'col'))
Inputs may be any that keep to these rules, and one draw needn't show every extreme that they name: `need_lists`: entries of a need list are distinct block rows, listed first, then padded with 4; every list has at least one entry, and on every device some list is full with 2 entries. `block_slots`: each slot's value p * 2 + q points at a listed (never padded) entry q of the device's need list p. `live_blocks`: some device uses all 384 slots in every draw.
All inputs are finite; a program needn't handle non-finite values.
Results may differ from a plain program's by a relative error of at most 0.00045.
Values sent between devices are 32-bit elements; how exact they have to be, the bound alone decides.
No kernel may reach another device: no remote copies, remote signals or barrier semaphores. Data moves between devices by JAX's collectives and lax.ppermute only.
A program may use at most 128 MiB of HBM per device.

v0:
```python
import jax
import jax.numpy as jnp
from jax import lax
from jax.sharding import PartitionSpec as P

BS = 64
ITERS = 2


HIGH = lax.Precision.HIGHEST


def local_gram(left, right):
    return jnp.einsum("ra,rb->ab", left, right, precision=HIGH)


def on_device(start_block, degree, block_values, block_rows, block_slots, need_lists, live_blocks):
    row_count = lax.axis_size("row")
    col_count = lax.axis_size("col")
    local_rows, block_width = start_block.shape
    owned_blocks = local_rows // BS
    list_length = need_lists.shape[1]
    capacity = block_values.shape[0]
    group_size = min(128, capacity)
    total_rows = local_rows * row_count * col_count
    live_count = live_blocks[0]
    flat_need = need_lists.reshape(-1)
    stripe_cols = block_slots // list_length * owned_blocks + flat_need[block_slots]
    start_gram = lax.psum(local_gram(start_block, start_block), ("row", "col")) / total_rows
    lower_factor = jnp.linalg.cholesky(start_gram)
    current = lax.linalg.triangular_solve(
        lower_factor, start_block, left_side=False, lower=True, transpose_a=True
    )
    basis_list = [current]
    alpha_list = []
    beta_list = []
    for iteration in range(ITERS):
        owned_rows = current.reshape(owned_blocks, BS, block_width)
        row_side = lax.all_gather(owned_rows, "row", axis=0, tiled=True)
        col_side = lax.all_gather(owned_rows, "col", axis=0, tiled=True)
        col_length = col_count * owned_blocks
        group_total = (live_count + group_size - 1) // group_size

        def group_step(group_index, partials):
            row_part, col_part = partials
            first_slot = group_index * group_size
            values_now = lax.dynamic_slice_in_dim(block_values, first_slot, group_size, 0).reshape(
                group_size, BS, BS
            )
            rows_now = lax.dynamic_slice_in_dim(block_rows, first_slot, group_size, 0)
            cols_now = lax.dynamic_slice_in_dim(stripe_cols, first_slot, group_size, 0)
            in_use = (first_slot + jnp.arange(group_size, dtype=jnp.int32) < live_count).astype(
                current.dtype
            )
            values_now = values_now * in_use[:, None, None]
            forward = jnp.einsum("sab,sbn->san", values_now, col_side[cols_now], precision=HIGH)
            backward = jnp.einsum("sba,sbn->san", values_now, row_side[rows_now], precision=HIGH)
            return (row_part.at[rows_now].add(forward), col_part.at[cols_now].add(backward))

        start_parts = (
            jnp.zeros((row_count * owned_blocks, BS, block_width), current.dtype),
            jnp.zeros((col_length, BS, block_width), current.dtype),
        )
        row_part, col_part = lax.fori_loop(0, group_total, group_step, start_parts)
        row_sum = lax.psum_scatter(row_part, "row", scatter_dimension=0, tiled=True)
        col_sum = lax.psum_scatter(col_part, "col", scatter_dimension=0, tiled=True)
        image_block = degree[:, None] * current - (row_sum + col_sum).reshape(
            local_rows, block_width
        )
        stacked = jnp.concatenate(basis_list, axis=1)
        alpha_block = lax.psum(local_gram(current, image_block), ("row", "col")) / total_rows
        image_block = image_block - jnp.dot(current, alpha_block, precision=HIGH)
        if iteration > 0:
            image_block = image_block - jnp.dot(basis_list[-2], beta_list[-1].T, precision=HIGH)
        projection = lax.psum(local_gram(stacked, image_block), ("row", "col")) / total_rows
        image_block = image_block - jnp.dot(stacked, projection, precision=HIGH)
        norm_gram = lax.psum(local_gram(image_block, image_block), ("row", "col")) / total_rows
        lower_factor = jnp.linalg.cholesky(norm_gram)
        current = lax.linalg.triangular_solve(
            lower_factor, image_block, left_side=False, lower=True, transpose_a=True
        )
        alpha_list.append(alpha_block)
        beta_list.append(lower_factor.T)
        basis_list.append(current)
    return (jnp.stack(alpha_list), jnp.stack(beta_list), current)


def solution(mesh):
    return jax.shard_map(
        on_device,
        mesh=mesh,
        in_specs=(
            P(("row", "col"), None),
            P(("row", "col")),
            P(("row", "col"), None),
            P(("row", "col")),
            P(("row", "col")),
            P(("row", "col"), None),
            P(("row", "col")),
        ),
        out_specs=(P(), P(), P(("row", "col"), None)),
        check_vma=False,
    )
```

profile of v0, /device:TPU:1, one launch (start us, length us, event | category | flops | bytes accessed | tf_op | source)
XLA Modules:
  0.0 1837.6 jit_solution(1668707022313247895)
XLA Ops:
  9.2 145.2 %all-reduce.8.cloned.1.call-done = f32[128,128]{0,1:T(8,128)} async-done(((f32[128,128]{0,1:T(8,128)}), f32[128,128]{0,1:T(8,128)}) %all-reduce.8.cloned.1.call-update) | async-done | bytes 65552 | tf_op jit(solution)/shard_map/psum | solution.py:29
  189.9 20.1 %fusion.27 = s32[384]{0:T(512)S(1)} fusion(s32[384]{0:T(512)S(1)} %copy-done.16, s32[]{:T(128)} %bitcast.7, s32[]{:T(128)} %bitcast.8, s32[]{:T(128)} %bitcast.9, s32[]{:T(128)} %bitcast.10, s32[]{:T(128)} %bitcast.11, s32[]{:T(128)} %bitcast.12, s32[]{:T(128)} %bitcast.13, s32[]{:T(128)} %bitcast.14, s32[]{:T(128)} %bitcast.15, s32[]{:T(128)} %bitcast.16, ...), kind=kLoop, calls=%fused_computation.85 | loop fusion | flops 31104 | bytes 3200 | tf_op jit(solution)/shard_map/add | solution.py:28
  210.0 37.6 %all-gather.5.cloned.1.call-done = f32[64,64,128]{2,1,0:T(8,128)} async-done(((f32[4,64,128]{2,1,0:T(8,128)}), f32[64,64,128]{2,1,0:T(8,128)}) %all-gather.5.cloned.1.call-update) | async-done | bytes 2097168 | tf_op jit(solution)/shard_map/all_gather | solution.py:40
  249.3 195.9 %while.24 = (s32[]{:T(128)}, f32[32,64,128]{2,1,0:T(8,128)S(1)}, f32[64,64,128]{2,1,0:T(8,128)}, s32[]{:T(128)}, s32[384]{0:T(512)S(1)}, /*index=5*/f32[384,4096...) while((s32[]{:T(128)}, f32[32,64,128]{2,1,0:T(8,128)S(1)}, ...), condition=%wide.region_6.9_spmd, body=%wide.region_3.0_spmd.sunk | while | flops 1613237376 | bytes 96483616 | solution.py:64
  273.4 13.5 scatter_fusion
  338.5 13.5 scatter_fusion
  364.9 13.5 scatter_fusion.1
  430.0 13.5 scatter_fusion.1
  446.9 28.6 %reduce-scatter.5.cloned.1.call-done = f32[4,64,128]{2,1,0:T(8,128)} async-done(((f32[32,64,128]{2,1,0:T(8,128)}), f32[4,64,128]{2,1,0:T(8,128)}) %reduce-scatter.5.cloned.1.call-update) | async-done | bytes 131088 | tf_op jit(solution)/shard_map/reduce_scatter | solution.py:65
  475.5 77.8 %reduce-scatter.7.cloned.1.call-done = f32[4,64,128]{2,1,0:T(8,128)} async-done(((f32[64,64,128]{2,1,0:T(8,128)}), f32[4,64,128]{2,1,0:T(8,128)}) %reduce-scatter.7.cloned.1.call-update) | async-done | bytes 131088 | tf_op jit(solution)/shard_map/reduce_scatter | solution.py:66
  555.4 141.9 %all-reduce.10.cloned.1.call-done = f32[128,128]{0,1:T(8,128)} async-done(((f32[128,128]{0,1:T(8,128)}), f32[128,128]{0,1:T(8,128)}) %all-reduce.10.cloned.1.call-update) | async-done | bytes 65552 | tf_op jit(solution)/shard_map/psum | solution.py:71
  699.4 138.6 %all-reduce.12.cloned.1.call-done = f32[128,128]{0,1:T(8,128)} async-done(((f32[128,128]{0,1:T(8,128)}), f32[128,128]{0,1:T(8,128)}) %all-reduce.12.cloned.1.call-update) | async-done | bytes 65552 | tf_op jit(solution)/shard_map/psum | solution.py:75
  840.1 137.9 %all-reduce.14.cloned.1.call-done = f32[128,128]{0,1:T(8,128)} async-done(((f32[128,128]{0,1:T(8,128)}), f32[128,128]{0,1:T(8,128)}) %all-reduce.14.cloned.1.call-update) | async-done | bytes 65552 | tf_op jit(solution)/shard_map/psum | solution.py:77
  1004.9 20.4 %all-gather.11.cloned.1.call-done = f32[32,64,128]{2,1,0:T(8,128)} async-done(((f32[4,64,128]{2,1,0:T(8,128)}), f32[32,64,128]{2,1,0:T(8,128)}) %all-gather.11.cloned.1.call-update) | async-done | bytes 1048592 | tf_op jit(solution)/shard_map/all_gather | solution.py:39
  1025.3 46.2 %all-gather.9.cloned.1.call-done = f32[64,64,128]{2,1,0:T(8,128)} async-done(((f32[4,64,128]{2,1,0:T(8,128)}), f32[64,64,128]{2,1,0:T(8,128)}) %all-gather.9.cloned.1.call-update) | async-done | bytes 2097168 | tf_op jit(solution)/shard_map/all_gather | solution.py:40
  1073.2 195.7 %while.25 = (s32[]{:T(128)}, f32[32,64,128]{2,1,0:T(8,128)S(1)}, f32[64,64,128]{2,1,0:T(8,128)}, s32[]{:T(128)}, s32[384]{0:T(512)S(1)}, /*index=5*/f32[384,4096...) while((s32[]{:T(128)}, f32[32,64,128]{2,1,0:T(8,128)S(1)}, ...), condition=%wide.region_15.18_spmd, body=%wide.region_12.0_spmd.sunk | while | flops 1613237376 | bytes 96483616 | solution.py:64
  1097.3 13.5 scatter_fusion.2
  1188.8 13.5 scatter_fusion.3
  1253.9 13.5 scatter_fusion.3
  1270.6 28.6 %reduce-scatter.9.cloned.1.call-done = f32[4,64,128]{2,1,0:T(8,128)} async-done(((f32[32,64,128]{2,1,0:T(8,128)}), f32[4,64,128]{2,1,0:T(8,128)}) %reduce-scatter.9.cloned.1.call-update) | async-done | bytes 131088 | tf_op jit(solution)/shard_map/reduce_scatter | solution.py:65
  1299.2 77.8 %reduce-scatter.11.cloned.1.call-done = f32[4,64,128]{2,1,0:T(8,128)} async-done(((f32[64,64,128]{2,1,0:T(8,128)}), f32[4,64,128]{2,1,0:T(8,128)}) %reduce-scatter.11.cloned.1.call-update) | async-done | bytes 131088 | tf_op jit(solution)/shard_map/reduce_scatter | solution.py:66
  1379.1 142.0 %all-reduce.16.cloned.1.call-done = f32[128,128]{0,1:T(8,128)} async-done(((f32[128,128]{0,1:T(8,128)}), f32[128,128]{0,1:T(8,128)}) %all-reduce.16.cloned.1.call-update) | async-done | bytes 65552 | tf_op jit(solution)/shard_map/psum | solution.py:71
  1525.1 138.9 %all-reduce.18.cloned.1.call-done = f32[256,128]{1,0:T(8,128)} async-done(((f32[256,128]{1,0:T(8,128)}), f32[256,128]{1,0:T(8,128)}) %all-reduce.18.cloned.1.call-update) | async-done | bytes 131088 | tf_op jit(solution)/shard_map/psum | solution.py:75
  1667.0 137.4 %all-reduce.20.cloned.1.call-done = f32[128,128]{0,1:T(8,128)} async-done(((f32[128,128]{0,1:T(8,128)}), f32[128,128]{0,1:T(8,128)}) %all-reduce.20.cloned.1.call-update) | async-done | bytes 65552 | tf_op jit(solution)/shard_map/psum | solution.py:77
  (223 shorter events, 407.7 us)
Async XLA Ops:
  7.2 147.2 %all-reduce.8.cloned.1.call-start = ((), (), s32[]{:S(2)}) async-start(), calls=%async_computation.4 | async-start | bytes 131072 | tf_op jit(solution)/shard_map/psum | solution.py:29
  9.1 200.9 %all-gather.7.cloned.1.call-start = ((), (), s32[]{:S(2)}) async-start(), calls=%async_computation.6 | async-start | bytes 1179648 | tf_op jit(solution)/shard_map/all_gather | solution.py:39
  180.2 67.4 %all-gather.5.cloned.1.call-start = ((), (), s32[]{:S(2)}) async-start(), calls=%async_computation.5 | async-start | bytes 2228224 | tf_op jit(solution)/shard_map/all_gather | solution.py:40
  180.9 294.6 %reduce-scatter.5.cloned.1.call-start = ((), (), s32[]{:S(2)}) async-start(), calls=%async_computation.7 | async-start | bytes 1179648 | tf_op jit(solution)/shard_map/reduce_scatter | solution.py:65
  181.6 67.6 %copy-start.15 = (s32[384]{0:T(512)S(1)}, s32[384]{0:T(512)}, u32[]{:S(2)}) copy-start(s32[384]{0:T(512)} %param.17) | copy-start | bytes 4612
  249.3 305.1 %copy-start.14 = (f32[256]{0:T(256)S(1)}, f32[256]{0:T(256)}, u32[]{:S(2)}) copy-start(f32[256]{0:T(256)} %param.15) | copy-start | bytes 3076
  273.4 13.5 copy-start.4
  446.2 107.1 %reduce-scatter.7.cloned.1.call-start = ((), (), s32[]{:S(2)}) async-start(), calls=%async_computation.8 | async-start | bytes 2228224 | tf_op jit(solution)/shard_map/reduce_scatter | solution.py:66
  446.8 250.5 %all-reduce.10.cloned.1.call-start = ((), (), s32[]{:S(2)}) async-start(), calls=%async_computation.9 | async-start | bytes 131072 | tf_op jit(solution)/shard_map/psum | solution.py:71
  555.3 282.7 %all-reduce.12.cloned.1.call-start = ((), (), s32[]{:S(2)}) async-start(), calls=%async_computation.10 | async-start | bytes 131072 | tf_op jit(solution)/shard_map/psum | solution.py:75
  699.3 278.7 %all-reduce.14.cloned.1.call-start = ((), (), s32[]{:S(2)}) async-start(), calls=%async_computation.11 | async-start | bytes 131072 | tf_op jit(solution)/shard_map/psum | solution.py:77
  840.1 185.2 %all-gather.11.cloned.1.call-start = ((), (), s32[]{:S(2)}) async-start(), calls=%async_computation.13 | async-start | bytes 1179648 | tf_op jit(solution)/shard_map/all_gather | solution.py:39
  991.5 33.8 %copy-start.10 = (f32[128,128]{1,0:T(8,128)}, f32[128,128]{1,0:T(8,128)S(1)}, u32[]{:S(2)}) copy-start(f32[128,128]{1,0:T(8,128)S(1)} %cholesky.70) | copy-start | bytes 196612
  1004.3 67.3 %all-gather.9.cloned.1.call-start = ((), (), s32[]{:S(2)}) async-start(), calls=%async_computation.12 | async-start | bytes 2228224 | tf_op jit(solution)/shard_map/all_gather | solution.py:40
  1004.9 294.4 %reduce-scatter.9.cloned.1.call-start = ((), (), s32[]{:S(2)}) async-start(), calls=%async_computation.14 | async-start | bytes 1179648 | tf_op jit(solution)/shard_map/reduce_scatter | solution.py:65
  1097.3 13.5 copy-start.5
  1269.0 110.1 %copy-start.12 = (f32[128,128]{0,1:T(8,128)S(1)}, f32[128,128]{0,1:T(8,128)}, u32[]{:S(2)}) copy-start(f32[128,128]{0,1:T(8,128)} %all-reduce.10.cloned.1.call-done) | copy-start | bytes 196612
  1269.0 253.2 %copy-start.11 = (f32[128,128]{1,0:T(8,128)S(1)}, f32[128,128]{1,0:T(8,128)}, u32[]{:S(2)}) copy-start(f32[128,128]{1,0:T(8,128)} %copy-done.10) | copy-start | bytes 196612
  1269.0 550.2 %copy-start.13 = (f32[1,128,128]{1,2,0:T(8,128)S(1)}, f32[1,128,128]{1,2,0:T(8,128)}, u32[]{:S(2)}) copy-start(f32[1,128,128]{1,2,0:T(8,128)} %get-tuple-element.212) | copy-start | bytes 196612
  1270.0 107.0 %reduce-scatter.11.cloned.1.call-start = ((), (), s32[]{:S(2)}) async-start(), calls=%async_computation.15 | async-start | bytes 2228224 | tf_op jit(solution)/shard_map/reduce_scatter | solution.py:66
  1270.0 560.9 %copy-start.1 = (f32[256,128]{1,0:T(8,128)S(1)}, f32[256,128]{1,0:T(8,128)}, u32[]{:S(2)}) copy-start(f32[256,128]{1,0:T(8,128)} %param.14) | copy-start | bytes 393220
  1270.5 250.6 %all-reduce.16.cloned.1.call-start = ((), (), s32[]{:S(2)}) async-start(), calls=%async_computation.16 | async-start | bytes 131072 | tf_op jit(solution)/shard_map/psum | solution.py:71
  1379.0 284.9 %all-reduce.18.cloned.1.call-start = ((), (), s32[]{:S(2)}) async-start(), calls=%async_computation.17 | async-start | bytes 262144 | tf_op jit(solution)/shard_map/psum | solution.py:75
  1524.2 280.2 %all-reduce.20.cloned.1.call-start = ((), (), s32[]{:S(2)}) async-start(), calls=%async_computation.18 | async-start | bytes 131072 | tf_op jit(solution)/shard_map/psum | solution.py:77
  (21 other events, 140.0 us)
Sparse Core Ops, SparseCore 0:
  13.3 141.0 all-reduce.7
  180.3 20.8 all-gather.6
  204.1 43.3 all-gather.4
  446.4 29.0 reduce-scatter.4
  479.0 74.2 reduce-scatter.6
  558.5 138.7 all-reduce.9
  703.3 134.6 all-reduce.11
  843.3 134.6 all-reduce.13
  1004.4 20.8 all-gather.10
  1028.1 43.4 all-gather.8
  1270.1 29.0 reduce-scatter.8
  1302.7 74.2 reduce-scatter.10
  1382.3 138.7 all-reduce.15
  1527.0 136.8 all-reduce.17
  1669.1 135.2 all-reduce.19
where the time goes:
time: 1850 us; the launch traced here: 1840 us
  waiting for transfers between devices  1300 us (70%)
  other arithmetic  265 us (14%)
  matrix products  146 us (8%)
  local copies, waits for them, and re-layouts  108 us (6%)
    psum x2, waiting for transfers between devices, on_device(): lax.psum(local_gram(current, image_block), ('row', 'col')) / total_rows  284 us
    psum x2, waiting for transfers between devices, on_device(): lax.psum(local_gram(stacked, image_block), ('row', 'col')) / total_rows  278 us
    psum x2, waiting for transfers between devices, on_device(): lax.psum(local_gram(image_block, image_block), ('row', 'col')) / total_rows  275 us
    reduce_scatter x2, waiting for transfers between devices, on_device(): col_sum = lax.psum_scatter(col_part, 'col', scatter_dimension=0, tiled=True)  156 us
    psum x1, waiting for transfers between devices, on_device(): lax.psum(local_gram(start_block, start_block), ('row', 'col')) / total_rows  145 us
    all_gather x2, waiting for transfers between devices, on_device(): col_side = lax.all_gather(owned_rows, 'col', axis=0, tiled=True)  83.8 us
    scatter-add x6, other arithmetic, group_step(): col_part.at[cols_now].add(backward)  80.9 us
    scatter-add x6, other arithmetic, group_step(): row_part.at[rows_now].add(forward)  80.9 us
  transfers between devices with their start and end apart: 15, of which 14 were waited for; matrix products, arithmetic and copies ran while one was open for 2% of the time, Pallas kernels for 0%

commit v1 on v0

v1 whole, which is shorter than its diff:
```python
import functools

import jax
import jax.numpy as jnp
from jax import lax
from jax.experimental import pallas as pl
from jax.experimental.pallas import tpu as pltpu
from jax.sharding import PartitionSpec as P

BS = 64
RB = 4
KS = 2
NB = 128
ROWS = RB * BS
N_ROW = 8
N_COL = 16
NROWS = ROWS * N_ROW * N_COL
CAP = 384
SIDE = 2048
SHIFT = 4.0
GROUPS = CAP // 8
STEP_GROUPS = 6
FILL_STEPS = GROUPS // STEP_GROUPS
CHUNK = 256
CHUNKS = SIDE // CHUNK
SUMS = 24

HIGH = lax.Precision.HIGHEST
F32, BF16 = jnp.float32, jnp.bfloat16
MIB = 2**20


def mm(a, b, ca=1, cb=0):
    return lax.dot_general(a, b, (((ca,), (cb,)), ((), ())), precision=HIGH, preferred_element_type=F32)


def split(x):
    high = x.astype(BF16)
    return high, (x - high.astype(F32)).astype(BF16)


def dense_kernel(rows_ref, slots_ref, live_ref, vals_ref, hi_ref, lo_ref, dense):
    i = pl.program_id(0)
    live = live_ref[0]

    @pl.when(i == 0)
    def _():
        def clear(t, c):
            dense[t // 8, pl.ds(pl.multiple_of((t % 8) * 256, 256), 256), :] = jnp.zeros((256, 128), F32)
            return c

        lax.fori_loop(0, 128, clear, 0)

    half = lax.broadcasted_iota(jnp.int32, (32, 128), 1) // 64

    @pl.when(i < FILL_STEPS)
    def _():
        def group(g, c):
            for s in range(8):
                slot = (i * STEP_GROUPS + g) * 8 + s
                first = rows_ref[slot] * BS
                q = slots_ref[slot]
                side = jnp.where(slot < live, q % 2, 2)
                two = vals_ref[g, pl.ds(s, 32, stride=8), :]
                turned = pltpu.roll(two, 64, 1)
                even = jnp.where(half == side, jnp.where(half == 0, two, turned), 0.0)
                odd = jnp.where(half == side, jnp.where(half == 0, turned, two), 0.0)
                dense[q // 2, pl.ds(first, 32, stride=2), :] += even
                dense[q // 2, pl.ds(first + 1, 32, stride=2), :] += odd
            return c

        left = (live + 7) // 8 - i * STEP_GROUPS
        lax.fori_loop(0, jnp.clip(left, 0, STEP_GROUPS), group, 0)

    @pl.when(i >= FILL_STEPS)
    def _():
        first = pl.multiple_of((i - FILL_STEPS) * CHUNK, CHUNK)
        for j in range(16):
            high, low = split(dense[j, pl.ds(first, CHUNK), :])
            hi_ref[:, j * 128 : (j + 1) * 128] = high
            lo_ref[:, j * 128 : (j + 1) * 128] = low


def dense_of(values, rel_rows, slots, live):
    grid = FILL_STEPS + CHUNKS
    out = pl.BlockSpec((CHUNK, SIDE), lambda i, *_: (jnp.maximum(i - FILL_STEPS, 0), 0))
    return pl.pallas_call(
        dense_kernel,
        grid_spec=pltpu.PrefetchScalarGridSpec(
            num_scalar_prefetch=3,
            grid=(grid,),
            in_specs=[pl.BlockSpec((STEP_GROUPS, 256, 128), lambda i, *_: (jnp.minimum(i, FILL_STEPS - 1), 0, 0))],
            out_specs=[out, out],
            scratch_shapes=[pltpu.VMEM((16, SIDE, 128), F32)],
        ),
        out_shape=[jax.ShapeDtypeStruct((SIDE, SIDE), BF16)] * 2,
        compiler_params=pltpu.CompilerParams(vmem_limit_bytes=40 * MIB),
        cost_estimate=pl.CostEstimate(flops=10**7, bytes_accessed=50 * 10**6, transcendentals=0),
        name="dense",
    )(rel_rows, slots, live, values)


def product_kernel(whole, need_ref, hi_ref, lo_ref, own, z1, z2, z3, far, cols, extra, keep, send, pay, xc, xr, acc):
    i = pl.program_id(0)

    @pl.when(i == 0)
    def _():
        def column(p, c):
            for k in range(KS):
                if whole:
                    first = jnp.minimum(need_ref[p * KS + k], RB - 1) * BS
                    block = cols[p, pl.ds(pl.multiple_of(first, BS), BS), :]
                else:
                    block = cols[p, k * BS : (k + 1) * BS, :]
                high, low = split(block)
                here = pl.ds(pl.multiple_of((p * KS + k) * BS, BS), BS)
                xc[here, 0:128] = high
                xc[here, 128:256] = low
            return c

        lax.fori_loop(0, N_COL, column, 0)
        for c in range(CHUNKS):
            piece = (own, z1, z2, z3)[c][...] if c < 4 else far[(c - 4) * CHUNK : (c - 3) * CHUNK, :]
            high, low = split(piece.T)
            xr[c, 0:128, :] = high
            xr[c, 128:256, :] = low

    hi, lo, x = hi_ref[...], lo_ref[...], xc[...]
    out = jnp.dot(hi, x, preferred_element_type=F32) + jnp.dot(lo, x, preferred_element_type=F32)
    out = out[:, :128] + out[:, 128:]

    @pl.when(i < 4)
    def _():
        keep[jnp.minimum(i, 3)] = out

    @pl.when(i >= 4)
    def _():
        send[jnp.maximum(i - 4, 0)] = out

    v = xr[i]
    for j in range(4):
        here = slice(j * 512, (j + 1) * 512)
        part = jnp.dot(v, hi_ref[:, here], preferred_element_type=F32) + jnp.dot(
            v, lo_ref[:, here], preferred_element_type=F32
        )
        before = acc[:, here]
        acc[:, here] = jnp.where(i == 0, part, before + part)

    @pl.when(i == CHUNKS - 1)
    def _():
        for p in range(N_COL):
            here = slice(p * 128, (p + 1) * 128)
            pay[p, 0:128, :] = (acc[0:128, here] + acc[128:256, here]).T
            pay[p, 128:, :] = extra[p]


def products(whole, need, hi, lo, pieces, cols, extra):
    def full(shape):
        return pl.BlockSpec(shape, lambda i, *_: (0,) * len(shape))

    more = extra.shape[1]
    chunk = pl.BlockSpec((CHUNK, SIDE), lambda i, *_: (i, 0))
    return pl.pallas_call(
        functools.partial(product_kernel, whole),
        grid_spec=pltpu.PrefetchScalarGridSpec(
            num_scalar_prefetch=1,
            grid=(CHUNKS,),
            in_specs=[chunk, chunk] + [full((ROWS, NB))] * 4 + [full((4 * ROWS, NB)), full(cols.shape), full(extra.shape)],
            out_specs=[full((4, ROWS, NB)), full((4, ROWS, NB)), full((N_COL, 128 + more, NB))],
            scratch_shapes=[
                pltpu.VMEM((SIDE, 256), BF16),
                pltpu.VMEM((CHUNKS, 256, CHUNK), BF16),
                pltpu.VMEM((256, SIDE), F32),
            ],
        ),
        out_shape=[
            jax.ShapeDtypeStruct((4, ROWS, NB), F32),
            jax.ShapeDtypeStruct((4, ROWS, NB), F32),
            jax.ShapeDtypeStruct((N_COL, 128 + more, NB), F32),
        ],
        compiler_params=pltpu.CompilerParams(vmem_limit_bytes=40 * MIB),
        cost_estimate=pl.CostEstimate(flops=8 * 10**9, bytes_accessed=22 * 10**6, transcendentals=0),
        name="products",
    )(need, hi, lo, *pieces, cols, extra)


def image_of(v, deg, s0, s1, s2, s3, arrived, needs):
    sums = s0[...] + s1[...] + s2[...] + s3[...]

    def peer(p, parts):
        for q in range(KS):
            block = arrived[p, q * BS : (q + 1) * BS, :]
            which = needs[p, q : q + 1, :]
            parts = tuple(parts[k] + jnp.where(which == float(k), block, 0.0) for k in range(RB))
        return parts

    zero = jnp.zeros((BS, NB), F32)
    parts = lax.fori_loop(0, N_COL, peer, (zero,) * RB)
    return (deg[...] - SHIFT) * v[...] - sums - jnp.concatenate(parts, axis=0)


def first_kernel(v, deg, s0, s1, s2, s3, arrived, image, pay, needs):
    needs[...] = arrived[:, 128:136, :]
    y = image_of(v, deg, s0, s1, s2, s3, arrived, needs)
    image[...] = y
    for p in range(N_COL):
        for q in range(KS):
            which = needs[p, q : q + 1, :]
            block = jnp.zeros((BS, NB), F32)
            for k in range(RB):
                block = jnp.where(which == float(k), image[k * BS : (k + 1) * BS, :], block)
            pay[p, q * BS : (q + 1) * BS, :] = block
    x = v[...]
    xt, yt = x.T, y.T
    for at, gram in ((128, mm(xt, x)), (136, mm(xt, y)), (144, mm(yt, y))):
        gram = gram * (1.0 / NROWS)
        for p in range(N_COL):
            pay[p, at : at + 8, :] = gram[8 * p : 8 * p + 8, :]


def first_image(v, deg, sums, arrived):
    return pl.pallas_call(
        first_kernel,
        out_shape=[
            jax.ShapeDtypeStruct((ROWS, NB), F32),
            jax.ShapeDtypeStruct((N_COL, 128 + SUMS, NB), F32),
            jax.ShapeDtypeStruct((N_COL, 8, NB), F32),
        ],
        compiler_params=pltpu.CompilerParams(vmem_limit_bytes=32 * MIB),
        name="first_image",
    )(v, deg, *sums, arrived)


PANEL = 16


def factor(a):
    lane = lax.broadcasted_iota(jnp.int32, (NB, NB), 1)
    sub = lax.broadcasted_iota(jnp.int32, (NB, NB), 0)
    z = jnp.where(lane == sub, 1.0, 0.0)
    row = lax.broadcasted_iota(jnp.int32, (PANEL, NB), 0)
    uppers, inverses = [], []
    for b in range(NB // PANEL):
        pa, pz = a[:PANEL], z[:PANEL]
        for t in range(PANEL):
            k = b * PANEL + t
            scale = lax.rsqrt(pa[t : t + 1, k : k + 1])
            ra, rz = pa[t : t + 1] * scale, pz[t : t + 1] * scale
            times = pa[:, k : k + 1] * scale
            pa = jnp.where(row == t, ra, jnp.where(row > t, pa - times * ra, pa))
            pz = jnp.where(row == t, rz, jnp.where(row > t, pz - times * rz, pz))
        uppers.append(pa)
        inverses.append(pz)
        if b < NB // PANEL - 1:
            done = (b + 1) * PANEL
            left = pa.T[done:, :]
            a = a[PANEL:] - mm(left, pa)
            z = z[PANEL:] - mm(left, pz)
    upper = jnp.where(lane >= sub, jnp.concatenate(uppers, axis=0), 0.0)
    return upper, jnp.concatenate(inverses, axis=0)


def eye():
    return jnp.where(
        lax.broadcasted_iota(jnp.int32, (NB, NB), 0) == lax.broadcasted_iota(jnp.int32, (NB, NB), 1), 1.0, 0.0
    )


def second_kernel(x_ref, y_ref, deg, s0, s1, s2, s3, arrived, needs, alpha, beta, v0_ref, v1_ref, w_ref, gram):
    y2 = image_of(y_ref, deg, s0, s1, s2, s3, arrived, needs)
    xx, xy, yy = (
        jnp.concatenate([arrived[p, at : at + 8, :] for p in range(N_COL)], axis=0) for at in (128, 136, 144)
    )
    x, y = x_ref[...], y_ref[...]
    _, inv0 = factor(xx)
    a0 = mm(mm(inv0, xy), inv0, 1, 1)
    b0 = mm(mm(inv0, yy), inv0, 1, 1)
    alpha[...] = a0 + SHIFT * eye()
    upper1, inv1 = factor(b0 - mm(a0, a0, 0, 0))
    beta[...] = upper1
    v0 = mm(x, inv0, 1, 1)
    t = mm(inv0, inv1, 0, 1)
    u = mm(mm(inv0, a0, 0, 0), inv1, 1, 1)
    v1 = mm(y, t) - mm(x, u)
    w = mm(y2, t) - mm(y, u)
    v0_ref[...], v1_ref[...], w_ref[...] = v0, v1, w
    gram[0:128, :] = mm(v0.T, w) * (1.0 / NROWS)
    gram[128:256, :] = mm(v1.T, w) * (1.0 / NROWS)
    gram[256:384, :] = mm(w.T, w) * (1.0 / NROWS)


def second_image(x, y, deg, sums, arrived, needs):
    square = jax.ShapeDtypeStruct((NB, NB), F32)
    owned = jax.ShapeDtypeStruct((ROWS, NB), F32)
    return pl.pallas_call(
        second_kernel,
        out_shape=[square, square, owned, owned, owned, jax.ShapeDtypeStruct((3 * NB, NB), F32)],
        compiler_params=pltpu.CompilerParams(vmem_limit_bytes=32 * MIB),
        name="second_image",
    )(x, y, deg, *sums, arrived, needs)


def last_kernel(v0, v1, w, gram, alpha0, beta0, alphas, betas, basis):
    a0, a1, b = gram[0:128, :], gram[128:256, :], gram[256:384, :]
    upper, inv = factor(b - mm(a0, a0, 0, 0) - mm(a1, a1, 0, 0))
    alphas[0], betas[0] = alpha0[...], beta0[...]
    alphas[1] = a1 + SHIFT * eye()
    betas[1] = upper
    w2 = w[...] - mm(v0[...], a0) - mm(v1[...], a1)
    basis[...] = mm(w2, inv, 1, 1)


def last_block(*args):
    pair = jax.ShapeDtypeStruct((2, NB, NB), F32)
    return pl.pallas_call(
        last_kernel,
        out_shape=[pair, pair, jax.ShapeDtypeStruct((ROWS, NB), F32)],
        compiler_params=pltpu.CompilerParams(vmem_limit_bytes=32 * MIB),
        name="last_block",
    )(*args)


CORE = [(i, i ^ 1) for i in range(N_ROW)]


def along_z(k):
    return [(i, ((i // 2 + k) % 4) * 2 + i % 2) for i in range(N_ROW)]


def along_x(k):
    return [(i, ((i // 4 + k) % 4) * 4 + i % 4) for i in range(N_COL)]


def along_y(k):
    return [(i, (i // 4) * 4 + (i % 4 + k) % 4) for i in range(N_COL)]


def row_pieces(own):
    three = [lax.ppermute(own, "row", along_z(k)) for k in (3, 2, 1)]
    far = lax.ppermute(jnp.concatenate([own, *three]), "row", CORE)
    return [own, *three, far]


def row_sums(keep, send):
    other = lax.ppermute(send, "row", CORE)
    parts = [keep[k] + other[k] for k in range(4)]
    return [parts[0]] + [lax.ppermute(parts[k], "row", along_z(k)) for k in (1, 2, 3)]


def swap(x):
    return lax.all_to_all(x, "col", 0, 0)


def ring_sum(x, axis, shift):
    return x + sum(lax.ppermute(x, axis, shift(k)) for k in (1, 3, 2))


def sum_all(x):
    core = lax.axis_index("row") % 2
    n = x.shape[0] // 2
    here = jnp.where(core == 0, x[:n], x[n:])
    there = jnp.where(core == 0, x[n:], x[:n])
    here = here + lax.ppermute(there, "row", CORE)
    here = ring_sum(here, "row", along_z)
    here = ring_sum(here, "col", along_x)
    here = ring_sum(here, "col", along_y)
    other = lax.ppermute(here, "row", CORE)
    return jnp.concatenate([jnp.where(core == 0, here, other), jnp.where(core == 0, other, here)])


def on_device(start_block, degree, block_values, block_rows, block_slots, need_lists, live_blocks):
    row = lax.axis_index("row")
    z, core = row // 2, row % 2
    owner, k = block_rows // RB, block_rows % RB
    rel_rows = (((owner % 2) ^ core) * 4 + (owner // 2 - z) % 4) * RB + k
    need = need_lists.reshape(-1)
    needs_out = jnp.broadcast_to(
        jnp.pad(need_lists.astype(F32), ((0, 0), (0, 8 - KS)))[:, :, None], (N_COL, 8, NB)
    )
    deg = jnp.broadcast_to(degree[:, None], (ROWS, NB))
    values = block_values.reshape(GROUPS, 8, 32, 128).transpose(0, 2, 1, 3).reshape(GROUPS, 256, 128)

    cols = swap(jnp.broadcast_to(start_block[None], (N_COL, ROWS, NB)))
    pieces = row_pieces(start_block)
    hi, lo = dense_of(values, rel_rows, block_slots, live_blocks)
    keep, send, pay = products(True, need, hi, lo, pieces, cols, needs_out)
    sums = row_sums(keep, send)
    y, pay, needs = first_image(start_block, deg, sums, swap(pay))

    cols = swap(pay)
    pieces = row_pieces(y)
    part = cols[:, 128:, :].sum(0)
    part = part + lax.ppermute(part, "row", CORE)
    part = ring_sum(part, "row", along_z)
    zero = jnp.zeros((N_COL, SUMS, NB), F32)
    keep, send, pay = products(False, need, hi, lo, pieces, cols, zero)
    pay = pay.at[:, 128:, :].set(jnp.broadcast_to(part[None], (N_COL, SUMS, NB)))
    sums = row_sums(keep, send)
    alpha, beta, v0, v1, w, gram = second_image(start_block, y, deg, sums, swap(pay), needs)
    return tuple(last_block(v0, v1, w, sum_all(gram), alpha, beta))


def solution(mesh):
    return jax.shard_map(
        on_device,
        mesh=mesh,
        in_specs=(
            P(("row", "col"), None),
            P(("row", "col")),
            P(("row", "col"), None),
            P(("row", "col")),
            P(("row", "col")),
            P(("row", "col"), None),
            P(("row", "col")),
        ),
        out_specs=(P(), P(), P(("row", "col"), None)),
        check_vma=False,
    )
```

time: 1850 us -> 257 us (0.14)
  waiting for transfers between devices: 1300 us -> 64.1 us
  other arithmetic: 265 us -> 0.37 us
  matrix products: 146 us -> 0 us
  Pallas kernels: 0 us -> 105 us
  local copies, waits for them, and re-layouts: 108 us -> 16.6 us
  starting transfers between devices: 0.61 us -> 69.3 us
    psum x7 -> x0, waiting for transfers between devices: 982 us -> none  [the longest x2 284 us: on_device(): lax.psum(local_gram(current, image_block), ('row', 'col')) / total_rows]
    reduce_scatter x4 -> x0, waiting for transfers between devices: 213 us -> none  [the longest x2 156 us: on_device(): col_sum = lax.psum_scatter(col_part, 'col', scatter_dimension=0, tiled=True)]
    scatter-add x12 -> x0, other arithmetic: 162 us -> none  [the longest x6 80.9 us: group_step(): col_part.at[cols_now].add(backward)]
    dot_general x24 -> x0, matrix products: 145 us -> none  [the longest x6 73.1 us: group_step(): jnp.einsum('sab,sbn->san', values_now, col_side[cols_now], precision=HIGH)]
    pallas_call x0 -> x6, Pallas kernels: none -> 105 us  [the longest x2 47.7 us: products(): pl.pallas_call(functools.partial(product_kernel, whole), grid_spec=pltpu....]
    all_gather x4 -> x0, waiting for transfers between devices: 104 us -> none  [the longest x2 83.8 us: on_device(): col_side = lax.all_gather(owned_rows, 'col', axis=0, tiled=True)]
    another operation x19 -> x0, other arithmetic: 69.9 us -> none  [the longest x6 24.7 us: on_device(): lower_factor = jnp.linalg.cholesky(norm_gram)]
    gather x14 -> x0, local copies, waits for them, and re-layouts: 44.9 us -> none  [the longest x6 26.7 us: group_step(): col_side[cols_now]]
  transfers between devices with their start and end apart: 15 -> 35, of which waited for: 14 -> 26; matrix products, arithmetic and copies ran while one was open for 2% -> 0% of each run, Pallas kernels for 0% -> 15%
where the time goes in v1:
time: 257 us
  Pallas kernels  105 us (41%)
  starting transfers between devices  69.3 us (27%)
  waiting for transfers between devices  64.1 us (25%)
  local copies, waits for them, and re-layouts  16.6 us (6%)
    pallas_call x2, Pallas kernels, products(): pl.pallas_call(functools.partial(product_kernel, whole), grid_spec=pltpu....  47.7 us
    pallas_call x1, Pallas kernels, second_image(): pl.pallas_call(second_kernel, out_shape=[square, square, owned, owned, ow...  27.2 us
    all_to_all x4, starting transfers between devices, swap(): return lax.all_to_all(x, 'col', 0, 0)  24.6 us
    all_to_all x4, waiting for transfers between devices, swap(): return lax.all_to_all(x, 'col', 0, 0)  19.6 us
    pallas_call x1, Pallas kernels, dense_of(): pl.pallas_call(dense_kernel, grid_spec=pltpu.PrefetchScalarGridSpec(num_s...  14.1 us
    ppermute x12, waiting for transfers between devices, ring_sum(): return x + sum((lax.ppermute(x, axis, shift(k)) for k in (1, 3, 2)))  13.8 us
    ppermute x6, waiting for transfers between devices, row_pieces(): three = [lax.ppermute(own, 'row', along_z(k)) for k in (3, 2, 1)]  13.7 us
    pallas_call x1, Pallas kernels, last_block(): pl.pallas_call(last_kernel, out_shape=[pair, pair, jax.ShapeDtypeStruct((...  13.4 us
  transfers between devices with their start and end apart: 35, of which 26 were waited for; matrix products, arithmetic and copies ran while one was open for 0% of the time, Pallas kernels for 15%

profile of v1, /device:TPU:1, one launch (start us, length us, event | category | flops | bytes accessed | tf_op | source)
XLA Modules:
  0.0 256.6 jit_solution(1284746975441693618)
XLA Ops:
  3.1 7.7 %all-to-all-start = ((f32[16,256,128]{2,1,0:T(8,128)}), f32[16,256,128]{2,1,0:T(8,128)S(1)}, u32[]{:S(2)}, u32[]{:S(2)}) async-start(f32[16,256,128]{2,1,0:T(8,128)} %broadcast_in_dim.9), calls=%async_computation | async-start | bytes 4194304 | tf_op jit(solution)/shard_map/all_to_all | solution.py:351
  10.8 3.8 %collective-permute-start = (f32[256,128]{1,0:T(8,128)S(1)}, f32[256,128]{1,0:T(8,128)S(1)}, u32[]{:S(2)}, u32[]{:S(2)}) collective-permute-start(f32[256,128]{1,0:T(8,128)S(1)} %copy-done.1), channel_id=1, source_target_pairs={{0,96},{16,112},{32,0},{48,16},{64,32},{80,48},{96,64},{112,80},{1... | collective-permute-start | bytes 393224 | tf_op jit(solution)/shard_map/ppermute | solution.py:339
  15.4 4.8 %collective-permute-done.z1 = f32[256,128]{1,0:T(8,128)S(1)} collective-permute-done((f32[256,128]{1,0:T(8,128)S(1)}, f32[256,128]{1,0:T(8,128)S(1)}, u32[]{:S(2)}, u32[]{:S(2)}) %collective-permute-start) | collective-permute-done | bytes 131104 | tf_op jit(solution)/shard_map/ppermute | solution.py:339
  20.2 3.5 %collective-permute-done.2.z3 = f32[256,128]{1,0:T(8,128)S(1)} collective-permute-done((f32[256,128]{1,0:T(8,128)S(1)}, f32[256,128]{1,0:T(8,128)S(1)}, u32[]{:S(2)}, u32[]{:S(2)}) %collective-permute-start.2) | collective-permute-done | bytes 131104 | tf_op jit(solution)/shard_map/ppermute | solution.py:339
  28.5 14.1 %dense.1 = (bf16[2048,2048]{1,0:T(8,128)(2,1)}, bf16[2048,2048]{1,0:T(8,128)(2,1)}) custom-call(s32[384]{0:T(512)S(1)} %fusion.12.rows_ref, s32[384]{0:T(512)S(1)} %copy-done.2, s32[1]{0:T(128)S(6)} %copy.16.live_ref, f32[48,256,128]{2,1,0:T(8,128)S(1)} %bitcast.21), custom_call_target="tpu_custom_call" | custom-call | flops 10000000 | bytes 50000000 | tf_op jit(solution)/shard_map/dense/pallas_call | solution.py:87
  42.6 3.4 %copy-done.3 = bf16[2048,2048]{1,0:T(8,128)(2,1)S(1)} copy-done((bf16[2048,2048]{1,0:T(8,128)(2,1)S(1)}, bf16[2048,2048]{1,0:T(8,128)(2,1)}, u32[]{:S(2)}) %copy-start.3) | copy-done | bytes 8388632
  46.0 24.0 %products.2 = (f32[4,256,128]{2,1,0:T(8,128)S(1)}, f32[4,256,128]{2,1,0:T(8,128)S(1)}, f32[16,136,128]{2,1,0:T(8,128)}) custom-call(s32[32]{0:T(128)S(1)} %reshape.56.need_ref, bf16[2048,2048]{1,0:T(8,128)(2,1)S(1)} %copy-done.3, bf16[2048,2048]{1,0:T(8,128)(2,1)} %get-tuple-element.33.lo_ref, f32[256,128]{1,0:T(8,128)S(1)} %copy-done.1, ...), custom_call_target="tpu_custom_call" | custom-call | flops 8000000000 | bytes 22000000 | tf_op jit(solution)/shard_map/products/pallas_call | solution.py:163
  70.8 9.3 %all-to-all-start.1 = ((f32[16,136,128]{2,1,0:T(8,128)}), f32[16,136,128]{2,1,0:T(8,128)S(1)}, u32[]{:S(2)}, u32[]{:S(2)}) async-start(f32[16,136,128]{2,1,0:T(8,128)} %get-tuple-element.36), calls=%async_computation.1 | async-start | bytes 2228224 | tf_op jit(solution)/shard_map/all_to_all | solution.py:351
  84.9 4.0 %collective-permute-done.5.s1 = f32[256,128]{1,0:T(8,128)S(1)} collective-permute-done((f32[256,128]{1,0:T(8,128)S(1)}, f32[256,128]{1,0:T(8,128)S(1)}, u32[]{:S(2)}, u32[]{:S(2)}) %collective-permute-start.5) | collective-permute-done | bytes 131104 | tf_op jit(solution)/shard_map/ppermute | solution.py:347
  91.5 7.6 %all-to-all-done.1.arrived = f32[16,136,128]{2,1,0:T(8,128)S(1)} async-done(((f32[16,136,128]{2,1,0:T(8,128)}), f32[16,136,128]{2,1,0:T(8,128)S(1)}, u32[]{:S(2)}, u32[]{:S(2)}) %all-to-all-start.1) | async-done | bytes 1114144 | tf_op jit(solution)/shard_map/all_to_all | solution.py:351
  101.5 3.7 %all-to-all-start.2 = ((f32[16,152,128]{2,1,0:T(8,128)}), f32[16,152,128]{2,1,0:T(8,128)S(1)}, u32[]{:S(2)}, u32[]{:S(2)}) async-start(f32[16,152,128]{2,1,0:T(8,128)} %get-tuple-element.38), calls=%async_computation.2 | async-start | bytes 2490368 | tf_op jit(solution)/shard_map/all_to_all | solution.py:351
  113.4 2.8 %collective-permute-start.11 = (f32[1024,128]{1,0:T(8,128)S(1)}, f32[1024,128]{1,0:T(8,128)S(1)}, u32[]{:S(2)}, u32[]{:S(2)}) collective-permute-start(f32[1024,128]{1,0:T(8,128)S(1)} %pad_maximum_fusion.1), channel_id=1, source_target_pairs={{0,16},{16,0},{32,48},{48,32},{64,80},{80,64},{96,112},{112,96},{1... | collective-permute-start | bytes 1572872 | tf_op jit(solution)/shard_map/ppermute | solution.py:340
  116.1 6.7 %all-to-all-done.2.cols = f32[16,152,128]{2,1,0:T(8,128)S(1)} async-done(((f32[16,152,128]{2,1,0:T(8,128)}), f32[16,152,128]{2,1,0:T(8,128)S(1)}, u32[]{:S(2)}, u32[]{:S(2)}) %all-to-all-start.2) | async-done | bytes 1245216 | tf_op jit(solution)/shard_map/all_to_all | solution.py:351
  122.8 3.5 %collective-permute-start.16 = (f32[24,128]{1,0:T(8,128)S(1)}, f32[24,128]{1,0:T(8,128)S(1)}, u32[]{:S(2)}, u32[]{:S(2)}) collective-permute-start(f32[24,128]{1,0:T(8,128)S(1)} %slice_reduce_fusion), channel_id=1, source_target_pairs={{0,16},{16,0},{32,48},{48,32},{64,80},{80,64},{96,112},{112,96},{1... | collective-permute-start | bytes 36872 | tf_op jit(solution)/shard_map/ppermute | solution.py:393
  130.7 3.4 %copy-done.4 = bf16[2048,2048]{1,0:T(8,128)(2,1)S(1)} copy-done((bf16[2048,2048]{1,0:T(8,128)(2,1)S(1)}, bf16[2048,2048]{1,0:T(8,128)(2,1)}, u32[]{:S(2)}) %copy-start.4) | copy-done | bytes 8388632
  135.1 23.7 %products.3 = (f32[4,256,128]{2,1,0:T(8,128)S(1)}, f32[4,256,128]{2,1,0:T(8,128)S(1)}, f32[16,152,128]{2,1,0:T(8,128)}) custom-call(s32[32]{0:T(128)S(1)} %reshape.56.need_ref, bf16[2048,2048]{1,0:T(8,128)(2,1)S(1)} %copy-done.4, bf16[2048,2048]{1,0:T(8,128)(2,1)} %get-tuple-element.33.lo_ref, f32[256,128]{1,0:T(8,128)S(1)} %get-tuple-element.37.own.y_ref, ...), custom_call_target="tpu_custom_call" | custom-call | flops 8000000000 | bytes 22000000 | tf_op jit(solution)/shard_map/products/pallas_call | solution.py:163
  160.3 3.8 %all-to-all-start.3 = ((f32[16,152,128]{2,1,0:T(8,128)}), f32[16,152,128]{2,1,0:T(8,128)S(1)}, u32[]{:S(2)}, u32[]{:S(2)}) async-start(f32[16,152,128]{2,1,0:T(8,128)} %broadcast_dynamic-update-slice_fusion), calls=%async_computation.3 | async-start | bytes 2490368 | tf_op jit(solution)/shard_map/all_to_all | solution.py:351
  172.8 3.7 %collective-permute-done.14.s2 = f32[256,128]{1,0:T(8,128)S(1)} collective-permute-done((f32[256,128]{1,0:T(8,128)S(1)}, f32[256,128]{1,0:T(8,128)S(1)}, u32[]{:S(2)}, u32[]{:S(2)}) %collective-permute-start.14) | collective-permute-done | bytes 131104 | tf_op jit(solution)/shard_map/ppermute | solution.py:347
  176.5 5.3 %all-to-all-done.3.arrived = f32[16,152,128]{2,1,0:T(8,128)S(1)} async-done(((f32[16,152,128]{2,1,0:T(8,128)}), f32[16,152,128]{2,1,0:T(8,128)S(1)}, u32[]{:S(2)}, u32[]{:S(2)}) %all-to-all-start.3) | async-done | bytes 1245216 | tf_op jit(solution)/shard_map/all_to_all | solution.py:351
  181.8 27.2 %second_image.1 = (f32[128,128]{1,0:T(8,128)S(1)}, f32[128,128]{1,0:T(8,128)S(1)}, f32[256,128]{1,0:T(8,128)S(1)}, f32[256,128]{1,0:T(8,128)S(1)}, f32[256,128]{1,0:T(8,128)S(1)}, /*index=5*/f32[384,128]{1,0:T(8,128)S(1)}) custom-call(f32[256,128]{1,0:T(8,128)S(1)} %copy-done.1, f32[256,128]{1,0:T(8,128)S(1)} %get-tuple-element.37.own.y_ref, ...), custom_call_target="tpu_custom_call" | custom-call | tf_op jit(solution)/shard_map/second_image/pallas_call | solution.py:295
  209.0 3.5 %collective-permute-start.20 = (f32[192,128]{1,0:T(8,128)S(1)}, f32[192,128]{1,0:T(8,128)S(1)}, u32[]{:S(2)}, u32[]{:S(2)}) collective-permute-start(f32[192,128]{1,0:T(8,128)S(1)} %slice_select_fusion), channel_id=1, source_target_pairs={{0,16},{16,0},{32,48},{48,32},{64,80},{80,64},{96,112},{112,96},{1... | collective-permute-start | bytes 294920 | tf_op jit(solution)/shard_map/ppermute | solution.py:363
  234.4 2.8 %collective-permute-done.29 = f32[192,128]{1,0:T(8,128)S(1)} collective-permute-done((f32[192,128]{1,0:T(8,128)S(1)}, f32[192,128]{1,0:T(8,128)S(1)}, u32[]{:S(2)}, u32[]{:S(2)}) %collective-permute-start.29) | collective-permute-done | bytes 98336 | tf_op jit(solution)/shard_map/ppermute | solution.py:355
  237.2 5.0 %collective-permute-start.30 = (f32[192,128]{1,0:T(8,128)S(1)}, f32[192,128]{1,0:T(8,128)S(1)}, u32[]{:S(2)}, u32[]{:S(2)}) collective-permute-start(f32[192,128]{1,0:T(8,128)S(1)} %add_add_fusion), channel_id=1, source_target_pairs={{0,16},{16,0},{32,48},{48,32},{64,80},{80,64},{96,112},{112,96},{1... | collective-permute-start | bytes 294920 | tf_op jit(solution)/shard_map/ppermute | solution.py:367
  243.2 13.4 %last_block.1 = (f32[2,128,128]{2,1,0:T(8,128)}, f32[2,128,128]{2,1,0:T(8,128)}, f32[256,128]{1,0:T(8,128)}) custom-call(f32[256,128]{1,0:T(8,128)S(1)} %get-tuple-element.43.v0, f32[256,128]{1,0:T(8,128)S(1)} %get-tuple-element.44.v1, f32[256,128]{1,0:T(8,128)S(1)} %get-tuple-element.45.w, f32[384,128]{1,0:T(8,128)S(1)} %pad_maximum_fusion.2.gram, ...), custom_call_target="tpu_custom_call" | custom-call | tf_op jit(solution)/shard_map/last_block/pallas_call | solution.py:315
  (105 shorter events, 64.3 us)
Async XLA Ops:
  3.1 39.4 %all-to-all-start = ((f32[16,256,128]{2,1,0:T(8,128)}), f32[16,256,128]{2,1,0:T(8,128)S(1)}, u32[]{:S(2)}, u32[]{:S(2)}) async-start(f32[16,256,128]{2,1,0:T(8,128)} %broadcast_in_dim.9), calls=%async_computation | async-start | bytes 4194304 | tf_op jit(solution)/shard_map/all_to_all | solution.py:351
  10.8 9.4 %collective-permute-start = (f32[256,128]{1,0:T(8,128)S(1)}, f32[256,128]{1,0:T(8,128)S(1)}, u32[]{:S(2)}, u32[]{:S(2)}) collective-permute-start(f32[256,128]{1,0:T(8,128)S(1)} %copy-done.1), channel_id=1, source_target_pairs={{0,96},{16,112},{32,0},{48,16},{64,32},{80,48},{96,64},{112,80},{1... | collective-permute-start | bytes 393224 | tf_op jit(solution)/shard_map/ppermute | solution.py:339
  14.7 5.6 %collective-permute-start.1 = (f32[256,128]{1,0:T(8,128)S(1)}, f32[256,128]{1,0:T(8,128)S(1)}, u32[]{:S(2)}, u32[]{:S(2)}) collective-permute-start(f32[256,128]{1,0:T(8,128)S(1)} %copy-done.1), channel_id=1, source_target_pairs={{0,64},{16,80},{32,96},{48,112},{64,0},{80,16},{96,32},{112,48},{1... | collective-permute-start | bytes 393224 | tf_op jit(solution)/shard_map/ppermute | solution.py:339
  14.7 9.1 %collective-permute-start.2 = (f32[256,128]{1,0:T(8,128)S(1)}, f32[256,128]{1,0:T(8,128)S(1)}, u32[]{:S(2)}, u32[]{:S(2)}) collective-permute-start(f32[256,128]{1,0:T(8,128)S(1)} %copy-done.1), channel_id=1, source_target_pairs={{0,32},{16,48},{32,64},{48,80},{64,96},{80,112},{96,0},{112,16},{1... | collective-permute-start | bytes 393224 | tf_op jit(solution)/shard_map/ppermute | solution.py:339
  23.8 18.7 %collective-permute-start.3 = (f32[1024,128]{1,0:T(8,128)S(1)}, f32[1024,128]{1,0:T(8,128)}, u32[]{:S(2)}, u32[]{:S(2)}) collective-permute-start(f32[1024,128]{1,0:T(8,128)S(1)} %pad_maximum_fusion), channel_id=1, source_target_pairs={{0,16},{16,0},{32,48},{48,32},{64,80},{80,64},{96,112},{112,96},{1... | collective-permute-start | bytes 1572872 | tf_op jit(solution)/shard_map/ppermute | solution.py:340
  70.8 28.4 %all-to-all-start.1 = ((f32[16,136,128]{2,1,0:T(8,128)}), f32[16,136,128]{2,1,0:T(8,128)S(1)}, u32[]{:S(2)}, u32[]{:S(2)}) async-start(f32[16,136,128]{2,1,0:T(8,128)} %get-tuple-element.36), calls=%async_computation.1 | async-start | bytes 2228224 | tf_op jit(solution)/shard_map/all_to_all | solution.py:351
  82.2 6.8 %collective-permute-start.5 = (f32[256,128]{1,0:T(8,128)S(1)}, f32[256,128]{1,0:T(8,128)S(1)}, u32[]{:S(2)}, u32[]{:S(2)}) collective-permute-start(f32[256,128]{1,0:T(8,128)S(1)} %get-tuple-element.55), channel_id=1, source_target_pairs={{0,32},{16,48},{32,64},{48,80},{64,96},{80,112},{96,0},{112,16},{1... | collective-permute-start | bytes 393224 | tf_op jit(solution)/shard_map/ppermute | solution.py:347
  82.2 8.5 %collective-permute-start.6 = (f32[256,128]{1,0:T(8,128)S(1)}, f32[256,128]{1,0:T(8,128)S(1)}, u32[]{:S(2)}, u32[]{:S(2)}) collective-permute-start(f32[256,128]{1,0:T(8,128)S(1)} %get-tuple-element.54), channel_id=1, source_target_pairs={{0,64},{16,80},{32,96},{48,112},{64,0},{80,16},{96,32},{112,48},{1... | collective-permute-start | bytes 393224 | tf_op jit(solution)/shard_map/ppermute | solution.py:347
  84.4 7.1 %collective-permute-start.7 = (f32[256,128]{1,0:T(8,128)S(1)}, f32[256,128]{1,0:T(8,128)S(1)}, u32[]{:S(2)}, u32[]{:S(2)}) collective-permute-start(f32[256,128]{1,0:T(8,128)S(1)} %get-tuple-element.53), channel_id=1, source_target_pairs={{0,96},{16,112},{32,0},{48,16},{64,32},{80,48},{96,64},{112,80},{1... | collective-permute-start | bytes 393224 | tf_op jit(solution)/shard_map/ppermute | solution.py:347
  101.5 21.3 %all-to-all-start.2 = ((f32[16,152,128]{2,1,0:T(8,128)}), f32[16,152,128]{2,1,0:T(8,128)S(1)}, u32[]{:S(2)}, u32[]{:S(2)}) async-start(f32[16,152,128]{2,1,0:T(8,128)} %get-tuple-element.38), calls=%async_computation.2 | async-start | bytes 2490368 | tf_op jit(solution)/shard_map/all_to_all | solution.py:351
  105.3 5.8 %collective-permute-start.8 = (f32[256,128]{1,0:T(8,128)S(1)}, f32[256,128]{1,0:T(8,128)S(1)}, u32[]{:S(2)}, u32[]{:S(2)}) collective-permute-start(f32[256,128]{1,0:T(8,128)S(1)} %get-tuple-element.37.own.y_ref), channel_id=1, source_target_pairs={{0,96},{16,112},{32,0},{48,16},{64,32},{80,48},{96,64},{112,80},{1... | collective-permute-start | bytes 393224 | tf_op jit(solution)/shard_map/ppermute | solution.py:339
  108.0 5.3 %collective-permute-start.9 = (f32[256,128]{1,0:T(8,128)S(1)}, f32[256,128]{1,0:T(8,128)S(1)}, u32[]{:S(2)}, u32[]{:S(2)}) collective-permute-start(f32[256,128]{1,0:T(8,128)S(1)} %get-tuple-element.37.own.y_ref), channel_id=1, source_target_pairs={{0,64},{16,80},{32,96},{48,112},{64,0},{80,16},{96,32},{112,48},{1... | collective-permute-start | bytes 393224 | tf_op jit(solution)/shard_map/ppermute | solution.py:339
  113.4 16.5 %collective-permute-start.11 = (f32[1024,128]{1,0:T(8,128)S(1)}, f32[1024,128]{1,0:T(8,128)S(1)}, u32[]{:S(2)}, u32[]{:S(2)}) collective-permute-start(f32[1024,128]{1,0:T(8,128)S(1)} %pad_maximum_fusion.1), channel_id=1, source_target_pairs={{0,16},{16,0},{32,48},{48,32},{64,80},{80,64},{96,112},{112,96},{1... | collective-permute-start | bytes 1572872 | tf_op jit(solution)/shard_map/ppermute | solution.py:340
  127.2 32.5 %collective-permute-start.17 = (f32[24,128]{1,0:T(8,128)S(1)}, f32[24,128]{1,0:T(8,128)S(1)}, u32[]{:S(2)}, u32[]{:S(2)}) collective-permute-start(f32[24,128]{1,0:T(8,128)S(1)} %add.142), channel_id=1, source_target_pairs={{0,32},{16,48},{32,64},{48,80},{64,96},{80,112},{96,0},{112,16},{1... | collective-permute-start | bytes 36872 | tf_op jit(solution)/shard_map/ppermute | solution.py:355
  127.2 32.5 %collective-permute-start.18 = (f32[24,128]{1,0:T(8,128)S(1)}, f32[24,128]{1,0:T(8,128)S(1)}, u32[]{:S(2)}, u32[]{:S(2)}) collective-permute-start(f32[24,128]{1,0:T(8,128)S(1)} %add.142), channel_id=1, source_target_pairs={{0,96},{16,112},{32,0},{48,16},{64,32},{80,48},{96,64},{112,80},{1... | collective-permute-start | bytes 36872 | tf_op jit(solution)/shard_map/ppermute | solution.py:355
  129.8 29.8 %collective-permute-start.19 = (f32[24,128]{1,0:T(8,128)S(1)}, f32[24,128]{1,0:T(8,128)S(1)}, u32[]{:S(2)}, u32[]{:S(2)}) collective-permute-start(f32[24,128]{1,0:T(8,128)S(1)} %add.142), channel_id=1, source_target_pairs={{0,64},{16,80},{32,96},{48,112},{64,0},{80,16},{96,32},{112,48},{1... | collective-permute-start | bytes 36872 | tf_op jit(solution)/shard_map/ppermute | solution.py:355
  160.3 21.4 %all-to-all-start.3 = ((f32[16,152,128]{2,1,0:T(8,128)}), f32[16,152,128]{2,1,0:T(8,128)S(1)}, u32[]{:S(2)}, u32[]{:S(2)}) async-start(f32[16,152,128]{2,1,0:T(8,128)} %broadcast_dynamic-update-slice_fusion), calls=%async_computation.3 | async-start | bytes 2490368 | tf_op jit(solution)/shard_map/all_to_all | solution.py:351
  166.8 6.0 %collective-permute-start.13 = (f32[256,128]{1,0:T(8,128)S(1)}, f32[256,128]{1,0:T(8,128)S(1)}, u32[]{:S(2)}, u32[]{:S(2)}) collective-permute-start(f32[256,128]{1,0:T(8,128)S(1)} %get-tuple-element.51), channel_id=1, source_target_pairs={{0,32},{16,48},{32,64},{48,80},{64,96},{80,112},{96,0},{112,16},{1... | collective-permute-start | bytes 393224 | tf_op jit(solution)/shard_map/ppermute | solution.py:347
  167.4 9.0 %collective-permute-start.14 = (f32[256,128]{1,0:T(8,128)S(1)}, f32[256,128]{1,0:T(8,128)S(1)}, u32[]{:S(2)}, u32[]{:S(2)}) collective-permute-start(f32[256,128]{1,0:T(8,128)S(1)} %get-tuple-element.50), channel_id=1, source_target_pairs={{0,64},{16,80},{32,96},{48,112},{64,0},{80,16},{96,32},{112,48},{1... | collective-permute-start | bytes 393224 | tf_op jit(solution)/shard_map/ppermute | solution.py:347
  170.2 6.3 %collective-permute-start.15 = (f32[256,128]{1,0:T(8,128)S(1)}, f32[256,128]{1,0:T(8,128)S(1)}, u32[]{:S(2)}, u32[]{:S(2)}) collective-permute-start(f32[256,128]{1,0:T(8,128)S(1)} %get-tuple-element.49), channel_id=1, source_target_pairs={{0,96},{16,112},{32,0},{48,16},{64,32},{80,48},{96,64},{112,80},{1... | collective-permute-start | bytes 393224 | tf_op jit(solution)/shard_map/ppermute | solution.py:347
  213.4 5.3 %collective-permute-start.21 = (f32[192,128]{1,0:T(8,128)S(1)}, f32[192,128]{1,0:T(8,128)S(1)}, u32[]{:S(2)}, u32[]{:S(2)}) collective-permute-start(f32[192,128]{1,0:T(8,128)S(1)} %select_add_fusion), channel_id=1, source_target_pairs={{0,32},{16,48},{32,64},{48,80},{64,96},{80,112},{96,0},{112,16},{1... | collective-permute-start | bytes 294920 | tf_op jit(solution)/shard_map/ppermute | solution.py:355
  221.2 5.3 %collective-permute-start.25 = (f32[192,128]{1,0:T(8,128)S(1)}, f32[192,128]{1,0:T(8,128)S(1)}, u32[]{:S(2)}, u32[]{:S(2)}) collective-permute-start(f32[192,128]{1,0:T(8,128)S(1)} %add_add_fusion.2), channel_id=1, source_target_pairs={{0,12},{1,13},{2,14},{3,15},{4,0},{5,1},{6,2},{7,3},{8,4},{9,5},{1... | collective-permute-start | bytes 294920 | tf_op jit(solution)/shard_map/ppermute | solution.py:355
  231.8 5.4 %collective-permute-start.29 = (f32[192,128]{1,0:T(8,128)S(1)}, f32[192,128]{1,0:T(8,128)S(1)}, u32[]{:S(2)}, u32[]{:S(2)}) collective-permute-start(f32[192,128]{1,0:T(8,128)S(1)} %add_add_fusion.1), channel_id=1, source_target_pairs={{0,2},{1,3},{2,0},{3,1},{4,6},{5,7},{6,4},{7,5},{8,10},{9,11},{10,... | collective-permute-start | bytes 294920 | tf_op jit(solution)/shard_map/ppermute | solution.py:355
  237.2 5.9 %collective-permute-start.30 = (f32[192,128]{1,0:T(8,128)S(1)}, f32[192,128]{1,0:T(8,128)S(1)}, u32[]{:S(2)}, u32[]{:S(2)}) collective-permute-start(f32[192,128]{1,0:T(8,128)S(1)} %add_add_fusion), channel_id=1, source_target_pairs={{0,16},{16,0},{32,48},{48,32},{64,80},{80,64},{96,112},{112,96},{1... | collective-permute-start | bytes 294920 | tf_op jit(solution)/shard_map/ppermute | solution.py:367
  (25 other events, 167.3 us)

commit v2 on v1

--- a/solution.py
+++ b/solution.py
@@ -94,94 +94,133 @@
             scratch_shapes=[pltpu.VMEM((16, SIDE, 128), F32)],
         ),
         out_shape=[jax.ShapeDtypeStruct((SIDE, SIDE), BF16)] * 2,
-        compiler_params=pltpu.CompilerParams(vmem_limit_bytes=40 * MIB),
+        compiler_params=pltpu.CompilerParams(vmem_limit_bytes=56 * MIB),
         cost_estimate=pl.CostEstimate(flops=10**7, bytes_accessed=50 * 10**6, transcendentals=0),
         name="dense",
     )(rel_rows, slots, live, values)
 
 
-def product_kernel(whole, need_ref, hi_ref, lo_ref, own, z1, z2, z3, far, cols, extra, keep, send, pay, xc, xr, acc):
-    i = pl.program_id(0)
-
-    @pl.when(i == 0)
-    def _():
-        def column(p, c):
-            for k in range(KS):
-                if whole:
-                    first = jnp.minimum(need_ref[p * KS + k], RB - 1) * BS
-                    block = cols[p, pl.ds(pl.multiple_of(first, BS), BS), :]
-                else:
-                    block = cols[p, k * BS : (k + 1) * BS, :]
-                high, low = split(block)
-                here = pl.ds(pl.multiple_of((p * KS + k) * BS, BS), BS)
-                xc[here, 0:128] = high
-                xc[here, 128:256] = low
-            return c
-
-        lax.fori_loop(0, N_COL, column, 0)
-        for c in range(CHUNKS):
-            piece = (own, z1, z2, z3)[c][...] if c < 4 else far[(c - 4) * CHUNK : (c - 3) * CHUNK, :]
-            high, low = split(piece.T)
-            xr[c, 0:128, :] = high
-            xr[c, 128:256, :] = low
-
-    hi, lo, x = hi_ref[...], lo_ref[...], xc[...]
-    out = jnp.dot(hi, x, preferred_element_type=F32) + jnp.dot(lo, x, preferred_element_type=F32)
-    out = out[:, :128] + out[:, 128:]
-
-    @pl.when(i < 4)
-    def _():
-        keep[jnp.minimum(i, 3)] = out
-
-    @pl.when(i >= 4)
-    def _():
-        send[jnp.maximum(i - 4, 0)] = out
-
-    v = xr[i]
-    for j in range(4):
-        here = slice(j * 512, (j + 1) * 512)
-        part = jnp.dot(v, hi_ref[:, here], preferred_element_type=F32) + jnp.dot(
-            v, lo_ref[:, here], preferred_element_type=F32
-        )
-        before = acc[:, here]
-        acc[:, here] = jnp.where(i == 0, part, before + part)
-
-    @pl.when(i == CHUNKS - 1)
-    def _():
-        for p in range(N_COL):
-            here = slice(p * 128, (p + 1) * 128)
-            pay[p, 0:128, :] = (acc[0:128, here] + acc[128:256, here]).T
+def fetches(columns, i, hi_any, lo_any, hi, lo, sems):
+    here = pl.ds(pl.multiple_of(i * CHUNK, CHUNK), CHUNK)
+    at = (slice(None), here) if columns else (here, slice(None))
+    return [
+        pltpu.make_async_copy(src.at[at], dst.at[at], sems.at[n, i])
+        for n, (src, dst) in enumerate(((hi_any, hi), (lo_any, lo)))
+    ]
+
+
+def begin_fetches(columns, *refs):
+    def begin(i, c):
+        for copy in fetches(columns, i, *refs):
+            copy.start()
+        return c
+
+    lax.fori_loop(0, CHUNKS, begin, 0)
+
+
+def forward_kernel(whole, need_ref, hi_any, lo_any, cols, keep, send, hi, lo, xc, sems):
+    begin_fetches(False, hi_any, lo_any, hi, lo, sems)
+
+    def column(p, c):
+        for k in range(KS):
+            if whole:
+                first = jnp.minimum(need_ref[p * KS + k], RB - 1) * BS
+                block = cols[p, pl.ds(pl.multiple_of(first, BS), BS), :]
+            else:
+                block = cols[p, k * BS : (k + 1) * BS, :]
+            high, low = split(block)
+            here = pl.ds(pl.multiple_of((p * KS + k) * BS, BS), BS)
+            xc[here, 0:128] = high
+            xc[here, 128:256] = low
+        return c
+
+    lax.fori_loop(0, N_COL, column, 0)
+
+    def chunk(i, c):
+        here = pl.ds(pl.multiple_of(i * CHUNK, CHUNK), CHUNK)
+        x = xc[...]
+        for copy in fetches(False, i, hi_any, lo_any, hi, lo, sems):
+            copy.wait()
+        out = jnp.dot(hi[here, :], x, preferred_element_type=F32) + jnp.dot(lo[here, :], x, preferred_element_type=F32)
+        out = out[:, :128] + out[:, 128:]
+
+        @pl.when(i < 4)
+        def _():
+            keep[jnp.minimum(i, 3)] = out
+
+        @pl.when(i >= 4)
+        def _():
+            send[jnp.maximum(i - 4, 0)] = out
+
+        return c
+
+    lax.fori_loop(0, CHUNKS, chunk, 0)
+
+
+def backward_kernel(hi_any, lo_any, own, z1, z2, z3, far, extra, pay, hi, lo, xr, sems):
+    begin_fetches(True, hi_any, lo_any, hi, lo, sems)
+    for c in range(CHUNKS):
+        piece = (own, z1, z2, z3)[c][...] if c < 4 else far[(c - 4) * CHUNK : (c - 3) * CHUNK, :]
+        high, low = split(piece.T)
+        xr[0:128, c * CHUNK : (c + 1) * CHUNK] = high
+        xr[128:256, c * CHUNK : (c + 1) * CHUNK] = low
+
+    def chunk(j, c):
+        here = pl.ds(pl.multiple_of(j * CHUNK, CHUNK), CHUNK)
+        v = xr[...]
+        for copy in fetches(True, j, hi_any, lo_any, hi, lo, sems):
+            copy.wait()
+        out = jnp.dot(v, hi[:, here], preferred_element_type=F32) + jnp.dot(v, lo[:, here], preferred_element_type=F32)
+        out = (out[:128] + out[128:]).T
+        for q in range(2):
+            p = j * 2 + q
+            pay[p, 0:128, :] = out[q * 128 : (q + 1) * 128]
             pay[p, 128:, :] = extra[p]
-
-
-def products(whole, need, hi, lo, pieces, cols, extra):
-    def full(shape):
-        return pl.BlockSpec(shape, lambda i, *_: (0,) * len(shape))
-
-    more = extra.shape[1]
-    chunk = pl.BlockSpec((CHUNK, SIDE), lambda i, *_: (i, 0))
-    return pl.pallas_call(
-        functools.partial(product_kernel, whole),
-        grid_spec=pltpu.PrefetchScalarGridSpec(
-            num_scalar_prefetch=1,
-            grid=(CHUNKS,),
-            in_specs=[chunk, chunk] + [full((ROWS, NB))] * 4 + [full((4 * ROWS, NB)), full(cols.shape), full(extra.shape)],
-            out_specs=[full((4, ROWS, NB)), full((4, ROWS, NB)), full((N_COL, 128 + more, NB))],
-            scratch_shapes=[
-                pltpu.VMEM((SIDE, 256), BF16),
-                pltpu.VMEM((CHUNKS, 256, CHUNK), BF16),
-                pltpu.VMEM((256, SIDE), F32),
-            ],
-        ),
-        out_shape=[
-            jax.ShapeDtypeStruct((4, ROWS, NB), F32),
-            jax.ShapeDtypeStruct((4, ROWS, NB), F32),
-            jax.ShapeDtypeStruct((N_COL, 128 + more, NB), F32),
+        return c
+
+    lax.fori_loop(0, CHUNKS, chunk, 0)
+
+
+VMEM = pl.BlockSpec(memory_space=pltpu.VMEM)
+ANYWHERE = pl.BlockSpec(memory_space=pl.ANY)
+PRODUCT = {
+    "compiler_params": pltpu.CompilerParams(vmem_limit_bytes=50 * MIB),
+    "cost_estimate": pl.CostEstimate(flops=4 * 10**9, bytes_accessed=20 * 10**6, transcendentals=0),
+}
+
+
+def forward(whole, need, hi, lo, cols):
+    return pl.pallas_call(
+        functools.partial(forward_kernel, whole),
+        in_specs=[pl.BlockSpec(memory_space=pltpu.SMEM), ANYWHERE, ANYWHERE, VMEM],
+        out_specs=[VMEM] * 2,
+        scratch_shapes=[
+            pltpu.VMEM((SIDE, SIDE), BF16),
+            pltpu.VMEM((SIDE, SIDE), BF16),
+            pltpu.VMEM((SIDE, 256), BF16),
+            pltpu.SemaphoreType.DMA((2, CHUNKS)),
         ],
-        compiler_params=pltpu.CompilerParams(vmem_limit_bytes=40 * MIB),
-        cost_estimate=pl.CostEstimate(flops=8 * 10**9, bytes_accessed=22 * 10**6, transcendentals=0),
-        name="products",
-    )(need, hi, lo, *pieces, cols, extra)
+        out_shape=[jax.ShapeDtypeStruct((4, ROWS, NB), F32)] * 2,
+        name="forward",
+        **PRODUCT,
+    )(need, hi, lo, cols)
+
+
+def backward(hi, lo, pieces, extra):
+    return pl.pallas_call(
+        backward_kernel,
+        in_specs=[ANYWHERE, ANYWHERE] + [VMEM] * 6,
+        out_specs=VMEM,
+        scratch_shapes=[
+            pltpu.VMEM((SIDE, SIDE), BF16),
+            pltpu.VMEM((SIDE, SIDE), BF16),
+            pltpu.VMEM((256, SIDE), BF16),
+            pltpu.SemaphoreType.DMA((2, CHUNKS)),
+        ],
+        out_shape=jax.ShapeDtypeStruct((N_COL, 128 + extra.shape[1], NB), F32),
+        name="backward",
+        **PRODUCT,
+    )(hi, lo, *pieces, extra)
 
 
 def image_of(v, deg, s0, s1, s2, s3, arrived, needs):
@@ -231,33 +270,49 @@
     )(v, deg, *sums, arrived)
 
 
-PANEL = 16
+PANEL = 64
+WINDOW = 8
 
 
 def factor(a):
-    lane = lax.broadcasted_iota(jnp.int32, (NB, NB), 1)
-    sub = lax.broadcasted_iota(jnp.int32, (NB, NB), 0)
-    z = jnp.where(lane == sub, 1.0, 0.0)
+    z = eye()
     row = lax.broadcasted_iota(jnp.int32, (PANEL, NB), 0)
     uppers, inverses = [], []
     for b in range(NB // PANEL):
         pa, pz = a[:PANEL], z[:PANEL]
-        for t in range(PANEL):
+        da = dz = jnp.zeros((PANEL, NB), F32)
+        for t in range(0, PANEL, WINDOW):
             k = b * PANEL + t
-            scale = lax.rsqrt(pa[t : t + 1, k : k + 1])
-            ra, rz = pa[t : t + 1] * scale, pz[t : t + 1] * scale
-            times = pa[:, k : k + 1] * scale
-            pa = jnp.where(row == t, ra, jnp.where(row > t, pa - times * ra, pa))
-            pz = jnp.where(row == t, rz, jnp.where(row > t, pz - times * rz, pz))
-        uppers.append(pa)
-        inverses.append(pz)
+            here = range(WINDOW)
+            cols = [jnp.broadcast_to(pa[:, k + i : k + i + 1], (PANEL, NB)) for i in here]
+            ra = [pa[t + i : t + i + 1, :] for i in here]
+            rz = [pz[t + i : t + i + 1, :] for i in here]
+            tops = [[cols[j][t + i : t + i + 1, :] for j in here] for i in here]
+            for i in here:
+                root = lax.rsqrt(tops[i][i])
+                inverse = root * root
+                for j in range(i + 1, WINDOW):
+                    times = tops[i][j] * inverse
+                    ra[j] = ra[j] - times * ra[i]
+                    rz[j] = rz[j] - times * rz[i]
+                    cols[j] = cols[j] - times * cols[i]
+                    for m in range(j, WINDOW):
+                        tops[j][m] = tops[j][m] - times * tops[i][m]
+                da = jnp.where(row == t + i, ra[i] * root, da)
+                dz = jnp.where(row == t + i, rz[i] * root, dz)
+                cols[i] = cols[i] * inverse
+            for i in here:
+                pa = pa - cols[i] * ra[i]
+                pz = pz - cols[i] * rz[i]
+        uppers.append(da)
+        inverses.append(dz)
         if b < NB // PANEL - 1:
-            done = (b + 1) * PANEL
-            left = pa.T[done:, :]
-            a = a[PANEL:] - mm(left, pa)
-            z = z[PANEL:] - mm(left, pz)
-    upper = jnp.where(lane >= sub, jnp.concatenate(uppers, axis=0), 0.0)
-    return upper, jnp.concatenate(inverses, axis=0)
+            left = da.T[(b + 1) * PANEL :, :]
+            a = a[PANEL:] - mm(left, da)
+            z = z[PANEL:] - mm(left, dz)
+    lane = lax.broadcasted_iota(jnp.int32, (NB, NB), 1)
+    sub = lax.broadcasted_iota(jnp.int32, (NB, NB), 0)
+    return jnp.where(lane >= sub, jnp.concatenate(uppers, axis=0), 0.0), jnp.concatenate(inverses, axis=0)
 
 
 def eye():
@@ -266,10 +321,10 @@
     )
 
 
-def second_kernel(x_ref, y_ref, deg, s0, s1, s2, s3, arrived, needs, alpha, beta, v0_ref, v1_ref, w_ref, gram):
+def second_kernel(x_ref, y_ref, deg, s0, s1, s2, s3, arrived, needs, grams, alpha, beta, v0_ref, v1_ref, w_ref, gram):
     y2 = image_of(y_ref, deg, s0, s1, s2, s3, arrived, needs)
     xx, xy, yy = (
-        jnp.concatenate([arrived[p, at : at + 8, :] for p in range(N_COL)], axis=0) for at in (128, 136, 144)
+        jnp.concatenate([grams[p, at : at + 8, :] for p in range(N_COL)], axis=0) for at in (0, 8, 16)
     )
     x, y = x_ref[...], y_ref[...]
     _, inv0 = factor(xx)
@@ -289,7 +344,7 @@
     gram[256:384, :] = mm(w.T, w) * (1.0 / NROWS)
 
 
-def second_image(x, y, deg, sums, arrived, needs):
+def second_image(x, y, deg, sums, arrived, needs, grams):
     square = jax.ShapeDtypeStruct((NB, NB), F32)
     owned = jax.ShapeDtypeStruct((ROWS, NB), F32)
     return pl.pallas_call(
@@ -297,7 +352,7 @@
         out_shape=[square, square, owned, owned, owned, jax.ShapeDtypeStruct((3 * NB, NB), F32)],
         compiler_params=pltpu.CompilerParams(vmem_limit_bytes=32 * MIB),
         name="second_image",
-    )(x, y, deg, *sums, arrived, needs)
+    )(x, y, deg, *sums, arrived, needs, grams)
 
 
 def last_kernel(v0, v1, w, gram, alpha0, beta0, alphas, betas, basis):
@@ -324,19 +379,21 @@
 
 
 def along_z(k):
-    return [(i, ((i // 2 + k) % 4) * 2 + i % 2) for i in range(N_ROW)]
+    return [(i, ((i // 2) ^ k) * 2 + i % 2) for i in range(N_ROW)]
 
 
 def along_x(k):
-    return [(i, ((i // 4 + k) % 4) * 4 + i % 4) for i in range(N_COL)]
+    return [(i, ((i // 4) ^ k) * 4 + i % 4) for i in range(N_COL)]
 
 
 def along_y(k):
-    return [(i, (i // 4) * 4 + (i % 4 + k) % 4) for i in range(N_COL)]
-
-
-def row_pieces(own):
-    three = [lax.ppermute(own, "row", along_z(k)) for k in (3, 2, 1)]
+    return [(i, (i // 4) * 4 + ((i % 4) ^ k)) for i in range(N_COL)]
+
+
+def row_pieces(own, *after):
+    three = [lax.ppermute(own, "row", along_z(k)) for k in (1, 2, 3)]
+    if after:
+        *three, _ = lax.optimization_barrier((*three, *after))
     far = lax.ppermute(jnp.concatenate([own, *three]), "row", CORE)
     return [own, *three, far]
 
@@ -352,7 +409,7 @@
 
 
 def ring_sum(x, axis, shift):
-    return x + sum(lax.ppermute(x, axis, shift(k)) for k in (1, 3, 2))
+    return x + sum(lax.ppermute(x, axis, shift(k)) for k in (1, 2, 3))
 
 
 def sum_all(x):
@@ -372,7 +429,7 @@
     row = lax.axis_index("row")
     z, core = row // 2, row % 2
     owner, k = block_rows // RB, block_rows % RB
-    rel_rows = (((owner % 2) ^ core) * 4 + (owner // 2 - z) % 4) * RB + k
+    rel_rows = (((owner % 2) ^ core) * 4 + ((owner // 2) ^ z)) * RB + k
     need = need_lists.reshape(-1)
     needs_out = jnp.broadcast_to(
         jnp.pad(need_lists.astype(F32), ((0, 0), (0, 8 - KS)))[:, :, None], (N_COL, 8, NB)
@@ -381,22 +438,25 @@
     values = block_values.reshape(GROUPS, 8, 32, 128).transpose(0, 2, 1, 3).reshape(GROUPS, 256, 128)
 
     cols = swap(jnp.broadcast_to(start_block[None], (N_COL, ROWS, NB)))
-    pieces = row_pieces(start_block)
     hi, lo = dense_of(values, rel_rows, block_slots, live_blocks)
-    keep, send, pay = products(True, need, hi, lo, pieces, cols, needs_out)
-    sums = row_sums(keep, send)
-    y, pay, needs = first_image(start_block, deg, sums, swap(pay))
+    pieces = row_pieces(start_block, hi)
+    back = swap(backward(hi, lo, pieces, needs_out))
+    sums = row_sums(*forward(True, need, hi, lo, cols))
+    y, pay, needs = first_image(start_block, deg, sums, back)
 
     cols = swap(pay)
     pieces = row_pieces(y)
+    back = backward(hi, lo, pieces, jnp.zeros((N_COL, 8, NB), F32))
+    cols, back = lax.optimization_barrier((cols, back))
+    back = swap(back)
+    keep, send = forward(False, need, hi, lo, cols)
+    cols, keep, send = lax.optimization_barrier((cols, keep, send))
     part = cols[:, 128:, :].sum(0)
     part = part + lax.ppermute(part, "row", CORE)
     part = ring_sum(part, "row", along_z)
-    zero = jnp.zeros((N_COL, SUMS, NB), F32)
-    keep, send, pay = products(False, need, hi, lo, pieces, cols, zero)
-    pay = pay.at[:, 128:, :].set(jnp.broadcast_to(part[None], (N_COL, SUMS, NB)))
+    grams = swap(jnp.broadcast_to(part[None], (N_COL, SUMS, NB)))
     sums = row_sums(keep, send)
-    alpha, beta, v0, v1, w, gram = second_image(start_block, y, deg, sums, swap(pay), needs)
+    alpha, beta, v0, v1, w, gram = second_image(start_block, y, deg, sums, back, needs, grams)
     return tuple(last_block(v0, v1, w, sum_all(gram), alpha, beta))
 
 

time: 257 us -> 203 us (0.79)
  Pallas kernels: 105 us -> 69.8 us
  waiting for transfers between devices: 64.1 us -> 39.7 us
  blocking collectives: 0 us -> 13.4 us
  local copies, waits for them, and re-layouts: 16.6 us -> 3.97 us
  starting transfers between devices: 69.3 us -> 72 us
    pallas_call x1, Pallas kernels: 27.2 us -> 9.91 us  [second_image(): pl.pallas_call(second_kernel, out_shape=[square, square, owned, owned, ow...]
    all_to_all x4, waiting for transfers between devices: 19.6 us -> 2.51 us  [swap(): return lax.all_to_all(x, 'col', 0, 0)]
    all_to_all x0 -> x1, blocking collectives: none -> 13.4 us  [swap(): return lax.all_to_all(x, 'col', 0, 0)]
    unnamed x30 -> x12, local copies, waits for them, and re-layouts: 13.2 us -> 1.26 us
    pallas_call x2 -> x4, Pallas kernels: 47.7 us -> 35.9 us  [the longest x2 19 us: backward(): pl.pallas_call(backward_kernel, in_specs=[ANYWHERE, ANYWHERE] + [VMEM] *...]
    ppermute x18, waiting for transfers between devices: 27.5 us -> 18.1 us  [the longest x12 13.4 us: ring_sum(): return x + sum((lax.ppermute(x, axis, shift(k)) for k in (1, 2, 3)))]
    pallas_call x1, Pallas kernels: 13.4 us -> 4.74 us  [last_block(): pl.pallas_call(last_kernel, out_shape=[pair, pair, jax.ShapeDtypeStruct((...]
    pallas_call x1, Pallas kernels: 14.1 us -> 17.8 us  [dense_of(): pl.pallas_call(dense_kernel, grid_spec=pltpu.PrefetchScalarGridSpec(num_s...]
  transfers between devices with their start and end apart: 35 -> 35, of which waited for: 26 -> 26; matrix products, arithmetic and copies ran while one was open for 0% -> 1% of each run, Pallas kernels for 15% -> 22%
where the time goes in v2:
time: 203 us; the launch traced here: 202 us
  starting transfers between devices  72 us (35%)
  Pallas kernels  69.8 us (34%)
  waiting for transfers between devices  39.7 us (20%)
  blocking collectives  13.4 us (7%)
  local copies, waits for them, and re-layouts  3.97 us (2%)
    all_to_all x4, starting transfers between devices, swap(): return lax.all_to_all(x, 'col', 0, 0)  24.8 us
    pallas_call x2, Pallas kernels, backward(): pl.pallas_call(backward_kernel, in_specs=[ANYWHERE, ANYWHERE] + [VMEM] *...  19 us
    pallas_call x1, Pallas kernels, dense_of(): pl.pallas_call(dense_kernel, grid_spec=pltpu.PrefetchScalarGridSpec(num_s...  17.8 us
    pallas_call x2, Pallas kernels, forward(): pl.pallas_call(functools.partial(forward_kernel, whole), in_specs=[pl.Blo...  16.9 us
    all_to_all x1, blocking collectives, swap(): return lax.all_to_all(x, 'col', 0, 0)  13.4 us
    ppermute x12, waiting for transfers between devices, ring_sum(): return x + sum((lax.ppermute(x, axis, shift(k)) for k in (1, 2, 3)))  13.4 us
    ppermute x12, starting transfers between devices, ring_sum(): return x + sum((lax.ppermute(x, axis, shift(k)) for k in (1, 2, 3)))  13.3 us
    ppermute x6, waiting for transfers between devices, row_sums(): lax.ppermute(parts[k], 'row', along_z(k))  10.2 us
  transfers between devices with their start and end apart: 35, of which 26 were waited for; matrix products, arithmetic and copies ran while one was open for 1% of the time, Pallas kernels for 22%

profile of v2, /device:TPU:1, one launch (start us, length us, event | category | flops | bytes accessed | tf_op | source)
XLA Modules:
  0.0 202.1 jit_solution(6364093141476190283)
XLA Ops:
  0.6 2.4 %broadcast_in_dim.11 = f32[16,256,128]{2,1,0:T(8,128)} broadcast(f32[256,128]{1,0:T(8,128)} %x_ref.1), dimensions={1,2} | broadcast | bytes 2228224 | tf_op jit(solution)/shard_map/broadcast_in_dim | solution.py:440
  3.1 7.7 %all-to-all-start = ((f32[16,256,128]{2,1,0:T(8,128)}), f32[16,256,128]{2,1,0:T(8,128)S(1)}, u32[]{:S(2)}, u32[]{:S(2)}) async-start(f32[16,256,128]{2,1,0:T(8,128)} %broadcast_in_dim.11), calls=%async_computation | async-start | bytes 4194304 | tf_op jit(solution)/shard_map/all_to_all | solution.py:408
  10.8 3.8 %collective-permute-start.6 = (f32[256,128]{1,0:T(8,128)S(1)}, f32[256,128]{1,0:T(8,128)S(1)}, u32[]{:S(2)}, u32[]{:S(2)}) collective-permute-start(f32[256,128]{1,0:T(8,128)S(1)} %copy-done), channel_id=1, source_target_pairs={{0,96},{16,112},{32,64},{48,80},{64,32},{80,48},{96,0},{112,16},{1... | collective-permute-start | bytes 393224 | tf_op jit(solution)/shard_map/ppermute | solution.py:394
  16.6 17.8 %dense.1 = (bf16[2048,2048]{1,0:T(8,128)(2,1)}, bf16[2048,2048]{1,0:T(8,128)(2,1)}) custom-call(s32[384]{0:T(512)} %fusion.12.rows_ref, s32[384]{0:T(512)} %slots_ref.1, s32[1]{0:T(128)S(6)} %copy.15.live_ref, f32[48,256,128]{2,1,0:T(8,128)} %bitcast.21), custom_call_target="tpu_custom_call" | custom-call | flops 10000000 | bytes 50000000 | tf_op jit(solution)/shard_map/dense/pallas_call | solution.py:87
  35.3 2.7 %collective-permute-start.7 = (f32[1024,128]{1,0:T(8,128)}, f32[1024,128]{1,0:T(8,128)S(1)}, u32[]{:S(2)}, u32[]{:S(2)}) collective-permute-start(f32[1024,128]{1,0:T(8,128)} %pad_maximum_fusion), channel_id=1, source_target_pairs={{0,16},{16,0},{32,48},{48,32},{64,80},{80,64},{96,112},{112,96},{1... | collective-permute-start | bytes 1572872 | tf_op jit(solution)/shard_map/ppermute | solution.py:397
  39.8 9.5 %backward.2 = f32[16,136,128]{2,1,0:T(8,128)} custom-call(bf16[2048,2048]{1,0:T(8,128)(2,1)} %get-tuple-element.26.hi_any, bf16[2048,2048]{1,0:T(8,128)(2,1)} %get-tuple-element.27.lo_any, f32[256,128]{1,0:T(8,128)S(1)} %copy-done, f32[256,128]{1,0:T(8,128)S(1)} %collective-permute-done.4.z1, f32[256,128]{1,0:T(8,128)S(1)} %collective-permute-done.5.z2, ...), custom_call_target="tpu_custom_call" | custom-call | flops 4000000000 | bytes 20000000 | tf_op jit(solution)/shard_map/backward/pallas_call | solution.py:210
  49.3 6.5 %all-to-all-start.1 = ((f32[16,136,128]{2,1,0:T(8,128)}), f32[16,136,128]{2,1,0:T(8,128)S(1)}, u32[]{:S(2)}, u32[]{:S(2)}) async-start(f32[16,136,128]{2,1,0:T(8,128)} %backward.2), calls=%async_computation.1 | async-start | bytes 2228224 | tf_op jit(solution)/shard_map/all_to_all | solution.py:408
  55.8 8.4 %forward.2 = (f32[4,256,128]{2,1,0:T(8,128)S(1)}, f32[4,256,128]{2,1,0:T(8,128)S(1)}) custom-call(s32[32]{0:T(128)S(1)} %reshape.27.need_ref, bf16[2048,2048]{1,0:T(8,128)(2,1)} %get-tuple-element.26.hi_any, bf16[2048,2048]{1,0:T(8,128)(2,1)} %get-tuple-element.27.lo_any, f32[16,256,128]{2,1,0:T(8,128)S(1)} %all-to-all-done.cols), custom_call_target="tpu_custom_call" | custom-call | flops 4000000000 | bytes 20000000 | tf_op jit(solution)/shard_map/forward/pallas_call | solution.py:193
  66.6 3.2 %collective-permute-start.3 = (f32[256,128]{1,0:T(8,128)S(1)}, f32[256,128]{1,0:T(8,128)S(1)}, u32[]{:S(2)}, u32[]{:S(2)}) collective-permute-start(f32[256,128]{1,0:T(8,128)S(1)} %get-tuple-element.53), channel_id=1, source_target_pairs={{0,96},{16,112},{32,64},{48,80},{64,32},{80,48},{96,0},{112,16},{1... | collective-permute-start | bytes 393224 | tf_op jit(solution)/shard_map/ppermute | solution.py:404
  72.2 3.2 %collective-permute-done.3.s3 = f32[256,128]{1,0:T(8,128)S(1)} collective-permute-done((f32[256,128]{1,0:T(8,128)S(1)}, f32[256,128]{1,0:T(8,128)S(1)}, u32[]{:S(2)}, u32[]{:S(2)}) %collective-permute-start.3) | collective-permute-done | bytes 131104 | tf_op jit(solution)/shard_map/ppermute | solution.py:404
  79.1 6.9 %all-to-all-start.2 = ((f32[16,152,128]{2,1,0:T(8,128)}), f32[16,152,128]{2,1,0:T(8,128)S(1)}, u32[]{:S(2)}, u32[]{:S(2)}) async-start(f32[16,152,128]{2,1,0:T(8,128)} %copy-done.1), calls=%async_computation.2 | async-start | bytes 2490368 | tf_op jit(solution)/shard_map/all_to_all | solution.py:408
  89.4 2.8 %collective-permute-done.10.z3 = f32[256,128]{1,0:T(8,128)S(1)} collective-permute-done((f32[256,128]{1,0:T(8,128)S(1)}, f32[256,128]{1,0:T(8,128)S(1)}, u32[]{:S(2)}, u32[]{:S(2)}) %collective-permute-start.10) | collective-permute-done | bytes 131104 | tf_op jit(solution)/shard_map/ppermute | solution.py:394
  94.2 3.3 %collective-permute-start.11 = (f32[1024,128]{1,0:T(8,128)S(1)}, f32[1024,128]{1,0:T(8,128)S(1)}, u32[]{:S(2)}, u32[]{:S(2)}) collective-permute-start(f32[1024,128]{1,0:T(8,128)S(1)} %pad_maximum_fusion.1), channel_id=1, source_target_pairs={{0,16},{16,0},{32,48},{48,32},{64,80},{80,64},{96,112},{112,96},{1... | collective-permute-start | bytes 1572872 | tf_op jit(solution)/shard_map/ppermute | solution.py:397
  99.0 9.5 %backward.3 = f32[16,136,128]{2,1,0:T(8,128)} custom-call(bf16[2048,2048]{1,0:T(8,128)(2,1)} %get-tuple-element.26.hi_any, bf16[2048,2048]{1,0:T(8,128)(2,1)} %get-tuple-element.27.lo_any, f32[256,128]{1,0:T(8,128)S(1)} %get-tuple-element.33.own.y_ref, f32[256,128]{1,0:T(8,128)S(1)} %collective-permute-done.8.z1, f32[256,128]{1,0:T(8,128)S(1)} %collective-permute-done.9.z2, ...), custom_call_target="tpu_custom_call" | custom-call | flops 4000000000 | bytes 20000000 | tf_op jit(solution)/shard_map/backward/pallas_call | solution.py:210
  108.5 8.4 %forward.3 = (f32[4,256,128]{2,1,0:T(8,128)S(1)}, f32[4,256,128]{2,1,0:T(8,128)S(1)}) custom-call(s32[32]{0:T(128)S(1)} %reshape.27.need_ref, bf16[2048,2048]{1,0:T(8,128)(2,1)} %get-tuple-element.26.hi_any, bf16[2048,2048]{1,0:T(8,128)(2,1)} %get-tuple-element.27.lo_any, f32[16,152,128]{2,1,0:T(8,128)S(1)} %all-to-all-done.2.cols), custom_call_target="tpu_custom_call" | custom-call | flops 4000000000 | bytes 20000000 | tf_op jit(solution)/shard_map/forward/pallas_call | solution.py:193
  124.1 13.4 %all_to_all.25.grams = f32[16,24,128]{2,1,0:T(8,128)S(1)} all-to-all(f32[16,24,128]{2,1,0:T(8,128)S(1)} %broadcast_in_dim.14), channel_id=1, replica_groups=mesh['row'=8,'col'=16] {'col'}, dimensions={0} | all-to-all | bytes 393216 | tf_op jit(solution)/shard_map/all_to_all | solution.py:408
  137.5 3.7 %all-to-all-start.3 = ((f32[16,136,128]{2,1,0:T(8,128)}), f32[16,136,128]{2,1,0:T(8,128)S(1)}, u32[]{:S(2)}, u32[]{:S(2)}) async-start(f32[16,136,128]{2,1,0:T(8,128)} %backward.3), calls=%async_computation.3 | async-start | bytes 2228224 | tf_op jit(solution)/shard_map/all_to_all | solution.py:408
  141.2 3.2 %collective-permute-start.12 = (f32[4,256,128]{2,1,0:T(8,128)S(1)}, f32[4,256,128]{2,1,0:T(8,128)S(1)}, u32[]{:S(2)}, u32[]{:S(2)}) collective-permute-start(f32[4,256,128]{2,1,0:T(8,128)S(1)} %get-tuple-element.39), channel_id=1, source_target_pairs={{0,16},{16,0},{32,48},{48,32},{64,80},{80,64},{96,112},{112,96},{1... | collective-permute-start | bytes 1572872 | tf_op jit(solution)/shard_map/ppermute | solution.py:402
  149.3 5.0 %collective-permute-done.15.s3 = f32[256,128]{1,0:T(8,128)S(1)} collective-permute-done((f32[256,128]{1,0:T(8,128)S(1)}, f32[256,128]{1,0:T(8,128)S(1)}, u32[]{:S(2)}, u32[]{:S(2)}) %collective-permute-start.15) | collective-permute-done | bytes 131104 | tf_op jit(solution)/shard_map/ppermute | solution.py:404
  156.0 9.9 %second_image.1 = (f32[128,128]{1,0:T(8,128)S(1)}, f32[128,128]{1,0:T(8,128)S(1)}, f32[256,128]{1,0:T(8,128)S(1)}, f32[256,128]{1,0:T(8,128)S(1)}, f32[256,128]{1,0:T(8,128)S(1)}, /*index=5*/f32[384,128]{1,0:T(8,128)S(1)}) custom-call(f32[256,128]{1,0:T(8,128)S(1)} %copy-done, f32[256,128]{1,0:T(8,128)S(1)} %get-tuple-element.33.own.y_ref, ...), custom_call_target="tpu_custom_call" | custom-call | tf_op jit(solution)/shard_map/second_image/pallas_call | solution.py:350
  165.9 4.2 %collective-permute-start.20 = (f32[192,128]{1,0:T(8,128)S(1)}, f32[192,128]{1,0:T(8,128)S(1)}, u32[]{:S(2)}, u32[]{:S(2)}) collective-permute-start(f32[192,128]{1,0:T(8,128)S(1)} %slice_select_fusion), channel_id=1, source_target_pairs={{0,16},{16,0},{32,48},{48,32},{64,80},{80,64},{96,112},{112,96},{1... | collective-permute-start | bytes 294920 | tf_op jit(solution)/shard_map/ppermute | solution.py:420
  189.0 2.5 %collective-permute-done.29 = f32[192,128]{1,0:T(8,128)S(1)} collective-permute-done((f32[192,128]{1,0:T(8,128)S(1)}, f32[192,128]{1,0:T(8,128)S(1)}, u32[]{:S(2)}, u32[]{:S(2)}) %collective-permute-start.29) | collective-permute-done | bytes 98336 | tf_op jit(solution)/shard_map/ppermute | solution.py:412
  192.1 4.3 %collective-permute-start.30 = (f32[192,128]{1,0:T(8,128)S(1)}, f32[192,128]{1,0:T(8,128)S(1)}, u32[]{:S(2)}, u32[]{:S(2)}) collective-permute-start(f32[192,128]{1,0:T(8,128)S(1)} %add_add_fusion), channel_id=1, source_target_pairs={{0,16},{16,0},{32,48},{48,32},{64,80},{80,64},{96,112},{112,96},{1... | collective-permute-start | bytes 294920 | tf_op jit(solution)/shard_map/ppermute | solution.py:424
  197.3 4.7 %last_block.1 = (f32[2,128,128]{2,1,0:T(8,128)}, f32[2,128,128]{2,1,0:T(8,128)}, f32[256,128]{1,0:T(8,128)}) custom-call(f32[256,128]{1,0:T(8,128)S(1)} %get-tuple-element.43.v0, f32[256,128]{1,0:T(8,128)S(1)} %get-tuple-element.44.v1, f32[256,128]{1,0:T(8,128)S(1)} %get-tuple-element.45.w, f32[384,128]{1,0:T(8,128)S(1)} %pad_maximum_fusion.2.gram, ...), custom_call_target="tpu_custom_call" | custom-call | tf_op jit(solution)/shard_map/last_block/pallas_call | solution.py:370
  (90 shorter events, 53.3 us)
Async XLA Ops:
  3.1 46.2 %all-to-all-start = ((f32[16,256,128]{2,1,0:T(8,128)}), f32[16,256,128]{2,1,0:T(8,128)S(1)}, u32[]{:S(2)}, u32[]{:S(2)}) async-start(f32[16,256,128]{2,1,0:T(8,128)} %broadcast_in_dim.11), calls=%async_computation | async-start | bytes 4194304 | tf_op jit(solution)/shard_map/all_to_all | solution.py:408
  10.8 23.6 %collective-permute-start.6 = (f32[256,128]{1,0:T(8,128)S(1)}, f32[256,128]{1,0:T(8,128)S(1)}, u32[]{:S(2)}, u32[]{:S(2)}) collective-permute-start(f32[256,128]{1,0:T(8,128)S(1)} %copy-done), channel_id=1, source_target_pairs={{0,96},{16,112},{32,64},{48,80},{64,32},{80,48},{96,0},{112,16},{1... | collective-permute-start | bytes 393224 | tf_op jit(solution)/shard_map/ppermute | solution.py:394
  14.6 19.8 %collective-permute-start.5 = (f32[256,128]{1,0:T(8,128)S(1)}, f32[256,128]{1,0:T(8,128)S(1)}, u32[]{:S(2)}, u32[]{:S(2)}) collective-permute-start(f32[256,128]{1,0:T(8,128)S(1)} %copy-done), channel_id=1, source_target_pairs={{0,64},{16,80},{32,96},{48,112},{64,0},{80,16},{96,32},{112,48},{1... | collective-permute-start | bytes 393224 | tf_op jit(solution)/shard_map/ppermute | solution.py:394
  14.6 19.8 %collective-permute-start.4 = (f32[256,128]{1,0:T(8,128)S(1)}, f32[256,128]{1,0:T(8,128)S(1)}, u32[]{:S(2)}, u32[]{:S(2)}) collective-permute-start(f32[256,128]{1,0:T(8,128)S(1)} %copy-done), channel_id=1, source_target_pairs={{0,32},{16,48},{32,0},{48,16},{64,96},{80,112},{96,64},{112,80},{1... | collective-permute-start | bytes 393224 | tf_op jit(solution)/shard_map/ppermute | solution.py:394
  49.3 22.9 %all-to-all-start.1 = ((f32[16,136,128]{2,1,0:T(8,128)}), f32[16,136,128]{2,1,0:T(8,128)S(1)}, u32[]{:S(2)}, u32[]{:S(2)}) async-start(f32[16,136,128]{2,1,0:T(8,128)} %backward.2), calls=%async_computation.1 | async-start | bytes 2228224 | tf_op jit(solution)/shard_map/all_to_all | solution.py:408
  66.6 8.8 %collective-permute-start.3 = (f32[256,128]{1,0:T(8,128)S(1)}, f32[256,128]{1,0:T(8,128)S(1)}, u32[]{:S(2)}, u32[]{:S(2)}) collective-permute-start(f32[256,128]{1,0:T(8,128)S(1)} %get-tuple-element.53), channel_id=1, source_target_pairs={{0,96},{16,112},{32,64},{48,80},{64,32},{80,48},{96,0},{112,16},{1... | collective-permute-start | bytes 393224 | tf_op jit(solution)/shard_map/ppermute | solution.py:404
  69.8 5.9 %collective-permute-start.2 = (f32[256,128]{1,0:T(8,128)S(1)}, f32[256,128]{1,0:T(8,128)S(1)}, u32[]{:S(2)}, u32[]{:S(2)}) collective-permute-start(f32[256,128]{1,0:T(8,128)S(1)} %get-tuple-element.54), channel_id=1, source_target_pairs={{0,64},{16,80},{32,96},{48,112},{64,0},{80,16},{96,32},{112,48},{1... | collective-permute-start | bytes 393224 | tf_op jit(solution)/shard_map/ppermute | solution.py:404
  70.2 6.4 %collective-permute-start.1 = (f32[256,128]{1,0:T(8,128)S(1)}, f32[256,128]{1,0:T(8,128)S(1)}, u32[]{:S(2)}, u32[]{:S(2)}) collective-permute-start(f32[256,128]{1,0:T(8,128)S(1)} %get-tuple-element.55), channel_id=1, source_target_pairs={{0,32},{16,48},{32,0},{48,16},{64,96},{80,112},{96,64},{112,80},{1... | collective-permute-start | bytes 393224 | tf_op jit(solution)/shard_map/ppermute | solution.py:404
  79.1 29.4 %all-to-all-start.2 = ((f32[16,152,128]{2,1,0:T(8,128)}), f32[16,152,128]{2,1,0:T(8,128)S(1)}, u32[]{:S(2)}, u32[]{:S(2)}) async-start(f32[16,152,128]{2,1,0:T(8,128)} %copy-done.1), calls=%async_computation.2 | async-start | bytes 2490368 | tf_op jit(solution)/shard_map/all_to_all | solution.py:408
  86.1 6.1 %collective-permute-start.10 = (f32[256,128]{1,0:T(8,128)S(1)}, f32[256,128]{1,0:T(8,128)S(1)}, u32[]{:S(2)}, u32[]{:S(2)}) collective-permute-start(f32[256,128]{1,0:T(8,128)S(1)} %get-tuple-element.33.own.y_ref), channel_id=1, source_target_pairs={{0,96},{16,112},{32,64},{48,80},{64,32},{80,48},{96,0},{112,16},{1... | collective-permute-start | bytes 393224 | tf_op jit(solution)/shard_map/ppermute | solution.py:394
  88.5 5.7 %collective-permute-start.9 = (f32[256,128]{1,0:T(8,128)S(1)}, f32[256,128]{1,0:T(8,128)S(1)}, u32[]{:S(2)}, u32[]{:S(2)}) collective-permute-start(f32[256,128]{1,0:T(8,128)S(1)} %get-tuple-element.33.own.y_ref), channel_id=1, source_target_pairs={{0,64},{16,80},{32,96},{48,112},{64,0},{80,16},{96,32},{112,48},{1... | collective-permute-start | bytes 393224 | tf_op jit(solution)/shard_map/ppermute | solution.py:394
  89.0 5.1 %collective-permute-start.8 = (f32[256,128]{1,0:T(8,128)S(1)}, f32[256,128]{1,0:T(8,128)S(1)}, u32[]{:S(2)}, u32[]{:S(2)}) collective-permute-start(f32[256,128]{1,0:T(8,128)S(1)} %get-tuple-element.33.own.y_ref), channel_id=1, source_target_pairs={{0,32},{16,48},{32,0},{48,16},{64,96},{80,112},{96,64},{112,80},{1... | collective-permute-start | bytes 393224 | tf_op jit(solution)/shard_map/ppermute | solution.py:394
  137.5 18.5 %all-to-all-start.3 = ((f32[16,136,128]{2,1,0:T(8,128)}), f32[16,136,128]{2,1,0:T(8,128)S(1)}, u32[]{:S(2)}, u32[]{:S(2)}) async-start(f32[16,136,128]{2,1,0:T(8,128)} %backward.3), calls=%async_computation.3 | async-start | bytes 2228224 | tf_op jit(solution)/shard_map/all_to_all | solution.py:408
  146.0 8.3 %collective-permute-start.15 = (f32[256,128]{1,0:T(8,128)S(1)}, f32[256,128]{1,0:T(8,128)S(1)}, u32[]{:S(2)}, u32[]{:S(2)}) collective-permute-start(f32[256,128]{1,0:T(8,128)S(1)} %get-tuple-element.49), channel_id=1, source_target_pairs={{0,96},{16,112},{32,64},{48,80},{64,32},{80,48},{96,0},{112,16},{1... | collective-permute-start | bytes 393224 | tf_op jit(solution)/shard_map/ppermute | solution.py:404
  147.1 7.2 %collective-permute-start.14 = (f32[256,128]{1,0:T(8,128)S(1)}, f32[256,128]{1,0:T(8,128)S(1)}, u32[]{:S(2)}, u32[]{:S(2)}) collective-permute-start(f32[256,128]{1,0:T(8,128)S(1)} %get-tuple-element.50), channel_id=1, source_target_pairs={{0,64},{16,80},{32,96},{48,112},{64,0},{80,16},{96,32},{112,48},{1... | collective-permute-start | bytes 393224 | tf_op jit(solution)/shard_map/ppermute | solution.py:404
  148.2 7.0 %collective-permute-start.13 = (f32[256,128]{1,0:T(8,128)S(1)}, f32[256,128]{1,0:T(8,128)S(1)}, u32[]{:S(2)}, u32[]{:S(2)}) collective-permute-start(f32[256,128]{1,0:T(8,128)S(1)} %get-tuple-element.51), channel_id=1, source_target_pairs={{0,32},{16,48},{32,0},{48,16},{64,96},{80,112},{96,64},{112,80},{1... | collective-permute-start | bytes 393224 | tf_op jit(solution)/shard_map/ppermute | solution.py:404
  165.9 5.2 %collective-permute-start.20 = (f32[192,128]{1,0:T(8,128)S(1)}, f32[192,128]{1,0:T(8,128)S(1)}, u32[]{:S(2)}, u32[]{:S(2)}) collective-permute-start(f32[192,128]{1,0:T(8,128)S(1)} %slice_select_fusion), channel_id=1, source_target_pairs={{0,16},{16,0},{32,48},{48,32},{64,80},{80,64},{96,112},{112,96},{1... | collective-permute-start | bytes 294920 | tf_op jit(solution)/shard_map/ppermute | solution.py:420
  171.1 5.3 %collective-permute-start.23 = (f32[192,128]{1,0:T(8,128)S(1)}, f32[192,128]{1,0:T(8,128)S(1)}, u32[]{:S(2)}, u32[]{:S(2)}) collective-permute-start(f32[192,128]{1,0:T(8,128)S(1)} %select_add_fusion), channel_id=1, source_target_pairs={{0,96},{16,112},{32,64},{48,80},{64,32},{80,48},{96,0},{112,16},{1... | collective-permute-start | bytes 294920 | tf_op jit(solution)/shard_map/ppermute | solution.py:412
  172.3 5.1 %collective-permute-start.22 = (f32[192,128]{1,0:T(8,128)S(1)}, f32[192,128]{1,0:T(8,128)S(1)}, u32[]{:S(2)}, u32[]{:S(2)}) collective-permute-start(f32[192,128]{1,0:T(8,128)S(1)} %select_add_fusion), channel_id=1, source_target_pairs={{0,64},{16,80},{32,96},{48,112},{64,0},{80,16},{96,32},{112,48},{1... | collective-permute-start | bytes 294920 | tf_op jit(solution)/shard_map/ppermute | solution.py:412
  173.3 5.6 %collective-permute-start.21 = (f32[192,128]{1,0:T(8,128)S(1)}, f32[192,128]{1,0:T(8,128)S(1)}, u32[]{:S(2)}, u32[]{:S(2)}) collective-permute-start(f32[192,128]{1,0:T(8,128)S(1)} %select_add_fusion), channel_id=1, source_target_pairs={{0,32},{16,48},{32,0},{48,16},{64,96},{80,112},{96,64},{112,80},{1... | collective-permute-start | bytes 294920 | tf_op jit(solution)/shard_map/ppermute | solution.py:412
  180.2 5.4 %collective-permute-start.24 = (f32[192,128]{1,0:T(8,128)S(1)}, f32[192,128]{1,0:T(8,128)S(1)}, u32[]{:S(2)}, u32[]{:S(2)}) collective-permute-start(f32[192,128]{1,0:T(8,128)S(1)} %add_add_fusion.2), channel_id=1, source_target_pairs={{0,4},{1,5},{2,6},{3,7},{4,0},{5,1},{6,2},{7,3},{8,12},{9,13},{10,... | collective-permute-start | bytes 294920 | tf_op jit(solution)/shard_map/ppermute | solution.py:412
  185.7 5.8 %collective-permute-start.29 = (f32[192,128]{1,0:T(8,128)S(1)}, f32[192,128]{1,0:T(8,128)S(1)}, u32[]{:S(2)}, u32[]{:S(2)}) collective-permute-start(f32[192,128]{1,0:T(8,128)S(1)} %add_add_fusion.1), channel_id=1, source_target_pairs={{0,3},{1,2},{2,1},{3,0},{4,7},{5,6},{6,5},{7,4},{8,11},{9,10},{10,... | collective-permute-start | bytes 294920 | tf_op jit(solution)/shard_map/ppermute | solution.py:412
  186.2 5.3 %collective-permute-start.28 = (f32[192,128]{1,0:T(8,128)S(1)}, f32[192,128]{1,0:T(8,128)S(1)}, u32[]{:S(2)}, u32[]{:S(2)}) collective-permute-start(f32[192,128]{1,0:T(8,128)S(1)} %add_add_fusion.1), channel_id=1, source_target_pairs={{0,2},{1,3},{2,0},{3,1},{4,6},{5,7},{6,4},{7,5},{8,10},{9,11},{10,... | collective-permute-start | bytes 294920 | tf_op jit(solution)/shard_map/ppermute | solution.py:412
  192.1 5.2 %collective-permute-start.30 = (f32[192,128]{1,0:T(8,128)S(1)}, f32[192,128]{1,0:T(8,128)S(1)}, u32[]{:S(2)}, u32[]{:S(2)}) collective-permute-start(f32[192,128]{1,0:T(8,128)S(1)} %add_add_fusion), channel_id=1, source_target_pairs={{0,16},{16,0},{32,48},{48,32},{64,80},{80,64},{96,112},{112,96},{1... | collective-permute-start | bytes 294920 | tf_op jit(solution)/shard_map/ppermute | solution.py:424
  (16 other events, 98.3 us)

commit v3 on v2

--- a/solution.py
+++ b/solution.py
@@ -23,7 +23,8 @@
 FILL_STEPS = GROUPS // STEP_GROUPS
 CHUNK = 256
 CHUNKS = SIDE // CHUNK
-SUMS = 24
+PART = NB // N_ROW
+SLICE = 3 * PART
 
 HIGH = lax.Precision.HIGHEST
 F32, BF16 = jnp.float32, jnp.bfloat16
@@ -160,7 +161,7 @@
 def backward_kernel(hi_any, lo_any, own, z1, z2, z3, far, extra, pay, hi, lo, xr, sems):
     begin_fetches(True, hi_any, lo_any, hi, lo, sems)
     for c in range(CHUNKS):
-        piece = (own, z1, z2, z3)[c][...] if c < 4 else far[(c - 4) * CHUNK : (c - 3) * CHUNK, :]
+        piece = (own, z1, z2, z3)[c][0:ROWS, :] if c < 4 else far[(c - 4) * CHUNK : (c - 3) * CHUNK, :]
         high, low = split(piece.T)
         xr[0:128, c * CHUNK : (c + 1) * CHUNK] = high
         xr[128:256, c * CHUNK : (c + 1) * CHUNK] = low
@@ -175,7 +176,7 @@
         for q in range(2):
             p = j * 2 + q
             pay[p, 0:128, :] = out[q * 128 : (q + 1) * 128]
-            pay[p, 128:, :] = extra[p]
+            pay[p, 128:, :] = extra[p] if len(extra.shape) == 3 else extra[...]
         return c
 
     lax.fori_loop(0, CHUNKS, chunk, 0)
@@ -185,7 +186,7 @@
 ANYWHERE = pl.BlockSpec(memory_space=pl.ANY)
 PRODUCT = {
     "compiler_params": pltpu.CompilerParams(vmem_limit_bytes=50 * MIB),
-    "cost_estimate": pl.CostEstimate(flops=4 * 10**9, bytes_accessed=20 * 10**6, transcendentals=0),
+    "cost_estimate": pl.CostEstimate(flops=10**6, bytes_accessed=10**5, transcendentals=0),
 }
 
 
@@ -217,7 +218,7 @@
             pltpu.VMEM((256, SIDE), BF16),
             pltpu.SemaphoreType.DMA((2, CHUNKS)),
         ],
-        out_shape=jax.ShapeDtypeStruct((N_COL, 128 + extra.shape[1], NB), F32),
+        out_shape=jax.ShapeDtypeStruct((N_COL, 128 + extra.shape[-2], NB), F32),
         name="backward",
         **PRODUCT,
     )(hi, lo, *pieces, extra)
@@ -238,7 +239,7 @@
     return (deg[...] - SHIFT) * v[...] - sums - jnp.concatenate(parts, axis=0)
 
 
-def first_kernel(v, deg, s0, s1, s2, s3, arrived, image, pay, needs):
+def first_kernel(v, deg, s0, s1, s2, s3, arrived, image, pay, needs, slices):
     needs[...] = arrived[:, 128:136, :]
     y = image_of(v, deg, s0, s1, s2, s3, arrived, needs)
     image[...] = y
@@ -251,10 +252,10 @@
             pay[p, q * BS : (q + 1) * BS, :] = block
     x = v[...]
     xt, yt = x.T, y.T
-    for at, gram in ((128, mm(xt, x)), (136, mm(xt, y)), (144, mm(yt, y))):
+    for n, gram in enumerate((mm(xt, x), mm(xt, y), mm(yt, y))):
         gram = gram * (1.0 / NROWS)
-        for p in range(N_COL):
-            pay[p, at : at + 8, :] = gram[8 * p : 8 * p + 8, :]
+        for r in range(N_ROW):
+            slices[r, n * PART : (n + 1) * PART, :] = gram[r * PART : (r + 1) * PART, :]
 
 
 def first_image(v, deg, sums, arrived):
@@ -262,8 +263,9 @@
         first_kernel,
         out_shape=[
             jax.ShapeDtypeStruct((ROWS, NB), F32),
-            jax.ShapeDtypeStruct((N_COL, 128 + SUMS, NB), F32),
+            jax.ShapeDtypeStruct((N_COL, 128, NB), F32),
             jax.ShapeDtypeStruct((N_COL, 8, NB), F32),
+            jax.ShapeDtypeStruct((N_ROW, SLICE, NB), F32),
         ],
         compiler_params=pltpu.CompilerParams(vmem_limit_bytes=32 * MIB),
         name="first_image",
@@ -321,10 +323,28 @@
     )
 
 
-def second_kernel(x_ref, y_ref, deg, s0, s1, s2, s3, arrived, needs, grams, alpha, beta, v0_ref, v1_ref, w_ref, gram):
-    y2 = image_of(y_ref, deg, s0, s1, s2, s3, arrived, needs)
+def image_kernel(v, deg, s0, s1, s2, s3, arrived, needs, image):
+    image[...] = image_of(v, deg, s0, s1, s2, s3, arrived, needs)
+
+
+def image(v, deg, sums, arrived, needs):
+    return pl.pallas_call(
+        image_kernel,
+        out_shape=jax.ShapeDtypeStruct((ROWS, NB), F32),
+        compiler_params=pltpu.CompilerParams(vmem_limit_bytes=32 * MIB),
+        name="image",
+    )(v, deg, *sums, arrived, needs)
+
+
+def second_kernel(place, x_ref, y_ref, y2_ref, near, far, alpha, beta, v0_ref, v1_ref, w_ref, gram, grams):
+    z, core = place[0], place[1]
+    for k in range(4):
+        here = slice(k * SLICE, (k + 1) * SLICE)
+        grams[(z ^ k) * 2 + core] = near[here, :]
+        grams[(z ^ k) * 2 + (1 - core)] = far[here, :]
+    y2 = y2_ref[...]
     xx, xy, yy = (
-        jnp.concatenate([grams[p, at : at + 8, :] for p in range(N_COL)], axis=0) for at in (0, 8, 16)
+        jnp.concatenate([grams[r, n * PART : (n + 1) * PART, :] for r in range(N_ROW)], axis=0) for n in range(3)
     )
     x, y = x_ref[...], y_ref[...]
     _, inv0 = factor(xx)
@@ -344,15 +364,18 @@
     gram[256:384, :] = mm(w.T, w) * (1.0 / NROWS)
 
 
-def second_image(x, y, deg, sums, arrived, needs, grams):
+def second_block(*args):
     square = jax.ShapeDtypeStruct((NB, NB), F32)
     owned = jax.ShapeDtypeStruct((ROWS, NB), F32)
     return pl.pallas_call(
         second_kernel,
+        in_specs=[pl.BlockSpec(memory_space=pltpu.SMEM)] + [VMEM] * 5,
+        out_specs=[VMEM] * 6,
         out_shape=[square, square, owned, owned, owned, jax.ShapeDtypeStruct((3 * NB, NB), F32)],
+        scratch_shapes=[pltpu.VMEM((N_ROW, SLICE, NB), F32)],
         compiler_params=pltpu.CompilerParams(vmem_limit_bytes=32 * MIB),
-        name="second_image",
-    )(x, y, deg, *sums, arrived, needs, grams)
+        name="second_block",
+    )(*args)
 
 
 def last_kernel(v0, v1, w, gram, alpha0, beta0, alphas, betas, basis):
@@ -398,6 +421,15 @@
     return [own, *three, far]
 
 
+def row_pieces_and_sums(own, slices, z, core):
+    chips = slices.reshape(N_ROW // 2, 2 * SLICE, NB)
+    three = [lax.ppermute(jnp.concatenate([own, chips[z ^ k]]), "row", along_z(k)) for k in (1, 2, 3)]
+    a, b, c = (got[ROWS:] for got in three)
+    pair = ((chips[z] + a) + (b + c)).reshape(2, SLICE, NB)
+    far = lax.ppermute(jnp.concatenate([own, *(got[:ROWS] for got in three), pair[1 - core]]), "row", CORE)
+    return [own, *three, far], pair[core] + far[4 * ROWS :]
+
+
 def row_sums(keep, send):
     other = lax.ppermute(send, "row", CORE)
     parts = [keep[k] + other[k] for k in range(4)]
@@ -409,7 +441,8 @@
 
 
 def ring_sum(x, axis, shift):
-    return x + sum(lax.ppermute(x, axis, shift(k)) for k in (1, 2, 3))
+    a, b, c = (lax.ppermute(x, axis, shift(k)) for k in (1, 2, 3))
+    return (x + a) + (b + c)
 
 
 def sum_all(x):
@@ -442,21 +475,20 @@
     pieces = row_pieces(start_block, hi)
     back = swap(backward(hi, lo, pieces, needs_out))
     sums = row_sums(*forward(True, need, hi, lo, cols))
-    y, pay, needs = first_image(start_block, deg, sums, back)
+    y, pay, needs, slices = first_image(start_block, deg, sums, back)
 
     cols = swap(pay)
-    pieces = row_pieces(y)
-    back = backward(hi, lo, pieces, jnp.zeros((N_COL, 8, NB), F32))
+    pieces, part = row_pieces_and_sums(y, slices, z, core)
+    back = backward(hi, lo, pieces, part)
     cols, back = lax.optimization_barrier((cols, back))
     back = swap(back)
-    keep, send = forward(False, need, hi, lo, cols)
-    cols, keep, send = lax.optimization_barrier((cols, keep, send))
-    part = cols[:, 128:, :].sum(0)
-    part = part + lax.ppermute(part, "row", CORE)
-    part = ring_sum(part, "row", along_z)
-    grams = swap(jnp.broadcast_to(part[None], (N_COL, SUMS, NB)))
-    sums = row_sums(keep, send)
-    alpha, beta, v0, v1, w, gram = second_image(start_block, y, deg, sums, back, needs, grams)
+    sums = row_sums(*forward(False, need, hi, lo, cols))
+    back, *sums = lax.optimization_barrier((back, *sums))
+    part = back[:, 128:, :].sum(0)
+    near = jnp.concatenate([part, *(lax.ppermute(part, "row", along_z(k)) for k in (1, 2, 3))])
+    far = lax.ppermute(near, "row", CORE)
+    y2 = image(y, deg, sums, back, needs)
+    alpha, beta, v0, v1, w, gram = second_block(jnp.stack([z, core]), start_block, y, y2, near, far)
     return tuple(last_block(v0, v1, w, sum_all(gram), alpha, beta))
 
 

time: 203 us -> 192 us (0.946)
  blocking collectives: 13.4 us -> 0 us
  Pallas kernels: 69.8 us -> 72.2 us
    all_to_all x1 -> x0, blocking collectives: 13.4 us -> none  [swap(): return lax.all_to_all(x, 'col', 0, 0)]
    ppermute x13 -> x17, starting transfers between devices: 13.7 us -> 25.8 us  [the longest x9 10 us: ring_sum(): a, b, c = (lax.ppermute(x, axis, shift(k)) for k in (1, 2, 3))]
    ppermute x13 -> x17, waiting for transfers between devices: 14.2 us -> 21.2 us  [the longest x9 11.4 us: ring_sum(): a, b, c = (lax.ppermute(x, axis, shift(k)) for k in (1, 2, 3))]
    ppermute x2 -> x1, starting transfers between devices: 5.93 us -> 0.16 us  [row_pieces(): far = lax.ppermute(jnp.concatenate([own, *three]), 'row', CORE)]
    ppermute x6 -> x3, waiting for transfers between devices: 4.74 us -> 0.01 us  [row_pieces(): three = [lax.ppermute(own, 'row', along_z(k)) for k in (1, 2, 3)]]
    all_to_all x4, starting transfers between devices: 24.8 us -> 29.1 us  [swap(): return lax.all_to_all(x, 'col', 0, 0)]
    ppermute x1, starting transfers between devices: 4.25 us -> 0.43 us  [sum_all(): here = here + lax.ppermute(there, 'row', CORE)]
    ppermute x6 -> x3, starting transfers between devices: 7.84 us -> 4.51 us  [row_pieces(): three = [lax.ppermute(own, 'row', along_z(k)) for k in (1, 2, 3)]]
  transfers between devices with their start and end apart: 35 -> 35, of which waited for: 26 -> 27; matrix products, arithmetic and copies ran while one was open for 1% -> 1% of each run, Pallas kernels for 22% -> 29%
where the time goes in v3:
time: 192 us
  starting transfers between devices  73.5 us (38%)
  Pallas kernels  72.2 us (38%)
  waiting for transfers between devices  40.1 us (21%)
  local copies, waits for them, and re-layouts  2.96 us (2%)
    all_to_all x4, starting transfers between devices, swap(): return lax.all_to_all(x, 'col', 0, 0)  29.1 us
    pallas_call x2, Pallas kernels, backward(): pl.pallas_call(backward_kernel, in_specs=[ANYWHERE, ANYWHERE] + [VMEM] *...  19.2 us
    pallas_call x1, Pallas kernels, dense_of(): pl.pallas_call(dense_kernel, grid_spec=pltpu.PrefetchScalarGridSpec(num_s...  18.7 us
    pallas_call x2, Pallas kernels, forward(): pl.pallas_call(functools.partial(forward_kernel, whole), in_specs=[pl.Blo...  16.9 us
    ppermute x9, waiting for transfers between devices, ring_sum(): a, b, c = (lax.ppermute(x, axis, shift(k)) for k in (1, 2, 3))  11.4 us
    ppermute x6, waiting for transfers between devices, row_sums(): lax.ppermute(parts[k], 'row', along_z(k))  10.7 us
    ppermute x9, starting transfers between devices, ring_sum(): a, b, c = (lax.ppermute(x, axis, shift(k)) for k in (1, 2, 3))  10 us
    pallas_call x1, Pallas kernels, second_block(): pl.pallas_call(second_kernel, in_specs=[pl.BlockSpec(memory_space=pltpu.S...  9.95 us
  transfers between devices with their start and end apart: 35, of which 27 were waited for; matrix products, arithmetic and copies ran while one was open for 1% of the time, Pallas kernels for 29%

profile of v3, /device:TPU:1, one launch (start us, length us, event | category | flops | bytes accessed | tf_op | source)
XLA Modules:
  0.0 192.2 jit_solution(323291829047760143)
XLA Ops:
  0.6 2.4 %broadcast_in_dim.7 = f32[16,256,128]{2,1,0:T(8,128)} broadcast(f32[256,128]{1,0:T(8,128)} %x_ref.1), dimensions={1,2} | broadcast | bytes 2228224 | tf_op jit(solution)/shard_map/broadcast_in_dim | solution.py:473
  3.1 7.7 %all-to-all-start = ((f32[16,256,128]{2,1,0:T(8,128)}), f32[16,256,128]{2,1,0:T(8,128)S(1)}, u32[]{:S(2)}, u32[]{:S(2)}) async-start(f32[16,256,128]{2,1,0:T(8,128)} %broadcast_in_dim.7), calls=%async_computation | async-start | bytes 4194304 | tf_op jit(solution)/shard_map/all_to_all | solution.py:440
  10.8 3.8 %collective-permute-start.6 = (f32[256,128]{1,0:T(8,128)S(1)}, f32[256,128]{1,0:T(8,128)S(1)}, u32[]{:S(2)}, u32[]{:S(2)}) collective-permute-start(f32[256,128]{1,0:T(8,128)S(1)} %copy-done), channel_id=1, source_target_pairs={{0,96},{16,112},{32,64},{48,80},{64,32},{80,48},{96,0},{112,16},{1... | collective-permute-start | bytes 393224 | tf_op jit(solution)/shard_map/ppermute | solution.py:417
  16.6 18.7 %dense.1 = (bf16[2048,2048]{1,0:T(8,128)(2,1)}, bf16[2048,2048]{1,0:T(8,128)(2,1)}) custom-call(s32[384]{0:T(512)} %fusion.13.rows_ref, s32[384]{0:T(512)} %slots_ref.1, s32[1]{0:T(128)S(6)} %copy.19.live_ref, f32[48,256,128]{2,1,0:T(8,128)} %bitcast.39), custom_call_target="tpu_custom_call" | custom-call | flops 10000000 | bytes 50000000 | tf_op jit(solution)/shard_map/dense/pallas_call | solution.py:88
  38.3 9.5 %backward.2 = f32[16,136,128]{2,1,0:T(8,128)} custom-call(bf16[2048,2048]{1,0:T(8,128)(2,1)} %get-tuple-element.29.hi_any, bf16[2048,2048]{1,0:T(8,128)(2,1)} %get-tuple-element.30.lo_any, f32[256,128]{1,0:T(8,128)S(1)} %copy-done, f32[256,128]{1,0:T(8,128)S(1)} %collective-permute-done.4.z1, f32[256,128]{1,0:T(8,128)S(1)} %collective-permute-done.5.z2, ...), custom_call_target="tpu_custom_call" | custom-call | flops 1000000 | bytes 100000 | tf_op jit(solution)/shard_map/backward/pallas_call | solution.py:211
  47.9 7.9 %all-to-all-start.1 = ((f32[16,136,128]{2,1,0:T(8,128)}), f32[16,136,128]{2,1,0:T(8,128)S(1)}, u32[]{:S(2)}, u32[]{:S(2)}) async-start(f32[16,136,128]{2,1,0:T(8,128)} %backward.2), calls=%async_computation.1 | async-start | bytes 2228224 | tf_op jit(solution)/shard_map/all_to_all | solution.py:440
  56.0 8.4 %forward.2 = (f32[4,256,128]{2,1,0:T(8,128)S(1)}, f32[4,256,128]{2,1,0:T(8,128)S(1)}) custom-call(s32[32]{0:T(128)S(1)} %reshape.32.need_ref, bf16[2048,2048]{1,0:T(8,128)(2,1)} %get-tuple-element.29.hi_any, bf16[2048,2048]{1,0:T(8,128)(2,1)} %get-tuple-element.30.lo_any, f32[16,256,128]{2,1,0:T(8,128)S(1)} %all-to-all-done.cols), custom_call_target="tpu_custom_call" | custom-call | flops 1000000 | bytes 100000 | tf_op jit(solution)/shard_map/forward/pallas_call | solution.py:194
  66.8 3.5 %collective-permute-start.3 = (f32[256,128]{1,0:T(8,128)S(1)}, f32[256,128]{1,0:T(8,128)S(1)}, u32[]{:S(2)}, u32[]{:S(2)}) collective-permute-start(f32[256,128]{1,0:T(8,128)S(1)} %get-tuple-element.59), channel_id=1, source_target_pairs={{0,96},{16,112},{32,64},{48,80},{64,32},{80,48},{96,0},{112,16},{1... | collective-permute-start | bytes 393224 | tf_op jit(solution)/shard_map/ppermute | solution.py:436
  72.1 3.6 %collective-permute-done.3.s3 = f32[256,128]{1,0:T(8,128)S(1)} collective-permute-done((f32[256,128]{1,0:T(8,128)S(1)}, f32[256,128]{1,0:T(8,128)S(1)}, u32[]{:S(2)}, u32[]{:S(2)}) %collective-permute-start.3) | collective-permute-done | bytes 131104 | tf_op jit(solution)/shard_map/ppermute | solution.py:436
  77.1 2.2 %first_image.1 = (f32[256,128]{1,0:T(8,128)S(1)}, f32[16,128,128]{2,1,0:T(8,128)}, f32[16,8,128]{2,1,0:T(8,128)S(1)}, f32[8,48,128]{2,1,0:T(8,128)S(1)}) custom-call(f32[256,128]{1,0:T(8,128)S(1)} %copy-done, f32[256,128]{1,0:T(8,128)S(1)} %broadcast_in_dim.6.deg, f32[256,128]{1,0:T(8,128)S(1)} %get-tuple-element.62.s0, ...), custom_call_target="tpu_custom_call" | custom-call | tf_op jit(solution)/shard_map/first_image/pallas_call | solution.py:262
  80.0 6.9 %all-to-all-start.2 = ((f32[16,128,128]{2,1,0:T(8,128)}), f32[16,128,128]{2,1,0:T(8,128)S(1)}, u32[]{:S(2)}, u32[]{:S(2)}) async-start(f32[16,128,128]{2,1,0:T(8,128)} %get-tuple-element.37), calls=%async_computation.2 | async-start | bytes 2097152 | tf_op jit(solution)/shard_map/all_to_all | solution.py:440
  90.1 4.9 %collective-permute-done.9.z2 = f32[352,128]{1,0:T(8,128)S(1)} collective-permute-done((f32[352,128]{1,0:T(8,128)S(1)}, f32[352,128]{1,0:T(8,128)S(1)}, u32[]{:S(2)}, u32[]{:S(2)}) %collective-permute-start.9) | collective-permute-done | bytes 180256 | tf_op jit(solution)/shard_map/ppermute | solution.py:426
  95.6 3.8 %collective-permute-start.11 = (f32[1072,128]{1,0:T(8,128)S(1)}, f32[1072,128]{1,0:T(8,128)S(1)}, u32[]{:S(2)}, u32[]{:S(2)}) collective-permute-start(f32[1072,128]{1,0:T(8,128)S(1)} %bitcast_dynamic-update-slice_fusion), channel_id=1, source_target_pairs={{0,16},{16,0},{32,48},{48,32},{64,80},{80,64},{96,112},{112,96},{1... | collective-permute-start | bytes 1646600 | tf_op jit(solution)/shard_map/ppermute | solution.py:429
  100.9 9.7 %backward.3 = f32[16,176,128]{2,1,0:T(8,128)} custom-call(bf16[2048,2048]{1,0:T(8,128)(2,1)} %get-tuple-element.29.hi_any, bf16[2048,2048]{1,0:T(8,128)(2,1)} %get-tuple-element.30.lo_any, f32[256,128]{1,0:T(8,128)S(1)} %get-tuple-element.36.own.v.y_ref, f32[352,128]{1,0:T(8,128)S(1)} %collective-permute-done.8.z1, ...), custom_call_target="tpu_custom_call" | custom-call | flops 1000000 | bytes 100000 | tf_op jit(solution)/shard_map/backward/pallas_call | solution.py:211
  110.6 6.6 %all-to-all-start.3 = ((f32[16,176,128]{2,1,0:T(8,128)}), f32[16,176,128]{2,1,0:T(8,128)S(1)}, u32[]{:S(2)}, u32[]{:S(2)}) async-start(f32[16,176,128]{2,1,0:T(8,128)} %backward.3), calls=%async_computation.3 | async-start | bytes 2883584 | tf_op jit(solution)/shard_map/all_to_all | solution.py:440
  117.2 8.4 %forward.3 = (f32[4,256,128]{2,1,0:T(8,128)S(1)}, f32[4,256,128]{2,1,0:T(8,128)S(1)}) custom-call(s32[32]{0:T(128)S(1)} %reshape.32.need_ref, bf16[2048,2048]{1,0:T(8,128)(2,1)} %get-tuple-element.29.hi_any, bf16[2048,2048]{1,0:T(8,128)(2,1)} %get-tuple-element.30.lo_any, f32[16,128,128]{2,1,0:T(8,128)S(1)} %all-to-all-done.2.cols), custom_call_target="tpu_custom_call" | custom-call | flops 1000000 | bytes 100000 | tf_op jit(solution)/shard_map/forward/pallas_call | solution.py:194
  131.3 2.7 %collective-permute-done.15.s3 = f32[256,128]{1,0:T(8,128)S(1)} collective-permute-done((f32[256,128]{1,0:T(8,128)S(1)}, f32[256,128]{1,0:T(8,128)S(1)}, u32[]{:S(2)}, u32[]{:S(2)}) %collective-permute-start.15) | collective-permute-done | bytes 131104 | tf_op jit(solution)/shard_map/ppermute | solution.py:436
  143.2 5.0 %collective-permute-start.19 = (f32[192,128]{1,0:T(8,128)S(1)}, f32[192,128]{1,0:T(8,128)S(1)}, u32[]{:S(2)}, u32[]{:S(2)}) collective-permute-start(f32[192,128]{1,0:T(8,128)S(1)} %pad_maximum_fusion.5.near), channel_id=1, source_target_pairs={{0,16},{16,0},{32,48},{48,32},{64,80},{80,64},{96,112},{112,96},{1... | collective-permute-start | bytes 294920 | tf_op jit(solution)/shard_map/ppermute | solution.py:489
  149.1 9.9 %second_block.1 = (f32[128,128]{1,0:T(8,128)S(1)}, f32[128,128]{1,0:T(8,128)S(1)}, f32[256,128]{1,0:T(8,128)S(1)}, f32[256,128]{1,0:T(8,128)S(1)}, f32[256,128]{1,0:T(8,128)S(1)}, /*index=5*/f32[384,128]{1,0:T(8,128)S(1)}) custom-call(s32[2]{0:T(128)S(1)} %pad_add_fusion.place, f32[256,128]{1,0:T(8,128)S(1)} %copy-done, ...), custom_call_target="tpu_custom_call" | custom-call | tf_op jit(solution)/shard_map/second_block/pallas_call | solution.py:370
  163.8 2.0 %collective-permute-done.23 = f32[192,128]{1,0:T(8,128)S(1)} collective-permute-done((f32[192,128]{1,0:T(8,128)S(1)}, f32[192,128]{1,0:T(8,128)S(1)}, u32[]{:S(2)}, u32[]{:S(2)}) %collective-permute-start.23) | collective-permute-done | bytes 98336 | tf_op jit(solution)/shard_map/ppermute | solution.py:444
  175.0 1.9 collective-permute-start.29
  179.8 2.1 %collective-permute-done.28 = f32[192,128]{1,0:T(8,128)S(1)} collective-permute-done((f32[192,128]{1,0:T(8,128)S(1)}, f32[192,128]{1,0:T(8,128)S(1)}, u32[]{:S(2)}, u32[]{:S(2)}) %collective-permute-start.28) | collective-permute-done | bytes 98336 | tf_op jit(solution)/shard_map/ppermute | solution.py:444
  181.9 4.5 %collective-permute-start.30 = (f32[192,128]{1,0:T(8,128)S(1)}, f32[192,128]{1,0:T(8,128)S(1)}, u32[]{:S(2)}, u32[]{:S(2)}) collective-permute-start(f32[192,128]{1,0:T(8,128)S(1)} %add_add_fusion), channel_id=1, source_target_pairs={{0,16},{16,0},{32,48},{48,32},{64,80},{80,64},{96,112},{112,96},{1... | collective-permute-start | bytes 294920 | tf_op jit(solution)/shard_map/ppermute | solution.py:457
  187.4 4.7 %last_block.1 = (f32[2,128,128]{2,1,0:T(8,128)}, f32[2,128,128]{2,1,0:T(8,128)}, f32[256,128]{1,0:T(8,128)}) custom-call(f32[256,128]{1,0:T(8,128)S(1)} %get-tuple-element.49.v0, f32[256,128]{1,0:T(8,128)S(1)} %get-tuple-element.50.v1, f32[256,128]{1,0:T(8,128)S(1)} %get-tuple-element.51.w, f32[384,128]{1,0:T(8,128)S(1)} %pad_maximum_fusion.4.gram, ...), custom_call_target="tpu_custom_call" | custom-call | tf_op jit(solution)/shard_map/last_block/pallas_call | solution.py:393
  (98 shorter events, 49.7 us)
Async XLA Ops:
  3.1 44.8 %all-to-all-start = ((f32[16,256,128]{2,1,0:T(8,128)}), f32[16,256,128]{2,1,0:T(8,128)S(1)}, u32[]{:S(2)}, u32[]{:S(2)}) async-start(f32[16,256,128]{2,1,0:T(8,128)} %broadcast_in_dim.7), calls=%async_computation | async-start | bytes 4194304 | tf_op jit(solution)/shard_map/all_to_all | solution.py:440
  10.8 24.5 %collective-permute-start.6 = (f32[256,128]{1,0:T(8,128)S(1)}, f32[256,128]{1,0:T(8,128)S(1)}, u32[]{:S(2)}, u32[]{:S(2)}) collective-permute-start(f32[256,128]{1,0:T(8,128)S(1)} %copy-done), channel_id=1, source_target_pairs={{0,96},{16,112},{32,64},{48,80},{64,32},{80,48},{96,0},{112,16},{1... | collective-permute-start | bytes 393224 | tf_op jit(solution)/shard_map/ppermute | solution.py:417
  14.6 20.6 %collective-permute-start.5 = (f32[256,128]{1,0:T(8,128)S(1)}, f32[256,128]{1,0:T(8,128)S(1)}, u32[]{:S(2)}, u32[]{:S(2)}) collective-permute-start(f32[256,128]{1,0:T(8,128)S(1)} %copy-done), channel_id=1, source_target_pairs={{0,64},{16,80},{32,96},{48,112},{64,0},{80,16},{96,32},{112,48},{1... | collective-permute-start | bytes 393224 | tf_op jit(solution)/shard_map/ppermute | solution.py:417
  14.6 20.6 %collective-permute-start.4 = (f32[256,128]{1,0:T(8,128)S(1)}, f32[256,128]{1,0:T(8,128)S(1)}, u32[]{:S(2)}, u32[]{:S(2)}) collective-permute-start(f32[256,128]{1,0:T(8,128)S(1)} %copy-done), channel_id=1, source_target_pairs={{0,32},{16,48},{32,0},{48,16},{64,96},{80,112},{96,64},{112,80},{1... | collective-permute-start | bytes 393224 | tf_op jit(solution)/shard_map/ppermute | solution.py:417
  47.9 24.3 %all-to-all-start.1 = ((f32[16,136,128]{2,1,0:T(8,128)}), f32[16,136,128]{2,1,0:T(8,128)S(1)}, u32[]{:S(2)}, u32[]{:S(2)}) async-start(f32[16,136,128]{2,1,0:T(8,128)} %backward.2), calls=%async_computation.1 | async-start | bytes 2228224 | tf_op jit(solution)/shard_map/all_to_all | solution.py:440
  66.8 9.0 %collective-permute-start.3 = (f32[256,128]{1,0:T(8,128)S(1)}, f32[256,128]{1,0:T(8,128)S(1)}, u32[]{:S(2)}, u32[]{:S(2)}) collective-permute-start(f32[256,128]{1,0:T(8,128)S(1)} %get-tuple-element.59), channel_id=1, source_target_pairs={{0,96},{16,112},{32,64},{48,80},{64,32},{80,48},{96,0},{112,16},{1... | collective-permute-start | bytes 393224 | tf_op jit(solution)/shard_map/ppermute | solution.py:436
  70.2 5.9 %collective-permute-start.2 = (f32[256,128]{1,0:T(8,128)S(1)}, f32[256,128]{1,0:T(8,128)S(1)}, u32[]{:S(2)}, u32[]{:S(2)}) collective-permute-start(f32[256,128]{1,0:T(8,128)S(1)} %get-tuple-element.60), channel_id=1, source_target_pairs={{0,64},{16,80},{32,96},{48,112},{64,0},{80,16},{96,32},{112,48},{1... | collective-permute-start | bytes 393224 | tf_op jit(solution)/shard_map/ppermute | solution.py:436
  70.2 6.8 %collective-permute-start.1 = (f32[256,128]{1,0:T(8,128)S(1)}, f32[256,128]{1,0:T(8,128)S(1)}, u32[]{:S(2)}, u32[]{:S(2)}) collective-permute-start(f32[256,128]{1,0:T(8,128)S(1)} %get-tuple-element.61), channel_id=1, source_target_pairs={{0,32},{16,48},{32,0},{48,16},{64,96},{80,112},{96,64},{112,80},{1... | collective-permute-start | bytes 393224 | tf_op jit(solution)/shard_map/ppermute | solution.py:436
  79.4 10.7 %collective-permute-start.8 = (f32[352,128]{1,0:T(8,128)S(1)}, f32[352,128]{1,0:T(8,128)S(1)}, u32[]{:S(2)}, u32[]{:S(2)}) collective-permute-start(f32[352,128]{1,0:T(8,128)S(1)} %get-tuple-element.70), channel_id=1, source_target_pairs={{0,32},{16,48},{32,0},{48,16},{64,96},{80,112},{96,64},{112,80},{1... | collective-permute-start | bytes 540680 | tf_op jit(solution)/shard_map/ppermute | solution.py:426
  80.0 30.6 %all-to-all-start.2 = ((f32[16,128,128]{2,1,0:T(8,128)}), f32[16,128,128]{2,1,0:T(8,128)S(1)}, u32[]{:S(2)}, u32[]{:S(2)}) async-start(f32[16,128,128]{2,1,0:T(8,128)} %get-tuple-element.37), calls=%async_computation.2 | async-start | bytes 2097152 | tf_op jit(solution)/shard_map/all_to_all | solution.py:440
  87.0 8.6 %collective-permute-start.10 = (f32[352,128]{1,0:T(8,128)S(1)}, f32[352,128]{1,0:T(8,128)S(1)}, u32[]{:S(2)}, u32[]{:S(2)}) collective-permute-start(f32[352,128]{1,0:T(8,128)S(1)} %get-tuple-element.68), channel_id=1, source_target_pairs={{0,96},{16,112},{32,64},{48,80},{64,32},{80,48},{96,0},{112,16},{1... | collective-permute-start | bytes 540680 | tf_op jit(solution)/shard_map/ppermute | solution.py:426
  88.8 6.2 %collective-permute-start.9 = (f32[352,128]{1,0:T(8,128)S(1)}, f32[352,128]{1,0:T(8,128)S(1)}, u32[]{:S(2)}, u32[]{:S(2)}) collective-permute-start(f32[352,128]{1,0:T(8,128)S(1)} %get-tuple-element.69), channel_id=1, source_target_pairs={{0,64},{16,80},{32,96},{48,112},{64,0},{80,16},{96,32},{112,48},{1... | collective-permute-start | bytes 540680 | tf_op jit(solution)/shard_map/ppermute | solution.py:426
  95.6 5.3 %collective-permute-start.11 = (f32[1072,128]{1,0:T(8,128)S(1)}, f32[1072,128]{1,0:T(8,128)S(1)}, u32[]{:S(2)}, u32[]{:S(2)}) collective-permute-start(f32[1072,128]{1,0:T(8,128)S(1)} %bitcast_dynamic-update-slice_fusion), channel_id=1, source_target_pairs={{0,16},{16,0},{32,48},{48,32},{64,80},{80,64},{96,112},{112,96},{1... | collective-permute-start | bytes 1646600 | tf_op jit(solution)/shard_map/ppermute | solution.py:429
  110.6 26.7 %all-to-all-start.3 = ((f32[16,176,128]{2,1,0:T(8,128)}), f32[16,176,128]{2,1,0:T(8,128)S(1)}, u32[]{:S(2)}, u32[]{:S(2)}) async-start(f32[16,176,128]{2,1,0:T(8,128)} %backward.3), calls=%async_computation.3 | async-start | bytes 2883584 | tf_op jit(solution)/shard_map/all_to_all | solution.py:440
  128.0 6.1 %collective-permute-start.15 = (f32[256,128]{1,0:T(8,128)S(1)}, f32[256,128]{1,0:T(8,128)S(1)}, u32[]{:S(2)}, u32[]{:S(2)}) collective-permute-start(f32[256,128]{1,0:T(8,128)S(1)} %get-tuple-element.55), channel_id=1, source_target_pairs={{0,96},{16,112},{32,64},{48,80},{64,32},{80,48},{96,0},{112,16},{1... | collective-permute-start | bytes 393224 | tf_op jit(solution)/shard_map/ppermute | solution.py:436
  129.7 6.0 %collective-permute-start.14 = (f32[256,128]{1,0:T(8,128)S(1)}, f32[256,128]{1,0:T(8,128)S(1)}, u32[]{:S(2)}, u32[]{:S(2)}) collective-permute-start(f32[256,128]{1,0:T(8,128)S(1)} %get-tuple-element.56), channel_id=1, source_target_pairs={{0,64},{16,80},{32,96},{48,112},{64,0},{80,16},{96,32},{112,48},{1... | collective-permute-start | bytes 393224 | tf_op jit(solution)/shard_map/ppermute | solution.py:436
  130.5 6.6 %collective-permute-start.13 = (f32[256,128]{1,0:T(8,128)S(1)}, f32[256,128]{1,0:T(8,128)S(1)}, u32[]{:S(2)}, u32[]{:S(2)}) collective-permute-start(f32[256,128]{1,0:T(8,128)S(1)} %get-tuple-element.57), channel_id=1, source_target_pairs={{0,32},{16,48},{32,0},{48,16},{64,96},{80,112},{96,64},{112,80},{1... | collective-permute-start | bytes 393224 | tf_op jit(solution)/shard_map/ppermute | solution.py:436
  143.2 5.9 %collective-permute-start.19 = (f32[192,128]{1,0:T(8,128)S(1)}, f32[192,128]{1,0:T(8,128)S(1)}, u32[]{:S(2)}, u32[]{:S(2)}) collective-permute-start(f32[192,128]{1,0:T(8,128)S(1)} %pad_maximum_fusion.5.near), channel_id=1, source_target_pairs={{0,16},{16,0},{32,48},{48,32},{64,80},{80,64},{96,112},{112,96},{1... | collective-permute-start | bytes 294920 | tf_op jit(solution)/shard_map/ppermute | solution.py:489
  160.5 5.3 %collective-permute-start.23 = (f32[192,128]{1,0:T(8,128)S(1)}, f32[192,128]{1,0:T(8,128)S(1)}, u32[]{:S(2)}, u32[]{:S(2)}) collective-permute-start(f32[192,128]{1,0:T(8,128)S(1)} %select_add_fusion), channel_id=1, source_target_pairs={{0,96},{16,112},{32,64},{48,80},{64,32},{80,48},{96,0},{112,16},{1... | collective-permute-start | bytes 294920 | tf_op jit(solution)/shard_map/ppermute | solution.py:444
  161.6 5.1 %collective-permute-start.22 = (f32[192,128]{1,0:T(8,128)S(1)}, f32[192,128]{1,0:T(8,128)S(1)}, u32[]{:S(2)}, u32[]{:S(2)}) collective-permute-start(f32[192,128]{1,0:T(8,128)S(1)} %select_add_fusion), channel_id=1, source_target_pairs={{0,64},{16,80},{32,96},{48,112},{64,0},{80,16},{96,32},{112,48},{1... | collective-permute-start | bytes 294920 | tf_op jit(solution)/shard_map/ppermute | solution.py:444
  162.7 5.5 %collective-permute-start.21 = (f32[192,128]{1,0:T(8,128)S(1)}, f32[192,128]{1,0:T(8,128)S(1)}, u32[]{:S(2)}, u32[]{:S(2)}) collective-permute-start(f32[192,128]{1,0:T(8,128)S(1)} %select_add_fusion), channel_id=1, source_target_pairs={{0,32},{16,48},{32,0},{48,16},{64,96},{80,112},{96,64},{112,80},{1... | collective-permute-start | bytes 294920 | tf_op jit(solution)/shard_map/ppermute | solution.py:444
  169.3 5.0 %collective-permute-start.25 = (f32[192,128]{1,0:T(8,128)S(1)}, f32[192,128]{1,0:T(8,128)S(1)}, u32[]{:S(2)}, u32[]{:S(2)}) collective-permute-start(f32[192,128]{1,0:T(8,128)S(1)} %add_add_fusion.2), channel_id=1, source_target_pairs={{0,8},{1,9},{2,10},{3,11},{4,12},{5,13},{6,14},{7,15},{8,0},{9,1},... | collective-permute-start | bytes 294920 | tf_op jit(solution)/shard_map/ppermute | solution.py:444
  169.9 5.1 %collective-permute-start.24 = (f32[192,128]{1,0:T(8,128)S(1)}, f32[192,128]{1,0:T(8,128)S(1)}, u32[]{:S(2)}, u32[]{:S(2)}) collective-permute-start(f32[192,128]{1,0:T(8,128)S(1)} %add_add_fusion.2), channel_id=1, source_target_pairs={{0,4},{1,5},{2,6},{3,7},{4,0},{5,1},{6,2},{7,3},{8,12},{9,13},{10,... | collective-permute-start | bytes 294920 | tf_op jit(solution)/shard_map/ppermute | solution.py:444
  181.9 5.4 %collective-permute-start.30 = (f32[192,128]{1,0:T(8,128)S(1)}, f32[192,128]{1,0:T(8,128)S(1)}, u32[]{:S(2)}, u32[]{:S(2)}) collective-permute-start(f32[192,128]{1,0:T(8,128)S(1)} %add_add_fusion), channel_id=1, source_target_pairs={{0,16},{16,0},{32,48},{48,32},{64,80},{80,64},{96,112},{112,96},{1... | collective-permute-start | bytes 294920 | tf_op jit(solution)/shard_map/ppermute | solution.py:457
  (17 other events, 124.4 us)

commit v4 on v3

--- a/solution.py
+++ b/solution.py
@@ -171,8 +171,8 @@
         v = xr[...]
         for copy in fetches(True, j, hi_any, lo_any, hi, lo, sems):
             copy.wait()
-        out = jnp.dot(v, hi[:, here], preferred_element_type=F32) + jnp.dot(v, lo[:, here], preferred_element_type=F32)
-        out = (out[:128] + out[128:]).T
+        out = jnp.dot(v, hi[:, here], preferred_element_type=F32)
+        out = (out[:128] + out[128:] + jnp.dot(v[:128], lo[:, here], preferred_element_type=F32)).T
         for q in range(2):
             p = j * 2 + q
             pay[p, 0:128, :] = out[q * 128 : (q + 1) * 128]

time: 192 us -> 191 us (level)
  Pallas kernels: 72.2 us -> 69.7 us
    pallas_call x2, Pallas kernels: 19.2 us -> 17.1 us  [backward(): pl.pallas_call(backward_kernel, in_specs=[ANYWHERE, ANYWHERE] + [VMEM] *...]
  transfers between devices with their start and end apart: 35 -> 35, of which waited for: 27 -> 26; matrix products, arithmetic and copies ran while one was open for 1% -> 1% of each run, Pallas kernels for 29% -> 28%
where the time goes in v4:
time: 191 us; the launch traced here: 190 us
  starting transfers between devices  73.9 us (39%)
  Pallas kernels  69.7 us (36%)
  waiting for transfers between devices  39.9 us (21%)
  local copies, waits for them, and re-layouts  2.96 us (2%)
    all_to_all x4, starting transfers between devices, swap(): return lax.all_to_all(x, 'col', 0, 0)  28.9 us
    pallas_call x1, Pallas kernels, dense_of(): pl.pallas_call(dense_kernel, grid_spec=pltpu.PrefetchScalarGridSpec(num_s...  18.3 us
    pallas_call x2, Pallas kernels, backward(): pl.pallas_call(backward_kernel, in_specs=[ANYWHERE, ANYWHERE] + [VMEM] *...  17.1 us
    pallas_call x2, Pallas kernels, forward(): pl.pallas_call(functools.partial(forward_kernel, whole), in_specs=[pl.Blo...  16.9 us
    ppermute x9, waiting for transfers between devices, ring_sum(): a, b, c = (lax.ppermute(x, axis, shift(k)) for k in (1, 2, 3))  11.4 us
    ppermute x9, starting transfers between devices, ring_sum(): a, b, c = (lax.ppermute(x, axis, shift(k)) for k in (1, 2, 3))  10 us
    pallas_call x1, Pallas kernels, second_block(): pl.pallas_call(second_kernel, in_specs=[pl.BlockSpec(memory_space=pltpu.S...  9.95 us
    ppermute x6, waiting for transfers between devices, row_sums(): lax.ppermute(parts[k], 'row', along_z(k))  9.88 us
  transfers between devices with their start and end apart: 35, of which 26 were waited for; matrix products, arithmetic and copies ran while one was open for 1% of the time, Pallas kernels for 28%

profile of v4, /device:TPU:1, one launch (start us, length us, event | category | flops | bytes accessed | tf_op | source)
XLA Modules:
  0.0 189.9 jit_solution(1673829753640438630)
XLA Ops:
  0.6 2.4 %broadcast_in_dim.7 = f32[16,256,128]{2,1,0:T(8,128)} broadcast(f32[256,128]{1,0:T(8,128)} %x_ref.1), dimensions={1,2} | broadcast | bytes 2228224 | tf_op jit(solution)/shard_map/broadcast_in_dim | solution.py:473
  3.1 7.7 %all-to-all-start = ((f32[16,256,128]{2,1,0:T(8,128)}), f32[16,256,128]{2,1,0:T(8,128)S(1)}, u32[]{:S(2)}, u32[]{:S(2)}) async-start(f32[16,256,128]{2,1,0:T(8,128)} %broadcast_in_dim.7), calls=%async_computation | async-start | bytes 4194304 | tf_op jit(solution)/shard_map/all_to_all | solution.py:440
  10.8 3.8 %collective-permute-start.6 = (f32[256,128]{1,0:T(8,128)S(1)}, f32[256,128]{1,0:T(8,128)S(1)}, u32[]{:S(2)}, u32[]{:S(2)}) collective-permute-start(f32[256,128]{1,0:T(8,128)S(1)} %copy-done), channel_id=1, source_target_pairs={{0,96},{16,112},{32,64},{48,80},{64,32},{80,48},{96,0},{112,16},{1... | collective-permute-start | bytes 393224 | tf_op jit(solution)/shard_map/ppermute | solution.py:417
  16.6 18.3 %dense.1 = (bf16[2048,2048]{1,0:T(8,128)(2,1)}, bf16[2048,2048]{1,0:T(8,128)(2,1)}) custom-call(s32[384]{0:T(512)} %fusion.13.rows_ref, s32[384]{0:T(512)} %slots_ref.1, s32[1]{0:T(128)S(6)} %copy.19.live_ref, f32[48,256,128]{2,1,0:T(8,128)} %bitcast.39), custom_call_target="tpu_custom_call" | custom-call | flops 10000000 | bytes 50000000 | tf_op jit(solution)/shard_map/dense/pallas_call | solution.py:88
  38.1 8.5 %backward.2 = f32[16,136,128]{2,1,0:T(8,128)} custom-call(bf16[2048,2048]{1,0:T(8,128)(2,1)} %get-tuple-element.29.hi_any, bf16[2048,2048]{1,0:T(8,128)(2,1)} %get-tuple-element.30.lo_any, f32[256,128]{1,0:T(8,128)S(1)} %copy-done, f32[256,128]{1,0:T(8,128)S(1)} %collective-permute-done.4.z1, f32[256,128]{1,0:T(8,128)S(1)} %collective-permute-done.5.z2, ...), custom_call_target="tpu_custom_call" | custom-call | flops 1000000 | bytes 100000 | tf_op jit(solution)/shard_map/backward/pallas_call | solution.py:211
  46.6 7.7 %all-to-all-start.1 = ((f32[16,136,128]{2,1,0:T(8,128)}), f32[16,136,128]{2,1,0:T(8,128)S(1)}, u32[]{:S(2)}, u32[]{:S(2)}) async-start(f32[16,136,128]{2,1,0:T(8,128)} %backward.2), calls=%async_computation.1 | async-start | bytes 2228224 | tf_op jit(solution)/shard_map/all_to_all | solution.py:440
  54.5 8.4 %forward.2 = (f32[4,256,128]{2,1,0:T(8,128)S(1)}, f32[4,256,128]{2,1,0:T(8,128)S(1)}) custom-call(s32[32]{0:T(128)S(1)} %reshape.32.need_ref, bf16[2048,2048]{1,0:T(8,128)(2,1)} %get-tuple-element.29.hi_any, bf16[2048,2048]{1,0:T(8,128)(2,1)} %get-tuple-element.30.lo_any, f32[16,256,128]{2,1,0:T(8,128)S(1)} %all-to-all-done.cols), custom_call_target="tpu_custom_call" | custom-call | flops 1000000 | bytes 100000 | tf_op jit(solution)/shard_map/forward/pallas_call | solution.py:194
  65.3 2.8 %collective-permute-start.3 = (f32[256,128]{1,0:T(8,128)S(1)}, f32[256,128]{1,0:T(8,128)S(1)}, u32[]{:S(2)}, u32[]{:S(2)}) collective-permute-start(f32[256,128]{1,0:T(8,128)S(1)} %get-tuple-element.59), channel_id=1, source_target_pairs={{0,96},{16,112},{32,64},{48,80},{64,32},{80,48},{96,0},{112,16},{1... | collective-permute-start | bytes 393224 | tf_op jit(solution)/shard_map/ppermute | solution.py:436
  70.7 3.0 %collective-permute-done.3.s3 = f32[256,128]{1,0:T(8,128)S(1)} collective-permute-done((f32[256,128]{1,0:T(8,128)S(1)}, f32[256,128]{1,0:T(8,128)S(1)}, u32[]{:S(2)}, u32[]{:S(2)}) %collective-permute-start.3) | collective-permute-done | bytes 131104 | tf_op jit(solution)/shard_map/ppermute | solution.py:436
  74.8 2.2 %first_image.1 = (f32[256,128]{1,0:T(8,128)S(1)}, f32[16,128,128]{2,1,0:T(8,128)}, f32[16,8,128]{2,1,0:T(8,128)S(1)}, f32[8,48,128]{2,1,0:T(8,128)S(1)}) custom-call(f32[256,128]{1,0:T(8,128)S(1)} %copy-done, f32[256,128]{1,0:T(8,128)S(1)} %broadcast_in_dim.6.deg, f32[256,128]{1,0:T(8,128)S(1)} %get-tuple-element.62.s0, ...), custom_call_target="tpu_custom_call" | custom-call | tf_op jit(solution)/shard_map/first_image/pallas_call | solution.py:262
  77.1 1.9 %collective-permute-start.8 = (f32[352,128]{1,0:T(8,128)S(1)}, f32[352,128]{1,0:T(8,128)S(1)}, u32[]{:S(2)}, u32[]{:S(2)}) collective-permute-start(f32[352,128]{1,0:T(8,128)S(1)} %get-tuple-element.70), channel_id=1, source_target_pairs={{0,32},{16,48},{32,0},{48,16},{64,96},{80,112},{96,64},{112,80},{1... | collective-permute-start | bytes 540680 | tf_op jit(solution)/shard_map/ppermute | solution.py:426
  79.0 6.9 %all-to-all-start.2 = ((f32[16,128,128]{2,1,0:T(8,128)}), f32[16,128,128]{2,1,0:T(8,128)S(1)}, u32[]{:S(2)}, u32[]{:S(2)}) async-start(f32[16,128,128]{2,1,0:T(8,128)} %get-tuple-element.37), calls=%async_computation.2 | async-start | bytes 2097152 | tf_op jit(solution)/shard_map/all_to_all | solution.py:440
  88.0 5.9 %collective-permute-done.9.z2 = f32[352,128]{1,0:T(8,128)S(1)} collective-permute-done((f32[352,128]{1,0:T(8,128)S(1)}, f32[352,128]{1,0:T(8,128)S(1)}, u32[]{:S(2)}, u32[]{:S(2)}) %collective-permute-start.9) | collective-permute-done | bytes 180256 | tf_op jit(solution)/shard_map/ppermute | solution.py:426
  93.9 4.3 %collective-permute-start.11 = (f32[1072,128]{1,0:T(8,128)S(1)}, f32[1072,128]{1,0:T(8,128)S(1)}, u32[]{:S(2)}, u32[]{:S(2)}) collective-permute-start(f32[1072,128]{1,0:T(8,128)S(1)} %bitcast_dynamic-update-slice_fusion), channel_id=1, source_target_pairs={{0,16},{16,0},{32,48},{48,32},{64,80},{80,64},{96,112},{112,96},{1... | collective-permute-start | bytes 1646600 | tf_op jit(solution)/shard_map/ppermute | solution.py:429
  99.8 8.6 %backward.3 = f32[16,176,128]{2,1,0:T(8,128)} custom-call(bf16[2048,2048]{1,0:T(8,128)(2,1)} %get-tuple-element.29.hi_any, bf16[2048,2048]{1,0:T(8,128)(2,1)} %get-tuple-element.30.lo_any, f32[256,128]{1,0:T(8,128)S(1)} %get-tuple-element.36.own.v.y_ref, f32[352,128]{1,0:T(8,128)S(1)} %collective-permute-done.8.z1, ...), custom_call_target="tpu_custom_call" | custom-call | flops 1000000 | bytes 100000 | tf_op jit(solution)/shard_map/backward/pallas_call | solution.py:211
  108.4 6.6 %all-to-all-start.3 = ((f32[16,176,128]{2,1,0:T(8,128)}), f32[16,176,128]{2,1,0:T(8,128)S(1)}, u32[]{:S(2)}, u32[]{:S(2)}) async-start(f32[16,176,128]{2,1,0:T(8,128)} %backward.3), calls=%async_computation.3 | async-start | bytes 2883584 | tf_op jit(solution)/shard_map/all_to_all | solution.py:440
  115.0 8.4 %forward.3 = (f32[4,256,128]{2,1,0:T(8,128)S(1)}, f32[4,256,128]{2,1,0:T(8,128)S(1)}) custom-call(s32[32]{0:T(128)S(1)} %reshape.32.need_ref, bf16[2048,2048]{1,0:T(8,128)(2,1)} %get-tuple-element.29.hi_any, bf16[2048,2048]{1,0:T(8,128)(2,1)} %get-tuple-element.30.lo_any, f32[16,128,128]{2,1,0:T(8,128)S(1)} %all-to-all-done.2.cols), custom_call_target="tpu_custom_call" | custom-call | flops 1000000 | bytes 100000 | tf_op jit(solution)/shard_map/forward/pallas_call | solution.py:194
  129.1 2.7 %collective-permute-done.15.s3 = f32[256,128]{1,0:T(8,128)S(1)} collective-permute-done((f32[256,128]{1,0:T(8,128)S(1)}, f32[256,128]{1,0:T(8,128)S(1)}, u32[]{:S(2)}, u32[]{:S(2)}) %collective-permute-start.15) | collective-permute-done | bytes 131104 | tf_op jit(solution)/shard_map/ppermute | solution.py:436
  141.0 5.0 %collective-permute-start.19 = (f32[192,128]{1,0:T(8,128)S(1)}, f32[192,128]{1,0:T(8,128)S(1)}, u32[]{:S(2)}, u32[]{:S(2)}) collective-permute-start(f32[192,128]{1,0:T(8,128)S(1)} %pad_maximum_fusion.5.near), channel_id=1, source_target_pairs={{0,16},{16,0},{32,48},{48,32},{64,80},{80,64},{96,112},{112,96},{1... | collective-permute-start | bytes 294920 | tf_op jit(solution)/shard_map/ppermute | solution.py:489
  146.9 9.9 %second_block.1 = (f32[128,128]{1,0:T(8,128)S(1)}, f32[128,128]{1,0:T(8,128)S(1)}, f32[256,128]{1,0:T(8,128)S(1)}, f32[256,128]{1,0:T(8,128)S(1)}, f32[256,128]{1,0:T(8,128)S(1)}, /*index=5*/f32[384,128]{1,0:T(8,128)S(1)}) custom-call(s32[2]{0:T(128)S(1)} %pad_add_fusion.place, f32[256,128]{1,0:T(8,128)S(1)} %copy-done, ...), custom_call_target="tpu_custom_call" | custom-call | tf_op jit(solution)/shard_map/second_block/pallas_call | solution.py:370
  161.6 2.0 %collective-permute-done.23 = f32[192,128]{1,0:T(8,128)S(1)} collective-permute-done((f32[192,128]{1,0:T(8,128)S(1)}, f32[192,128]{1,0:T(8,128)S(1)}, u32[]{:S(2)}, u32[]{:S(2)}) %collective-permute-start.23) | collective-permute-done | bytes 98336 | tf_op jit(solution)/shard_map/ppermute | solution.py:444
  177.5 2.1 %collective-permute-done.28 = f32[192,128]{1,0:T(8,128)S(1)} collective-permute-done((f32[192,128]{1,0:T(8,128)S(1)}, f32[192,128]{1,0:T(8,128)S(1)}, u32[]{:S(2)}, u32[]{:S(2)}) %collective-permute-start.28) | collective-permute-done | bytes 98336 | tf_op jit(solution)/shard_map/ppermute | solution.py:444
  179.7 4.5 %collective-permute-start.30 = (f32[192,128]{1,0:T(8,128)S(1)}, f32[192,128]{1,0:T(8,128)S(1)}, u32[]{:S(2)}, u32[]{:S(2)}) collective-permute-start(f32[192,128]{1,0:T(8,128)S(1)} %add_add_fusion), channel_id=1, source_target_pairs={{0,16},{16,0},{32,48},{48,32},{64,80},{80,64},{96,112},{112,96},{1... | collective-permute-start | bytes 294920 | tf_op jit(solution)/shard_map/ppermute | solution.py:457
  185.2 4.7 %last_block.1 = (f32[2,128,128]{2,1,0:T(8,128)}, f32[2,128,128]{2,1,0:T(8,128)}, f32[256,128]{1,0:T(8,128)}) custom-call(f32[256,128]{1,0:T(8,128)S(1)} %get-tuple-element.49.v0, f32[256,128]{1,0:T(8,128)S(1)} %get-tuple-element.50.v1, f32[256,128]{1,0:T(8,128)S(1)} %get-tuple-element.51.w, f32[384,128]{1,0:T(8,128)S(1)} %pad_maximum_fusion.4.gram, ...), custom_call_target="tpu_custom_call" | custom-call | tf_op jit(solution)/shard_map/last_block/pallas_call | solution.py:393
  (98 shorter events, 49.9 us)
Async XLA Ops:
  3.1 43.5 %all-to-all-start = ((f32[16,256,128]{2,1,0:T(8,128)}), f32[16,256,128]{2,1,0:T(8,128)S(1)}, u32[]{:S(2)}, u32[]{:S(2)}) async-start(f32[16,256,128]{2,1,0:T(8,128)} %broadcast_in_dim.7), calls=%async_computation | async-start | bytes 4194304 | tf_op jit(solution)/shard_map/all_to_all | solution.py:440
  10.8 24.1 %collective-permute-start.6 = (f32[256,128]{1,0:T(8,128)S(1)}, f32[256,128]{1,0:T(8,128)S(1)}, u32[]{:S(2)}, u32[]{:S(2)}) collective-permute-start(f32[256,128]{1,0:T(8,128)S(1)} %copy-done), channel_id=1, source_target_pairs={{0,96},{16,112},{32,64},{48,80},{64,32},{80,48},{96,0},{112,16},{1... | collective-permute-start | bytes 393224 | tf_op jit(solution)/shard_map/ppermute | solution.py:417
  14.6 20.3 %collective-permute-start.5 = (f32[256,128]{1,0:T(8,128)S(1)}, f32[256,128]{1,0:T(8,128)S(1)}, u32[]{:S(2)}, u32[]{:S(2)}) collective-permute-start(f32[256,128]{1,0:T(8,128)S(1)} %copy-done), channel_id=1, source_target_pairs={{0,64},{16,80},{32,96},{48,112},{64,0},{80,16},{96,32},{112,48},{1... | collective-permute-start | bytes 393224 | tf_op jit(solution)/shard_map/ppermute | solution.py:417
  14.6 20.3 %collective-permute-start.4 = (f32[256,128]{1,0:T(8,128)S(1)}, f32[256,128]{1,0:T(8,128)S(1)}, u32[]{:S(2)}, u32[]{:S(2)}) collective-permute-start(f32[256,128]{1,0:T(8,128)S(1)} %copy-done), channel_id=1, source_target_pairs={{0,32},{16,48},{32,0},{48,16},{64,96},{80,112},{96,64},{112,80},{1... | collective-permute-start | bytes 393224 | tf_op jit(solution)/shard_map/ppermute | solution.py:417
  46.6 24.0 %all-to-all-start.1 = ((f32[16,136,128]{2,1,0:T(8,128)}), f32[16,136,128]{2,1,0:T(8,128)S(1)}, u32[]{:S(2)}, u32[]{:S(2)}) async-start(f32[16,136,128]{2,1,0:T(8,128)} %backward.2), calls=%async_computation.1 | async-start | bytes 2228224 | tf_op jit(solution)/shard_map/all_to_all | solution.py:440
  65.3 8.3 %collective-permute-start.3 = (f32[256,128]{1,0:T(8,128)S(1)}, f32[256,128]{1,0:T(8,128)S(1)}, u32[]{:S(2)}, u32[]{:S(2)}) collective-permute-start(f32[256,128]{1,0:T(8,128)S(1)} %get-tuple-element.59), channel_id=1, source_target_pairs={{0,96},{16,112},{32,64},{48,80},{64,32},{80,48},{96,0},{112,16},{1... | collective-permute-start | bytes 393224 | tf_op jit(solution)/shard_map/ppermute | solution.py:436
  68.1 5.9 %collective-permute-start.2 = (f32[256,128]{1,0:T(8,128)S(1)}, f32[256,128]{1,0:T(8,128)S(1)}, u32[]{:S(2)}, u32[]{:S(2)}) collective-permute-start(f32[256,128]{1,0:T(8,128)S(1)} %get-tuple-element.60), channel_id=1, source_target_pairs={{0,64},{16,80},{32,96},{48,112},{64,0},{80,16},{96,32},{112,48},{1... | collective-permute-start | bytes 393224 | tf_op jit(solution)/shard_map/ppermute | solution.py:436
  69.0 5.7 %collective-permute-start.1 = (f32[256,128]{1,0:T(8,128)S(1)}, f32[256,128]{1,0:T(8,128)S(1)}, u32[]{:S(2)}, u32[]{:S(2)}) collective-permute-start(f32[256,128]{1,0:T(8,128)S(1)} %get-tuple-element.61), channel_id=1, source_target_pairs={{0,32},{16,48},{32,0},{48,16},{64,96},{80,112},{96,64},{112,80},{1... | collective-permute-start | bytes 393224 | tf_op jit(solution)/shard_map/ppermute | solution.py:436
  77.1 10.9 %collective-permute-start.8 = (f32[352,128]{1,0:T(8,128)S(1)}, f32[352,128]{1,0:T(8,128)S(1)}, u32[]{:S(2)}, u32[]{:S(2)}) collective-permute-start(f32[352,128]{1,0:T(8,128)S(1)} %get-tuple-element.70), channel_id=1, source_target_pairs={{0,32},{16,48},{32,0},{48,16},{64,96},{80,112},{96,64},{112,80},{1... | collective-permute-start | bytes 540680 | tf_op jit(solution)/shard_map/ppermute | solution.py:426
  79.0 29.4 %all-to-all-start.2 = ((f32[16,128,128]{2,1,0:T(8,128)}), f32[16,128,128]{2,1,0:T(8,128)S(1)}, u32[]{:S(2)}, u32[]{:S(2)}) async-start(f32[16,128,128]{2,1,0:T(8,128)} %get-tuple-element.37), calls=%async_computation.2 | async-start | bytes 2097152 | tf_op jit(solution)/shard_map/all_to_all | solution.py:440
  86.0 7.9 %collective-permute-start.10 = (f32[352,128]{1,0:T(8,128)S(1)}, f32[352,128]{1,0:T(8,128)S(1)}, u32[]{:S(2)}, u32[]{:S(2)}) collective-permute-start(f32[352,128]{1,0:T(8,128)S(1)} %get-tuple-element.68), channel_id=1, source_target_pairs={{0,96},{16,112},{32,64},{48,80},{64,32},{80,48},{96,0},{112,16},{1... | collective-permute-start | bytes 540680 | tf_op jit(solution)/shard_map/ppermute | solution.py:426
  87.6 6.2 %collective-permute-start.9 = (f32[352,128]{1,0:T(8,128)S(1)}, f32[352,128]{1,0:T(8,128)S(1)}, u32[]{:S(2)}, u32[]{:S(2)}) collective-permute-start(f32[352,128]{1,0:T(8,128)S(1)} %get-tuple-element.69), channel_id=1, source_target_pairs={{0,64},{16,80},{32,96},{48,112},{64,0},{80,16},{96,32},{112,48},{1... | collective-permute-start | bytes 540680 | tf_op jit(solution)/shard_map/ppermute | solution.py:426
  93.9 5.9 %collective-permute-start.11 = (f32[1072,128]{1,0:T(8,128)S(1)}, f32[1072,128]{1,0:T(8,128)S(1)}, u32[]{:S(2)}, u32[]{:S(2)}) collective-permute-start(f32[1072,128]{1,0:T(8,128)S(1)} %bitcast_dynamic-update-slice_fusion), channel_id=1, source_target_pairs={{0,16},{16,0},{32,48},{48,32},{64,80},{80,64},{96,112},{112,96},{1... | collective-permute-start | bytes 1646600 | tf_op jit(solution)/shard_map/ppermute | solution.py:429
  108.4 26.6 %all-to-all-start.3 = ((f32[16,176,128]{2,1,0:T(8,128)}), f32[16,176,128]{2,1,0:T(8,128)S(1)}, u32[]{:S(2)}, u32[]{:S(2)}) async-start(f32[16,176,128]{2,1,0:T(8,128)} %backward.3), calls=%async_computation.3 | async-start | bytes 2883584 | tf_op jit(solution)/shard_map/all_to_all | solution.py:440
  125.8 6.0 %collective-permute-start.15 = (f32[256,128]{1,0:T(8,128)S(1)}, f32[256,128]{1,0:T(8,128)S(1)}, u32[]{:S(2)}, u32[]{:S(2)}) collective-permute-start(f32[256,128]{1,0:T(8,128)S(1)} %get-tuple-element.55), channel_id=1, source_target_pairs={{0,96},{16,112},{32,64},{48,80},{64,32},{80,48},{96,0},{112,16},{1... | collective-permute-start | bytes 393224 | tf_op jit(solution)/shard_map/ppermute | solution.py:436
  127.5 6.0 %collective-permute-start.14 = (f32[256,128]{1,0:T(8,128)S(1)}, f32[256,128]{1,0:T(8,128)S(1)}, u32[]{:S(2)}, u32[]{:S(2)}) collective-permute-start(f32[256,128]{1,0:T(8,128)S(1)} %get-tuple-element.56), channel_id=1, source_target_pairs={{0,64},{16,80},{32,96},{48,112},{64,0},{80,16},{96,32},{112,48},{1... | collective-permute-start | bytes 393224 | tf_op jit(solution)/shard_map/ppermute | solution.py:436
  127.5 7.5 %collective-permute-start.13 = (f32[256,128]{1,0:T(8,128)S(1)}, f32[256,128]{1,0:T(8,128)S(1)}, u32[]{:S(2)}, u32[]{:S(2)}) collective-permute-start(f32[256,128]{1,0:T(8,128)S(1)} %get-tuple-element.57), channel_id=1, source_target_pairs={{0,32},{16,48},{32,0},{48,16},{64,96},{80,112},{96,64},{112,80},{1... | collective-permute-start | bytes 393224 | tf_op jit(solution)/shard_map/ppermute | solution.py:436
  141.0 5.9 %collective-permute-start.19 = (f32[192,128]{1,0:T(8,128)S(1)}, f32[192,128]{1,0:T(8,128)S(1)}, u32[]{:S(2)}, u32[]{:S(2)}) collective-permute-start(f32[192,128]{1,0:T(8,128)S(1)} %pad_maximum_fusion.5.near), channel_id=1, source_target_pairs={{0,16},{16,0},{32,48},{48,32},{64,80},{80,64},{96,112},{112,96},{1... | collective-permute-start | bytes 294920 | tf_op jit(solution)/shard_map/ppermute | solution.py:489
  158.2 5.3 %collective-permute-start.23 = (f32[192,128]{1,0:T(8,128)S(1)}, f32[192,128]{1,0:T(8,128)S(1)}, u32[]{:S(2)}, u32[]{:S(2)}) collective-permute-start(f32[192,128]{1,0:T(8,128)S(1)} %select_add_fusion), channel_id=1, source_target_pairs={{0,96},{16,112},{32,64},{48,80},{64,32},{80,48},{96,0},{112,16},{1... | collective-permute-start | bytes 294920 | tf_op jit(solution)/shard_map/ppermute | solution.py:444
  159.4 5.1 %collective-permute-start.22 = (f32[192,128]{1,0:T(8,128)S(1)}, f32[192,128]{1,0:T(8,128)S(1)}, u32[]{:S(2)}, u32[]{:S(2)}) collective-permute-start(f32[192,128]{1,0:T(8,128)S(1)} %select_add_fusion), channel_id=1, source_target_pairs={{0,64},{16,80},{32,96},{48,112},{64,0},{80,16},{96,32},{112,48},{1... | collective-permute-start | bytes 294920 | tf_op jit(solution)/shard_map/ppermute | solution.py:444
  160.5 5.5 %collective-permute-start.21 = (f32[192,128]{1,0:T(8,128)S(1)}, f32[192,128]{1,0:T(8,128)S(1)}, u32[]{:S(2)}, u32[]{:S(2)}) collective-permute-start(f32[192,128]{1,0:T(8,128)S(1)} %select_add_fusion), channel_id=1, source_target_pairs={{0,32},{16,48},{32,0},{48,16},{64,96},{80,112},{96,64},{112,80},{1... | collective-permute-start | bytes 294920 | tf_op jit(solution)/shard_map/ppermute | solution.py:444
  167.1 5.0 %collective-permute-start.25 = (f32[192,128]{1,0:T(8,128)S(1)}, f32[192,128]{1,0:T(8,128)S(1)}, u32[]{:S(2)}, u32[]{:S(2)}) collective-permute-start(f32[192,128]{1,0:T(8,128)S(1)} %add_add_fusion.2), channel_id=1, source_target_pairs={{0,8},{1,9},{2,10},{3,11},{4,12},{5,13},{6,14},{7,15},{8,0},{9,1},... | collective-permute-start | bytes 294920 | tf_op jit(solution)/shard_map/ppermute | solution.py:444
  167.7 5.1 %collective-permute-start.24 = (f32[192,128]{1,0:T(8,128)S(1)}, f32[192,128]{1,0:T(8,128)S(1)}, u32[]{:S(2)}, u32[]{:S(2)}) collective-permute-start(f32[192,128]{1,0:T(8,128)S(1)} %add_add_fusion.2), channel_id=1, source_target_pairs={{0,4},{1,5},{2,6},{3,7},{4,0},{5,1},{6,2},{7,3},{8,12},{9,13},{10,... | collective-permute-start | bytes 294920 | tf_op jit(solution)/shard_map/ppermute | solution.py:444
  179.7 5.4 %collective-permute-start.30 = (f32[192,128]{1,0:T(8,128)S(1)}, f32[192,128]{1,0:T(8,128)S(1)}, u32[]{:S(2)}, u32[]{:S(2)}) collective-permute-start(f32[192,128]{1,0:T(8,128)S(1)} %add_add_fusion), channel_id=1, source_target_pairs={{0,16},{16,0},{32,48},{48,32},{64,80},{80,64},{96,112},{112,96},{1... | collective-permute-start | bytes 294920 | tf_op jit(solution)/shard_map/ppermute | solution.py:457
  (17 other events, 124.6 us)

commit v5 on v4

--- a/solution.py
+++ b/solution.py
@@ -142,8 +142,8 @@
         x = xc[...]
         for copy in fetches(False, i, hi_any, lo_any, hi, lo, sems):
             copy.wait()
-        out = jnp.dot(hi[here, :], x, preferred_element_type=F32) + jnp.dot(lo[here, :], x, preferred_element_type=F32)
-        out = out[:, :128] + out[:, 128:]
+        out = jnp.dot(hi[here, :], x, preferred_element_type=F32)
+        out = out[:, :128] + out[:, 128:] + jnp.dot(lo[here, :], x[:, :128], preferred_element_type=F32)
 
         @pl.when(i < 4)
         def _():

time: 191 us -> 191 us (level)
  no operation moved by 1% of the time
where the time goes in v5:
time: 191 us; the launch traced here: 190 us
  starting transfers between devices  74 us (39%)
  Pallas kernels  70.2 us (37%)
  waiting for transfers between devices  39.7 us (21%)
  local copies, waits for them, and re-layouts  2.96 us (2%)
    all_to_all x4, starting transfers between devices, swap(): return lax.all_to_all(x, 'col', 0, 0)  28.5 us
    pallas_call x1, Pallas kernels, dense_of(): pl.pallas_call(dense_kernel, grid_spec=pltpu.PrefetchScalarGridSpec(num_s...  18.8 us
    pallas_call x2, Pallas kernels, backward(): pl.pallas_call(backward_kernel, in_specs=[ANYWHERE, ANYWHERE] + [VMEM] *...  17.1 us
    pallas_call x2, Pallas kernels, forward(): pl.pallas_call(functools.partial(forward_kernel, whole), in_specs=[pl.Blo...  16.9 us
    ppermute x9, waiting for transfers between devices, ring_sum(): a, b, c = (lax.ppermute(x, axis, shift(k)) for k in (1, 2, 3))  11.3 us
    ppermute x9, starting transfers between devices, ring_sum(): a, b, c = (lax.ppermute(x, axis, shift(k)) for k in (1, 2, 3))  10 us
    pallas_call x1, Pallas kernels, second_block(): pl.pallas_call(second_kernel, in_specs=[pl.BlockSpec(memory_space=pltpu.S...  9.95 us
    ppermute x6, waiting for transfers between devices, row_sums(): lax.ppermute(parts[k], 'row', along_z(k))  9.82 us
  transfers between devices with their start and end apart: 35, of which 26 were waited for; matrix products, arithmetic and copies ran while one was open for 1% of the time, Pallas kernels for 28%

profile of v5, /device:TPU:1, one launch (start us, length us, event | category | flops | bytes accessed | tf_op | source)
XLA Modules:
  0.0 190.4 jit_solution(7069720832761172274)
XLA Ops:
  0.6 2.4 %broadcast_in_dim.7 = f32[16,256,128]{2,1,0:T(8,128)} broadcast(f32[256,128]{1,0:T(8,128)} %x_ref.1), dimensions={1,2} | broadcast | bytes 2228224 | tf_op jit(solution)/shard_map/broadcast_in_dim | solution.py:473
  3.1 7.7 %all-to-all-start = ((f32[16,256,128]{2,1,0:T(8,128)}), f32[16,256,128]{2,1,0:T(8,128)S(1)}, u32[]{:S(2)}, u32[]{:S(2)}) async-start(f32[16,256,128]{2,1,0:T(8,128)} %broadcast_in_dim.7), calls=%async_computation | async-start | bytes 4194304 | tf_op jit(solution)/shard_map/all_to_all | solution.py:440
  10.8 3.8 %collective-permute-start.6 = (f32[256,128]{1,0:T(8,128)S(1)}, f32[256,128]{1,0:T(8,128)S(1)}, u32[]{:S(2)}, u32[]{:S(2)}) collective-permute-start(f32[256,128]{1,0:T(8,128)S(1)} %copy-done), channel_id=1, source_target_pairs={{0,96},{16,112},{32,64},{48,80},{64,32},{80,48},{96,0},{112,16},{1... | collective-permute-start | bytes 393224 | tf_op jit(solution)/shard_map/ppermute | solution.py:417
  16.6 18.8 %dense.1 = (bf16[2048,2048]{1,0:T(8,128)(2,1)}, bf16[2048,2048]{1,0:T(8,128)(2,1)}) custom-call(s32[384]{0:T(512)} %fusion.13.rows_ref, s32[384]{0:T(512)} %slots_ref.1, s32[1]{0:T(128)S(6)} %copy.19.live_ref, f32[48,256,128]{2,1,0:T(8,128)} %bitcast.39), custom_call_target="tpu_custom_call" | custom-call | flops 10000000 | bytes 50000000 | tf_op jit(solution)/shard_map/dense/pallas_call | solution.py:88
  39.6 8.5 %backward.2 = f32[16,136,128]{2,1,0:T(8,128)} custom-call(bf16[2048,2048]{1,0:T(8,128)(2,1)} %get-tuple-element.29.hi_any, bf16[2048,2048]{1,0:T(8,128)(2,1)} %get-tuple-element.30.lo_any, f32[256,128]{1,0:T(8,128)S(1)} %copy-done, f32[256,128]{1,0:T(8,128)S(1)} %collective-permute-done.4.z1, f32[256,128]{1,0:T(8,128)S(1)} %collective-permute-done.5.z2, ...), custom_call_target="tpu_custom_call" | custom-call | flops 1000000 | bytes 100000 | tf_op jit(solution)/shard_map/backward/pallas_call | solution.py:211
  48.1 7.3 %all-to-all-start.1 = ((f32[16,136,128]{2,1,0:T(8,128)}), f32[16,136,128]{2,1,0:T(8,128)S(1)}, u32[]{:S(2)}, u32[]{:S(2)}) async-start(f32[16,136,128]{2,1,0:T(8,128)} %backward.2), calls=%async_computation.1 | async-start | bytes 2228224 | tf_op jit(solution)/shard_map/all_to_all | solution.py:440
  55.6 8.5 %forward.2 = (f32[4,256,128]{2,1,0:T(8,128)S(1)}, f32[4,256,128]{2,1,0:T(8,128)S(1)}) custom-call(s32[32]{0:T(128)S(1)} %reshape.32.need_ref, bf16[2048,2048]{1,0:T(8,128)(2,1)} %get-tuple-element.29.hi_any, bf16[2048,2048]{1,0:T(8,128)(2,1)} %get-tuple-element.30.lo_any, f32[16,256,128]{2,1,0:T(8,128)S(1)} %all-to-all-done.cols), custom_call_target="tpu_custom_call" | custom-call | flops 1000000 | bytes 100000 | tf_op jit(solution)/shard_map/forward/pallas_call | solution.py:194
  66.4 2.8 %collective-permute-start.3 = (f32[256,128]{1,0:T(8,128)S(1)}, f32[256,128]{1,0:T(8,128)S(1)}, u32[]{:S(2)}, u32[]{:S(2)}) collective-permute-start(f32[256,128]{1,0:T(8,128)S(1)} %get-tuple-element.59), channel_id=1, source_target_pairs={{0,96},{16,112},{32,64},{48,80},{64,32},{80,48},{96,0},{112,16},{1... | collective-permute-start | bytes 393224 | tf_op jit(solution)/shard_map/ppermute | solution.py:436
  69.8 1.9 %all-to-all-done.1.arrived = f32[16,136,128]{2,1,0:T(8,128)S(1)} async-done(((f32[16,136,128]{2,1,0:T(8,128)}), f32[16,136,128]{2,1,0:T(8,128)S(1)}, u32[]{:S(2)}, u32[]{:S(2)}) %all-to-all-start.1) | async-done | bytes 1114144 | tf_op jit(solution)/shard_map/all_to_all | solution.py:440
  71.8 2.9 %collective-permute-done.3.s3 = f32[256,128]{1,0:T(8,128)S(1)} collective-permute-done((f32[256,128]{1,0:T(8,128)S(1)}, f32[256,128]{1,0:T(8,128)S(1)}, u32[]{:S(2)}, u32[]{:S(2)}) %collective-permute-start.3) | collective-permute-done | bytes 131104 | tf_op jit(solution)/shard_map/ppermute | solution.py:436
  75.9 2.2 %first_image.1 = (f32[256,128]{1,0:T(8,128)S(1)}, f32[16,128,128]{2,1,0:T(8,128)}, f32[16,8,128]{2,1,0:T(8,128)S(1)}, f32[8,48,128]{2,1,0:T(8,128)S(1)}) custom-call(f32[256,128]{1,0:T(8,128)S(1)} %copy-done, f32[256,128]{1,0:T(8,128)S(1)} %broadcast_in_dim.6.deg, f32[256,128]{1,0:T(8,128)S(1)} %get-tuple-element.62.s0, ...), custom_call_target="tpu_custom_call" | custom-call | tf_op jit(solution)/shard_map/first_image/pallas_call | solution.py:262
  79.5 6.9 %all-to-all-start.2 = ((f32[16,128,128]{2,1,0:T(8,128)}), f32[16,128,128]{2,1,0:T(8,128)S(1)}, u32[]{:S(2)}, u32[]{:S(2)}) async-start(f32[16,128,128]{2,1,0:T(8,128)} %get-tuple-element.37), calls=%async_computation.2 | async-start | bytes 2097152 | tf_op jit(solution)/shard_map/all_to_all | solution.py:440
  89.0 5.3 %collective-permute-done.9.z2 = f32[352,128]{1,0:T(8,128)S(1)} collective-permute-done((f32[352,128]{1,0:T(8,128)S(1)}, f32[352,128]{1,0:T(8,128)S(1)}, u32[]{:S(2)}, u32[]{:S(2)}) %collective-permute-start.9) | collective-permute-done | bytes 180256 | tf_op jit(solution)/shard_map/ppermute | solution.py:426
  94.4 4.3 %collective-permute-start.11 = (f32[1072,128]{1,0:T(8,128)S(1)}, f32[1072,128]{1,0:T(8,128)S(1)}, u32[]{:S(2)}, u32[]{:S(2)}) collective-permute-start(f32[1072,128]{1,0:T(8,128)S(1)} %bitcast_dynamic-update-slice_fusion), channel_id=1, source_target_pairs={{0,16},{16,0},{32,48},{48,32},{64,80},{80,64},{96,112},{112,96},{1... | collective-permute-start | bytes 1646600 | tf_op jit(solution)/shard_map/ppermute | solution.py:429
  100.2 8.6 %backward.3 = f32[16,176,128]{2,1,0:T(8,128)} custom-call(bf16[2048,2048]{1,0:T(8,128)(2,1)} %get-tuple-element.29.hi_any, bf16[2048,2048]{1,0:T(8,128)(2,1)} %get-tuple-element.30.lo_any, f32[256,128]{1,0:T(8,128)S(1)} %get-tuple-element.36.own.v.y_ref, f32[352,128]{1,0:T(8,128)S(1)} %collective-permute-done.8.z1, ...), custom_call_target="tpu_custom_call" | custom-call | flops 1000000 | bytes 100000 | tf_op jit(solution)/shard_map/backward/pallas_call | solution.py:211
  108.8 6.6 %all-to-all-start.3 = ((f32[16,176,128]{2,1,0:T(8,128)}), f32[16,176,128]{2,1,0:T(8,128)S(1)}, u32[]{:S(2)}, u32[]{:S(2)}) async-start(f32[16,176,128]{2,1,0:T(8,128)} %backward.3), calls=%async_computation.3 | async-start | bytes 2883584 | tf_op jit(solution)/shard_map/all_to_all | solution.py:440
  115.4 8.5 %forward.3 = (f32[4,256,128]{2,1,0:T(8,128)S(1)}, f32[4,256,128]{2,1,0:T(8,128)S(1)}) custom-call(s32[32]{0:T(128)S(1)} %reshape.32.need_ref, bf16[2048,2048]{1,0:T(8,128)(2,1)} %get-tuple-element.29.hi_any, bf16[2048,2048]{1,0:T(8,128)(2,1)} %get-tuple-element.30.lo_any, f32[16,128,128]{2,1,0:T(8,128)S(1)} %all-to-all-done.2.cols), custom_call_target="tpu_custom_call" | custom-call | flops 1000000 | bytes 100000 | tf_op jit(solution)/shard_map/forward/pallas_call | solution.py:194
  129.6 2.7 %collective-permute-done.15.s3 = f32[256,128]{1,0:T(8,128)S(1)} collective-permute-done((f32[256,128]{1,0:T(8,128)S(1)}, f32[256,128]{1,0:T(8,128)S(1)}, u32[]{:S(2)}, u32[]{:S(2)}) %collective-permute-start.15) | collective-permute-done | bytes 131104 | tf_op jit(solution)/shard_map/ppermute | solution.py:436
  141.6 4.8 %collective-permute-start.19 = (f32[192,128]{1,0:T(8,128)S(1)}, f32[192,128]{1,0:T(8,128)S(1)}, u32[]{:S(2)}, u32[]{:S(2)}) collective-permute-start(f32[192,128]{1,0:T(8,128)S(1)} %pad_maximum_fusion.5.near), channel_id=1, source_target_pairs={{0,16},{16,0},{32,48},{48,32},{64,80},{80,64},{96,112},{112,96},{1... | collective-permute-start | bytes 294920 | tf_op jit(solution)/shard_map/ppermute | solution.py:489
  147.3 10.0 %second_block.1 = (f32[128,128]{1,0:T(8,128)S(1)}, f32[128,128]{1,0:T(8,128)S(1)}, f32[256,128]{1,0:T(8,128)S(1)}, f32[256,128]{1,0:T(8,128)S(1)}, f32[256,128]{1,0:T(8,128)S(1)}, /*index=5*/f32[384,128]{1,0:T(8,128)S(1)}) custom-call(s32[2]{0:T(128)S(1)} %pad_add_fusion.place, f32[256,128]{1,0:T(8,128)S(1)} %copy-done, ...), custom_call_target="tpu_custom_call" | custom-call | tf_op jit(solution)/shard_map/second_block/pallas_call | solution.py:370
  162.1 2.0 %collective-permute-done.23 = f32[192,128]{1,0:T(8,128)S(1)} collective-permute-done((f32[192,128]{1,0:T(8,128)S(1)}, f32[192,128]{1,0:T(8,128)S(1)}, u32[]{:S(2)}, u32[]{:S(2)}) %collective-permute-start.23) | collective-permute-done | bytes 98336 | tf_op jit(solution)/shard_map/ppermute | solution.py:444
  178.0 2.1 %collective-permute-done.28 = f32[192,128]{1,0:T(8,128)S(1)} collective-permute-done((f32[192,128]{1,0:T(8,128)S(1)}, f32[192,128]{1,0:T(8,128)S(1)}, u32[]{:S(2)}, u32[]{:S(2)}) %collective-permute-start.28) | collective-permute-done | bytes 98336 | tf_op jit(solution)/shard_map/ppermute | solution.py:444
  180.2 4.5 %collective-permute-start.30 = (f32[192,128]{1,0:T(8,128)S(1)}, f32[192,128]{1,0:T(8,128)S(1)}, u32[]{:S(2)}, u32[]{:S(2)}) collective-permute-start(f32[192,128]{1,0:T(8,128)S(1)} %add_add_fusion), channel_id=1, source_target_pairs={{0,16},{16,0},{32,48},{48,32},{64,80},{80,64},{96,112},{112,96},{1... | collective-permute-start | bytes 294920 | tf_op jit(solution)/shard_map/ppermute | solution.py:457
  185.6 4.7 %last_block.1 = (f32[2,128,128]{2,1,0:T(8,128)}, f32[2,128,128]{2,1,0:T(8,128)}, f32[256,128]{1,0:T(8,128)}) custom-call(f32[256,128]{1,0:T(8,128)S(1)} %get-tuple-element.49.v0, f32[256,128]{1,0:T(8,128)S(1)} %get-tuple-element.50.v1, f32[256,128]{1,0:T(8,128)S(1)} %get-tuple-element.51.w, f32[384,128]{1,0:T(8,128)S(1)} %pad_maximum_fusion.4.gram, ...), custom_call_target="tpu_custom_call" | custom-call | tf_op jit(solution)/shard_map/last_block/pallas_call | solution.py:393
  (98 shorter events, 51.1 us)
Async XLA Ops:
  3.1 45.0 %all-to-all-start = ((f32[16,256,128]{2,1,0:T(8,128)}), f32[16,256,128]{2,1,0:T(8,128)S(1)}, u32[]{:S(2)}, u32[]{:S(2)}) async-start(f32[16,256,128]{2,1,0:T(8,128)} %broadcast_in_dim.7), calls=%async_computation | async-start | bytes 4194304 | tf_op jit(solution)/shard_map/all_to_all | solution.py:440
  10.8 24.6 %collective-permute-start.6 = (f32[256,128]{1,0:T(8,128)S(1)}, f32[256,128]{1,0:T(8,128)S(1)}, u32[]{:S(2)}, u32[]{:S(2)}) collective-permute-start(f32[256,128]{1,0:T(8,128)S(1)} %copy-done), channel_id=1, source_target_pairs={{0,96},{16,112},{32,64},{48,80},{64,32},{80,48},{96,0},{112,16},{1... | collective-permute-start | bytes 393224 | tf_op jit(solution)/shard_map/ppermute | solution.py:417
  14.6 20.7 %collective-permute-start.5 = (f32[256,128]{1,0:T(8,128)S(1)}, f32[256,128]{1,0:T(8,128)S(1)}, u32[]{:S(2)}, u32[]{:S(2)}) collective-permute-start(f32[256,128]{1,0:T(8,128)S(1)} %copy-done), channel_id=1, source_target_pairs={{0,64},{16,80},{32,96},{48,112},{64,0},{80,16},{96,32},{112,48},{1... | collective-permute-start | bytes 393224 | tf_op jit(solution)/shard_map/ppermute | solution.py:417
  14.6 20.8 %collective-permute-start.4 = (f32[256,128]{1,0:T(8,128)S(1)}, f32[256,128]{1,0:T(8,128)S(1)}, u32[]{:S(2)}, u32[]{:S(2)}) collective-permute-start(f32[256,128]{1,0:T(8,128)S(1)} %copy-done), channel_id=1, source_target_pairs={{0,32},{16,48},{32,0},{48,16},{64,96},{80,112},{96,64},{112,80},{1... | collective-permute-start | bytes 393224 | tf_op jit(solution)/shard_map/ppermute | solution.py:417
  48.1 23.7 %all-to-all-start.1 = ((f32[16,136,128]{2,1,0:T(8,128)}), f32[16,136,128]{2,1,0:T(8,128)S(1)}, u32[]{:S(2)}, u32[]{:S(2)}) async-start(f32[16,136,128]{2,1,0:T(8,128)} %backward.2), calls=%async_computation.1 | async-start | bytes 2228224 | tf_op jit(solution)/shard_map/all_to_all | solution.py:440
  66.4 8.3 %collective-permute-start.3 = (f32[256,128]{1,0:T(8,128)S(1)}, f32[256,128]{1,0:T(8,128)S(1)}, u32[]{:S(2)}, u32[]{:S(2)}) collective-permute-start(f32[256,128]{1,0:T(8,128)S(1)} %get-tuple-element.59), channel_id=1, source_target_pairs={{0,96},{16,112},{32,64},{48,80},{64,32},{80,48},{96,0},{112,16},{1... | collective-permute-start | bytes 393224 | tf_op jit(solution)/shard_map/ppermute | solution.py:436
  69.2 5.9 %collective-permute-start.2 = (f32[256,128]{1,0:T(8,128)S(1)}, f32[256,128]{1,0:T(8,128)S(1)}, u32[]{:S(2)}, u32[]{:S(2)}) collective-permute-start(f32[256,128]{1,0:T(8,128)S(1)} %get-tuple-element.60), channel_id=1, source_target_pairs={{0,64},{16,80},{32,96},{48,112},{64,0},{80,16},{96,32},{112,48},{1... | collective-permute-start | bytes 393224 | tf_op jit(solution)/shard_map/ppermute | solution.py:436
  69.5 6.3 %collective-permute-start.1 = (f32[256,128]{1,0:T(8,128)S(1)}, f32[256,128]{1,0:T(8,128)S(1)}, u32[]{:S(2)}, u32[]{:S(2)}) collective-permute-start(f32[256,128]{1,0:T(8,128)S(1)} %get-tuple-element.61), channel_id=1, source_target_pairs={{0,32},{16,48},{32,0},{48,16},{64,96},{80,112},{96,64},{112,80},{1... | collective-permute-start | bytes 393224 | tf_op jit(solution)/shard_map/ppermute | solution.py:436
  78.1 10.9 %collective-permute-start.8 = (f32[352,128]{1,0:T(8,128)S(1)}, f32[352,128]{1,0:T(8,128)S(1)}, u32[]{:S(2)}, u32[]{:S(2)}) collective-permute-start(f32[352,128]{1,0:T(8,128)S(1)} %get-tuple-element.70), channel_id=1, source_target_pairs={{0,32},{16,48},{32,0},{48,16},{64,96},{80,112},{96,64},{112,80},{1... | collective-permute-start | bytes 540680 | tf_op jit(solution)/shard_map/ppermute | solution.py:426
  79.5 29.4 %all-to-all-start.2 = ((f32[16,128,128]{2,1,0:T(8,128)}), f32[16,128,128]{2,1,0:T(8,128)S(1)}, u32[]{:S(2)}, u32[]{:S(2)}) async-start(f32[16,128,128]{2,1,0:T(8,128)} %get-tuple-element.37), calls=%async_computation.2 | async-start | bytes 2097152 | tf_op jit(solution)/shard_map/all_to_all | solution.py:440
  86.4 7.9 %collective-permute-start.10 = (f32[352,128]{1,0:T(8,128)S(1)}, f32[352,128]{1,0:T(8,128)S(1)}, u32[]{:S(2)}, u32[]{:S(2)}) collective-permute-start(f32[352,128]{1,0:T(8,128)S(1)} %get-tuple-element.68), channel_id=1, source_target_pairs={{0,96},{16,112},{32,64},{48,80},{64,32},{80,48},{96,0},{112,16},{1... | collective-permute-start | bytes 540680 | tf_op jit(solution)/shard_map/ppermute | solution.py:426
  88.1 6.2 %collective-permute-start.9 = (f32[352,128]{1,0:T(8,128)S(1)}, f32[352,128]{1,0:T(8,128)S(1)}, u32[]{:S(2)}, u32[]{:S(2)}) collective-permute-start(f32[352,128]{1,0:T(8,128)S(1)} %get-tuple-element.69), channel_id=1, source_target_pairs={{0,64},{16,80},{32,96},{48,112},{64,0},{80,16},{96,32},{112,48},{1... | collective-permute-start | bytes 540680 | tf_op jit(solution)/shard_map/ppermute | solution.py:426
  94.4 5.9 %collective-permute-start.11 = (f32[1072,128]{1,0:T(8,128)S(1)}, f32[1072,128]{1,0:T(8,128)S(1)}, u32[]{:S(2)}, u32[]{:S(2)}) collective-permute-start(f32[1072,128]{1,0:T(8,128)S(1)} %bitcast_dynamic-update-slice_fusion), channel_id=1, source_target_pairs={{0,16},{16,0},{32,48},{48,32},{64,80},{80,64},{96,112},{112,96},{1... | collective-permute-start | bytes 1646600 | tf_op jit(solution)/shard_map/ppermute | solution.py:429
  108.8 26.9 %all-to-all-start.3 = ((f32[16,176,128]{2,1,0:T(8,128)}), f32[16,176,128]{2,1,0:T(8,128)S(1)}, u32[]{:S(2)}, u32[]{:S(2)}) async-start(f32[16,176,128]{2,1,0:T(8,128)} %backward.3), calls=%async_computation.3 | async-start | bytes 2883584 | tf_op jit(solution)/shard_map/all_to_all | solution.py:440
  126.3 6.0 %collective-permute-start.15 = (f32[256,128]{1,0:T(8,128)S(1)}, f32[256,128]{1,0:T(8,128)S(1)}, u32[]{:S(2)}, u32[]{:S(2)}) collective-permute-start(f32[256,128]{1,0:T(8,128)S(1)} %get-tuple-element.55), channel_id=1, source_target_pairs={{0,96},{16,112},{32,64},{48,80},{64,32},{80,48},{96,0},{112,16},{1... | collective-permute-start | bytes 393224 | tf_op jit(solution)/shard_map/ppermute | solution.py:436
  128.0 6.0 %collective-permute-start.14 = (f32[256,128]{1,0:T(8,128)S(1)}, f32[256,128]{1,0:T(8,128)S(1)}, u32[]{:S(2)}, u32[]{:S(2)}) collective-permute-start(f32[256,128]{1,0:T(8,128)S(1)} %get-tuple-element.56), channel_id=1, source_target_pairs={{0,64},{16,80},{32,96},{48,112},{64,0},{80,16},{96,32},{112,48},{1... | collective-permute-start | bytes 393224 | tf_op jit(solution)/shard_map/ppermute | solution.py:436
  128.4 7.0 %collective-permute-start.13 = (f32[256,128]{1,0:T(8,128)S(1)}, f32[256,128]{1,0:T(8,128)S(1)}, u32[]{:S(2)}, u32[]{:S(2)}) collective-permute-start(f32[256,128]{1,0:T(8,128)S(1)} %get-tuple-element.57), channel_id=1, source_target_pairs={{0,32},{16,48},{32,0},{48,16},{64,96},{80,112},{96,64},{112,80},{1... | collective-permute-start | bytes 393224 | tf_op jit(solution)/shard_map/ppermute | solution.py:436
  141.6 5.7 %collective-permute-start.19 = (f32[192,128]{1,0:T(8,128)S(1)}, f32[192,128]{1,0:T(8,128)S(1)}, u32[]{:S(2)}, u32[]{:S(2)}) collective-permute-start(f32[192,128]{1,0:T(8,128)S(1)} %pad_maximum_fusion.5.near), channel_id=1, source_target_pairs={{0,16},{16,0},{32,48},{48,32},{64,80},{80,64},{96,112},{112,96},{1... | collective-permute-start | bytes 294920 | tf_op jit(solution)/shard_map/ppermute | solution.py:489
  158.7 5.3 %collective-permute-start.23 = (f32[192,128]{1,0:T(8,128)S(1)}, f32[192,128]{1,0:T(8,128)S(1)}, u32[]{:S(2)}, u32[]{:S(2)}) collective-permute-start(f32[192,128]{1,0:T(8,128)S(1)} %select_add_fusion), channel_id=1, source_target_pairs={{0,96},{16,112},{32,64},{48,80},{64,32},{80,48},{96,0},{112,16},{1... | collective-permute-start | bytes 294920 | tf_op jit(solution)/shard_map/ppermute | solution.py:444
  159.9 5.1 %collective-permute-start.22 = (f32[192,128]{1,0:T(8,128)S(1)}, f32[192,128]{1,0:T(8,128)S(1)}, u32[]{:S(2)}, u32[]{:S(2)}) collective-permute-start(f32[192,128]{1,0:T(8,128)S(1)} %select_add_fusion), channel_id=1, source_target_pairs={{0,64},{16,80},{32,96},{48,112},{64,0},{80,16},{96,32},{112,48},{1... | collective-permute-start | bytes 294920 | tf_op jit(solution)/shard_map/ppermute | solution.py:444
  161.0 5.5 %collective-permute-start.21 = (f32[192,128]{1,0:T(8,128)S(1)}, f32[192,128]{1,0:T(8,128)S(1)}, u32[]{:S(2)}, u32[]{:S(2)}) collective-permute-start(f32[192,128]{1,0:T(8,128)S(1)} %select_add_fusion), channel_id=1, source_target_pairs={{0,32},{16,48},{32,0},{48,16},{64,96},{80,112},{96,64},{112,80},{1... | collective-permute-start | bytes 294920 | tf_op jit(solution)/shard_map/ppermute | solution.py:444
  167.6 5.0 %collective-permute-start.25 = (f32[192,128]{1,0:T(8,128)S(1)}, f32[192,128]{1,0:T(8,128)S(1)}, u32[]{:S(2)}, u32[]{:S(2)}) collective-permute-start(f32[192,128]{1,0:T(8,128)S(1)} %add_add_fusion.2), channel_id=1, source_target_pairs={{0,8},{1,9},{2,10},{3,11},{4,12},{5,13},{6,14},{7,15},{8,0},{9,1},... | collective-permute-start | bytes 294920 | tf_op jit(solution)/shard_map/ppermute | solution.py:444
  168.1 5.1 %collective-permute-start.24 = (f32[192,128]{1,0:T(8,128)S(1)}, f32[192,128]{1,0:T(8,128)S(1)}, u32[]{:S(2)}, u32[]{:S(2)}) collective-permute-start(f32[192,128]{1,0:T(8,128)S(1)} %add_add_fusion.2), channel_id=1, source_target_pairs={{0,4},{1,5},{2,6},{3,7},{4,0},{5,1},{6,2},{7,3},{8,12},{9,13},{10,... | collective-permute-start | bytes 294920 | tf_op jit(solution)/shard_map/ppermute | solution.py:444
  180.2 5.4 %collective-permute-start.30 = (f32[192,128]{1,0:T(8,128)S(1)}, f32[192,128]{1,0:T(8,128)S(1)}, u32[]{:S(2)}, u32[]{:S(2)}) collective-permute-start(f32[192,128]{1,0:T(8,128)S(1)} %add_add_fusion), channel_id=1, source_target_pairs={{0,16},{16,0},{32,48},{48,32},{64,80},{80,64},{96,112},{112,96},{1... | collective-permute-start | bytes 294920 | tf_op jit(solution)/shard_map/ppermute | solution.py:457
  (17 other events, 126.6 us)
